TPU v7x, 32 devices: a whole 2x2x4 slice. The times are simulated.
32 devices in a mesh: group: 4 (over x, core), site: 8 (over z, y).
Axes of the slice: x: 2, y: 2, z: 4, core: 2. Of those that a mesh axis runs over, the one named last changes fastest.
Arguments:
- residual_in: bfloat16 [8, 64, 128, 128], P('site', 'group'), may hold values from -6 to 6
- self_block: bfloat16 [8, 64, 64, 128], P('site'), may hold values from -0.25 to 0.25
- hop_blocks: bfloat16 [8, 64, 8, 64, 128], P('site'), may hold values from -0.1875 to 0.1875
Outputs:
- correction: float32 [8, 64, 128, 128], P('site', 'group')
- residual_out: float32 [8, 64, 128, 128], P('site', 'group')
All inputs are finite; a program needn't handle non-finite values.
Results may differ from a plain program's by a relative error of at most 0.017.
Values may be sent and summed in bfloat16 or wider, within the bound.
No kernel may reach another device: no remote copies, remote signals or barrier semaphores. Data moves between devices by JAX's collectives and lax.ppermute only.
A program may use at most 64 MiB of HBM per device.

v0:
```python
import jax
import jax.numpy as jnp
from jax import lax
from jax.sharding import PartitionSpec as P

XP = 2
LY = 4
LZ = 2
STEPS = 4


diagonal_shift = 1.5
center_value = 1.5
half_width = 1.0


def extended(value, sides, width):
    for axis, dim in sides:
        size, length = (lax.axis_size(axis), value.shape[dim])
        up = [(i, (i + 1) % size) for i in range(size)]
        down = [(j, i) for i, j in up]
        last = lax.slice_in_dim(value, length - width, length, axis=dim)
        leading = lax.slice_in_dim(value, 0, width, axis=dim)
        before = lax.ppermute(last, axis, up)
        after = lax.ppermute(leading, axis, down)
        value = jnp.concatenate([before, value, after], axis=dim)
    return value


def paired(vector):
    half = vector.shape[-1] // 2
    real_part = vector[..., :half]
    imag_part = vector[..., half:]
    conjugate = jnp.concatenate([real_part, -imag_part], axis=-1)
    swapped = jnp.concatenate([imag_part, real_part], axis=-1)
    return jnp.concatenate([conjugate, swapped], axis=-2)


def apply_blocks(vector, around, own_self, own_hops):
    count = vector.shape[2]
    own_out = jnp.einsum(
        "tsab,tskb->tska", own_self, paired(vector), preferred_element_type=jnp.float32
    )
    hop_out = jnp.einsum(
        "tsmab,tsmkb->tska", own_hops, paired(around), preferred_element_type=jnp.float32
    )
    total = own_out + hop_out
    mixed = jnp.concatenate([total[:, :, :count], total[:, :, count:]], axis=-1)
    return diagonal_shift * vector.astype(jnp.float32) + mixed


def body(residual_in, self_block, hop_blocks):
    slices = residual_in.shape[0]
    sources = lax.all_to_all(residual_in, "group", split_axis=2, concat_axis=1, tiled=True)
    planes = XP * lax.axis_size("group")
    residual = sources.astype(jnp.float32)
    correction = jnp.zeros(residual.shape, jnp.float32)
    ratio = half_width / center_value
    direction = residual / center_value
    for number in range(STEPS):
        if number > 0:
            ratio_next = 1.0 / (2.0 * center_value / half_width - ratio)
            direction = ratio_next * ratio * direction + 2.0 * ratio_next / half_width * residual
            ratio = ratio_next
        correction = correction + direction
        sent = direction.astype(jnp.bfloat16)
        flat_shape = sent.shape
        padded = extended(sent, (("site", 0),), 1)
        grid = padded.reshape((slices + 2, planes, LY, LZ) + flat_shape[2:])
        center = grid[1:-1]
        moved = []
        for axis_number in (1, 2, 3):
            moved.append(jnp.roll(center, -1, axis_number))
            moved.append(jnp.roll(center, 1, axis_number))
        moved.append(grid[2:])
        moved.append(grid[:-2])
        residual = residual - apply_blocks(
            sent,
            jnp.stack([piece.reshape(flat_shape) for piece in moved], axis=2),
            self_block,
            hop_blocks,
        )
    correction, residual = (
        lax.all_to_all(
            correction.astype(jnp.bfloat16), "group", split_axis=1, concat_axis=2, tiled=True
        ).astype(correction.dtype),
        lax.all_to_all(
            residual.astype(jnp.bfloat16), "group", split_axis=1, concat_axis=2, tiled=True
        ).astype(residual.dtype),
    )
    return (correction, residual)


def solution(mesh):
    return jax.shard_map(
        body,
        mesh=mesh,
        in_specs=(
            P("site", "group", None, None),
            P("site", None, None, None),
            P("site", None, None, None, None),
        ),
        out_specs=(P("site", "group", None, None), P("site", "group", None, None)),
        check_vma=False,
    )
```

profile of v0, /device:TPU:0, one launch (start us, length us, event | category | flops | bytes accessed | tf_op | source)
XLA Modules:
  0.0 230.5 jit_solution(4989054654641899809)
XLA Ops:
  2.1 12.9 %all_to_all.12 = bf16[1,16,128,128]{3,1,0,2:T(8,128)(2,1)S(1)} all-to-all(bf16[1,16,128,128]{3,1,0,2:T(8,128)(2,1)S(1)} %copy.12), channel_id=1, replica_groups=mesh['group'=4,'site'=8] {'group'}, dimensions={2} | all-to-all | bytes 1048576 | tf_op jit(solution)/shard_map/all_to_all | solution.py:54
  15.9 4.6 %collective-permute-start = (bf16[1,64,32,128]{3,2,1,0:T(8,128)(2,1)S(1)}, bf16[1,64,32,128]{3,2,1,0:T(8,128)(2,1)S(1)}, u32[]{:S(2)}, u32[]{:S(2)}) collective-permute-start(bf16[1,64,32,128]{3,2,1,0:T(8,128)(2,1)S(1)} %multiply_convert_fusion.1), channel_id=1, source_target_pairs={{1,0},{2,1},{3,2},{4,3},{5,4},{6,5},{7,6},{0,7},{9,8},{10,9},{11,1... | collective-permute-start | bytes 1572872 | tf_op jit(solution)/shard_map/ppermute | solution.py:25
  21.4 2.1 fusion.44
  23.5 17.0 %collective-permute-done = bf16[1,64,32,128]{3,2,1,0:T(8,128)(2,1)S(1)} collective-permute-done((bf16[1,64,32,128]{3,2,1,0:T(8,128)(2,1)S(1)}, bf16[1,64,32,128]{3,2,1,0:T(8,128)(2,1)S(1)}, u32[]{:S(2)}, u32[]{:S(2)}) %collective-permute-start) | collective-permute-done | bytes 524320 | tf_op jit(solution)/shard_map/ppermute | solution.py:25
  40.6 4.2 %slice_negate_fusion.7 = (bf16[1,64,8,32,64]{4,3,1,2,0:T(8,128)(2,1)S(1)}, bf16[1,64,8,32,64]{4,3,1,2,0:T(8,128)(2,1)}, bf16[1,64,8,32,64]{4,3,1,2,0:T(8,128)(2,1)}) fusion(bf16[1,64,8,32,128]{4,3,1,2,0:T(8,128)(2,1)S(1)} %bitcast_dynamic-update-slice_fusion.6), kind=kLoop, calls=%fused_computation.181 | loop fusion | flops 1048576 | bytes 10485760 | tf_op jit(solution)/shard_map/neg | solution.py:34
  44.8 12.0 %fusion.35 = f32[1,64,64,64]{3,2,1,0:T(8,128)} fusion(f32[64,64,64]{2,1,0:T(8,128)} %fusion.44, bf16[1,64,8,32,64]{4,3,1,2,0:T(8,128)(2,1)} %get-tuple-element.19, bf16[1,64,8,32,64]{4,3,1,2,0:T(8,128)(2,1)} %get-tuple-element.18, bf16[1,64,8,32,64]{4,3,1,2,0:T(8,128)(2,1)S(1)} %get-tuple-element.17, bf16[1,64,8,64,128]{4,3,2,1,0:T(8,128)(2,1)} %param.5), kind=kOutput, calls=%fused_computation.43 | convolution fusion | flops 570687488 | bytes 16777216 | tf_op jit(solution)/shard_map/tsmab,tsmkb->tska/dot_general | solution.py:44
  61.1 4.7 %collective-permute-start.2 = (bf16[1,64,32,128]{3,2,1,0:T(8,128)(2,1)S(1)}, bf16[1,64,32,128]{3,2,1,0:T(8,128)(2,1)S(1)}, u32[]{:S(2)}, u32[]{:S(2)}) collective-permute-start(bf16[1,64,32,128]{3,2,1,0:T(8,128)(2,1)S(1)} %get-tuple-element.4), channel_id=1, source_target_pairs={{1,0},{2,1},{3,2},{4,3},{5,4},{6,5},{7,6},{0,7},{9,8},{10,9},{11,1... | collective-permute-start | bytes 1572872 | tf_op jit(solution)/shard_map/ppermute | solution.py:25
  67.5 19.3 %collective-permute-done.2 = bf16[1,64,32,128]{3,2,1,0:T(8,128)(2,1)S(1)} collective-permute-done((bf16[1,64,32,128]{3,2,1,0:T(8,128)(2,1)S(1)}, bf16[1,64,32,128]{3,2,1,0:T(8,128)(2,1)S(1)}, u32[]{:S(2)}, u32[]{:S(2)}) %collective-permute-start.2) | collective-permute-done | bytes 524320 | tf_op jit(solution)/shard_map/ppermute | solution.py:25
  86.9 5.4 %slice_negate_fusion.6 = (bf16[1,64,8,32,64]{4,3,1,2,0:T(8,128)(2,1)}, bf16[1,64,8,32,64]{4,3,1,2,0:T(8,128)(2,1)}, bf16[1,64,8,32,64]{4,3,1,2,0:T(8,128)(2,1)}) fusion(bf16[1,64,8,32,128]{4,3,1,2,0:T(8,128)(2,1)S(1)} %bitcast_dynamic-update-slice_fusion.4), kind=kLoop, calls=%fused_computation.180 | loop fusion | flops 1048576 | bytes 10485760 | tf_op jit(solution)/shard_map/neg | solution.py:34
  92.3 12.6 %fusion.34 = f32[1,64,64,64]{3,2,1,0:T(8,128)} fusion(f32[64,64,64]{2,1,0:T(8,128)S(1)} %fusion.52, bf16[1,64,8,32,64]{4,3,1,2,0:T(8,128)(2,1)} %get-tuple-element.16, bf16[1,64,8,32,64]{4,3,1,2,0:T(8,128)(2,1)} %get-tuple-element.15, bf16[1,64,8,32,64]{4,3,1,2,0:T(8,128)(2,1)} %get-tuple-element.14, bf16[1,64,8,64,128]{4,3,2,1,0:T(8,128)(2,1)} %param.5), kind=kOutput, calls=%fused_computation.41 | convolution fusion | flops 570687488 | bytes 16777216 | tf_op jit(solution)/shard_map/tsmab,tsmkb->tska/dot_general | solution.py:44
  108.0 1.8 fusion.91
  109.8 3.2 %collective-permute-start.4 = (bf16[1,64,32,128]{3,2,1,0:T(8,128)(2,1)S(1)}, bf16[1,64,32,128]{3,2,1,0:T(8,128)(2,1)S(1)}, u32[]{:S(2)}, u32[]{:S(2)}) collective-permute-start(bf16[1,64,32,128]{3,2,1,0:T(8,128)(2,1)S(1)} %get-tuple-element.2), channel_id=1, source_target_pairs={{1,0},{2,1},{3,2},{4,3},{5,4},{6,5},{7,6},{0,7},{9,8},{10,9},{11,1... | collective-permute-start | bytes 1572872 | tf_op jit(solution)/shard_map/ppermute | solution.py:25
  114.0 2.1 fusion.61
  116.0 19.1 %collective-permute-done.4 = bf16[1,64,32,128]{3,2,1,0:T(8,128)(2,1)S(1)} collective-permute-done((bf16[1,64,32,128]{3,2,1,0:T(8,128)(2,1)S(1)}, bf16[1,64,32,128]{3,2,1,0:T(8,128)(2,1)S(1)}, u32[]{:S(2)}, u32[]{:S(2)}) %collective-permute-start.4) | collective-permute-done | bytes 524320 | tf_op jit(solution)/shard_map/ppermute | solution.py:25
  135.3 5.4 %slice_negate_fusion.5 = (bf16[1,64,8,32,64]{4,3,1,2,0:T(8,128)(2,1)}, bf16[1,64,8,32,64]{4,3,1,2,0:T(8,128)(2,1)}, bf16[1,64,8,32,64]{4,3,1,2,0:T(8,128)(2,1)}) fusion(bf16[1,64,8,32,128]{4,3,1,2,0:T(8,128)(2,1)S(1)} %bitcast_dynamic-update-slice_fusion.2), kind=kLoop, calls=%fused_computation.179 | loop fusion | flops 1048576 | bytes 10485760 | tf_op jit(solution)/shard_map/neg | solution.py:34
  140.7 13.1 %fusion.33 = f32[1,64,64,64]{3,2,1,0:T(8,128)} fusion(f32[64,64,64]{2,1,0:T(8,128)} %fusion.61, bf16[1,64,8,32,64]{4,3,1,2,0:T(8,128)(2,1)} %get-tuple-element.13, bf16[1,64,8,32,64]{4,3,1,2,0:T(8,128)(2,1)} %get-tuple-element.12, bf16[1,64,8,32,64]{4,3,1,2,0:T(8,128)(2,1)} %get-tuple-element.11, bf16[1,64,8,64,128]{4,3,2,1,0:T(8,128)(2,1)} %param.5), kind=kOutput, calls=%fused_computation.39 | convolution fusion | flops 570687488 | bytes 16777216 | tf_op jit(solution)/shard_map/tsmab,tsmkb->tska/dot_general | solution.py:44
  158.9 2.0 collective-permute-start.6
  162.7 20.4 %collective-permute-done.6 = bf16[1,64,32,128]{3,2,1,0:T(8,128)(2,1)S(1)} collective-permute-done((bf16[1,64,32,128]{3,2,1,0:T(8,128)(2,1)S(1)}, bf16[1,64,32,128]{3,2,1,0:T(8,128)(2,1)S(1)}, u32[]{:S(2)}, u32[]{:S(2)}) %collective-permute-start.6) | collective-permute-done | bytes 524320 | tf_op jit(solution)/shard_map/ppermute | solution.py:25
  183.3 5.4 %slice_negate_fusion.4 = (bf16[1,64,8,32,64]{4,3,1,2,0:T(8,128)(2,1)}, bf16[1,64,8,32,64]{4,3,1,2,0:T(8,128)(2,1)}, bf16[1,64,8,32,64]{4,3,1,2,0:T(8,128)(2,1)}) fusion(bf16[1,64,8,32,128]{4,3,1,2,0:T(8,128)(2,1)S(1)} %bitcast_dynamic-update-slice_fusion), kind=kLoop, calls=%fused_computation.178 | loop fusion | flops 1048576 | bytes 10485760 | tf_op jit(solution)/shard_map/neg | solution.py:34
  188.7 12.6 %fusion.32 = f32[1,64,64,64]{3,2,1,0:T(8,128)} fusion(f32[64,64,64]{2,1,0:T(8,128)S(1)} %fusion.70, bf16[1,64,8,32,64]{4,3,1,2,0:T(8,128)(2,1)} %get-tuple-element.10, bf16[1,64,8,32,64]{4,3,1,2,0:T(8,128)(2,1)} %get-tuple-element.9, bf16[1,64,8,32,64]{4,3,1,2,0:T(8,128)(2,1)} %get-tuple-element.8, bf16[1,64,8,64,128]{4,3,2,1,0:T(8,128)(2,1)} %param.5), kind=kOutput, calls=%fused_computation.37 | convolution fusion | flops 570687488 | bytes 16777216 | tf_op jit(solution)/shard_map/tsmab,tsmkb->tska/dot_general | solution.py:44
  201.3 1.9 fusion.103
  205.3 11.7 %all_to_all.13 = bf16[1,64,32,128]{3,2,0,1:T(8,128)(2,1)S(1)} all-to-all(bf16[1,64,32,128]{3,2,0,1:T(8,128)(2,1)S(1)} %get-tuple-element.7), channel_id=1, replica_groups=mesh['group'=4,'site'=8] {'group'}, dimensions={1} | all-to-all | bytes 1048576 | tf_op jit(solution)/shard_map/all_to_all | solution.py:84
  217.0 3.5 %all-to-all-start.2 = ((bf16[1,64,32,128]{3,2,0,1:T(8,128)(2,1)}), bf16[1,64,32,128]{3,2,0,1:T(8,128)(2,1)S(1)}, u32[]{:S(2)}, u32[]{:S(2)}) async-start(bf16[1,64,32,128]{3,2,0,1:T(8,128)(2,1)} %get-tuple-element.6), calls=%async_computation.2 | async-start | bytes 1048576 | tf_op jit(solution)/shard_map/all_to_all | solution.py:87
  221.7 7.6 %all-to-all-done.2 = bf16[1,64,32,128]{3,2,0,1:T(8,128)(2,1)S(1)} async-done(((bf16[1,64,32,128]{3,2,0,1:T(8,128)(2,1)}), bf16[1,64,32,128]{3,2,0,1:T(8,128)(2,1)S(1)}, u32[]{:S(2)}, u32[]{:S(2)}) %all-to-all-start.2) | async-done | bytes 524320 | tf_op jit(solution)/shard_map/all_to_all | solution.py:87
  (117 shorter events, 24.6 us)
Async XLA Ops:
  0.6 20.8 %copy-start = (bf16[1,64,64,128]{3,2,1,0:T(8,128)(2,1)S(1)}, bf16[1,64,64,128]{3,2,1,0:T(8,128)(2,1)}, u32[]{:S(2)}) copy-start(bf16[1,64,64,128]{3,2,1,0:T(8,128)(2,1)} %param.4) | copy-start | bytes 3145732
  15.9 24.6 %collective-permute-start = (bf16[1,64,32,128]{3,2,1,0:T(8,128)(2,1)S(1)}, bf16[1,64,32,128]{3,2,1,0:T(8,128)(2,1)S(1)}, u32[]{:S(2)}, u32[]{:S(2)}) collective-permute-start(bf16[1,64,32,128]{3,2,1,0:T(8,128)(2,1)S(1)} %multiply_convert_fusion.1), channel_id=1, source_target_pairs={{1,0},{2,1},{3,2},{4,3},{5,4},{6,5},{7,6},{0,7},{9,8},{10,9},{11,1... | collective-permute-start | bytes 1572872 | tf_op jit(solution)/shard_map/ppermute | solution.py:25
  20.5 20.1 %collective-permute-start.1 = (bf16[1,64,32,128]{3,2,1,0:T(8,128)(2,1)S(1)}, bf16[1,64,32,128]{3,2,1,0:T(8,128)(2,1)S(1)}, u32[]{:S(2)}, u32[]{:S(2)}) collective-permute-start(bf16[1,64,32,128]{3,2,1,0:T(8,128)(2,1)S(1)} %multiply_convert_fusion.1), channel_id=1, source_target_pairs={{0,1},{1,2},{2,3},{3,4},{4,5},{5,6},{6,7},{7,0},{8,9},{9,10},{10,1... | collective-permute-start | bytes 1572872 | tf_op jit(solution)/shard_map/ppermute | solution.py:24
  61.1 25.7 %collective-permute-start.2 = (bf16[1,64,32,128]{3,2,1,0:T(8,128)(2,1)S(1)}, bf16[1,64,32,128]{3,2,1,0:T(8,128)(2,1)S(1)}, u32[]{:S(2)}, u32[]{:S(2)}) collective-permute-start(bf16[1,64,32,128]{3,2,1,0:T(8,128)(2,1)S(1)} %get-tuple-element.4), channel_id=1, source_target_pairs={{1,0},{2,1},{3,2},{4,3},{5,4},{6,5},{7,6},{0,7},{9,8},{10,9},{11,1... | collective-permute-start | bytes 1572872 | tf_op jit(solution)/shard_map/ppermute | solution.py:25
  65.8 21.0 %collective-permute-start.3 = (bf16[1,64,32,128]{3,2,1,0:T(8,128)(2,1)S(1)}, bf16[1,64,32,128]{3,2,1,0:T(8,128)(2,1)S(1)}, u32[]{:S(2)}, u32[]{:S(2)}) collective-permute-start(bf16[1,64,32,128]{3,2,1,0:T(8,128)(2,1)S(1)} %get-tuple-element.4), channel_id=1, source_target_pairs={{0,1},{1,2},{2,3},{3,4},{4,5},{5,6},{6,7},{7,0},{8,9},{9,10},{10,1... | collective-permute-start | bytes 1572872 | tf_op jit(solution)/shard_map/ppermute | solution.py:24
  106.7 1.3 copy-start.1
  109.8 25.3 %collective-permute-start.4 = (bf16[1,64,32,128]{3,2,1,0:T(8,128)(2,1)S(1)}, bf16[1,64,32,128]{3,2,1,0:T(8,128)(2,1)S(1)}, u32[]{:S(2)}, u32[]{:S(2)}) collective-permute-start(bf16[1,64,32,128]{3,2,1,0:T(8,128)(2,1)S(1)} %get-tuple-element.2), channel_id=1, source_target_pairs={{1,0},{2,1},{3,2},{4,3},{5,4},{6,5},{7,6},{0,7},{9,8},{10,9},{11,1... | collective-permute-start | bytes 1572872 | tf_op jit(solution)/shard_map/ppermute | solution.py:25
  113.0 22.2 %collective-permute-start.5 = (bf16[1,64,32,128]{3,2,1,0:T(8,128)(2,1)S(1)}, bf16[1,64,32,128]{3,2,1,0:T(8,128)(2,1)S(1)}, u32[]{:S(2)}, u32[]{:S(2)}) collective-permute-start(bf16[1,64,32,128]{3,2,1,0:T(8,128)(2,1)S(1)} %get-tuple-element.2), channel_id=1, source_target_pairs={{0,1},{1,2},{2,3},{3,4},{4,5},{5,6},{6,7},{7,0},{8,9},{9,10},{10,1... | collective-permute-start | bytes 1572872 | tf_op jit(solution)/shard_map/ppermute | solution.py:24
  155.6 1.7 copy-start.3
  155.6 1.7 copy-start.5
  156.8 1.2 copy-start.2
  156.8 1.5 copy-start.7
  158.9 24.2 %collective-permute-start.6 = (bf16[1,64,32,128]{3,2,1,0:T(8,128)(2,1)S(1)}, bf16[1,64,32,128]{3,2,1,0:T(8,128)(2,1)S(1)}, u32[]{:S(2)}, u32[]{:S(2)}) collective-permute-start(bf16[1,64,32,128]{3,2,1,0:T(8,128)(2,1)S(1)} %fusion.90), channel_id=1, source_target_pairs={{1,0},{2,1},{3,2},{4,3},{5,4},{6,5},{7,6},{0,7},{9,8},{10,9},{11,1... | collective-permute-start | bytes 1572872 | tf_op jit(solution)/shard_map/ppermute | solution.py:25
  160.9 22.3 %collective-permute-start.7 = (bf16[1,64,32,128]{3,2,1,0:T(8,128)(2,1)S(1)}, bf16[1,64,32,128]{3,2,1,0:T(8,128)(2,1)S(1)}, u32[]{:S(2)}, u32[]{:S(2)}) collective-permute-start(bf16[1,64,32,128]{3,2,1,0:T(8,128)(2,1)S(1)} %fusion.90), channel_id=1, source_target_pairs={{0,1},{1,2},{2,3},{3,4},{4,5},{5,6},{6,7},{7,0},{8,9},{9,10},{10,1... | collective-permute-start | bytes 1572872 | tf_op jit(solution)/shard_map/ppermute | solution.py:24
  201.3 1.9 copy-start.4
  201.3 2.2 copy-start.6
  217.0 12.3 %all-to-all-start.2 = ((bf16[1,64,32,128]{3,2,0,1:T(8,128)(2,1)}), bf16[1,64,32,128]{3,2,0,1:T(8,128)(2,1)S(1)}, u32[]{:S(2)}, u32[]{:S(2)}) async-start(bf16[1,64,32,128]{3,2,0,1:T(8,128)(2,1)} %get-tuple-element.6), calls=%async_computation.2 | async-start | bytes 1048576 | tf_op jit(solution)/shard_map/all_to_all | solution.py:87
where the time goes:
time: 231 us; the launch traced here: 230 us
  waiting for transfers between devices  83.4 us (36%)
  matrix products  56 us (24%)
  other arithmetic  31.2 us (14%)
  blocking collectives  24.6 us (11%)
  starting transfers between devices  18 us (8%)
  local copies, waits for them, and re-layouts  16 us (7%)
    ppermute x4, waiting for transfers between devices, extended(): after = lax.ppermute(leading, axis, down)  75.7 us
    dot_general x4, matrix products, apply_blocks(): jnp.einsum('tsmab,tsmkb->tska', own_hops, paired(around), preferred_eleme...  50.4 us
    neg x8, other arithmetic, paired(): conjugate = jnp.concatenate([real_part, -imag_part], axis=-1)  21.4 us
    ppermute x4, starting transfers between devices, extended(): after = lax.ppermute(leading, axis, down)  14.5 us
    all_to_all x1, blocking collectives, body(): lax.all_to_all(residual_in, 'group', split_axis=2, concat_axis=1, tiled=T...  12.9 us
    all_to_all x1, blocking collectives, body(): lax.all_to_all(correction.astype(jnp.bfloat16), 'group', split_axis=1, co...  11.7 us
    all_to_all x1, waiting for transfers between devices, body(): lax.all_to_all(residual.astype(jnp.bfloat16), 'group', split_axis=1, conc...  7.61 us
    slice x4, local copies, waits for them, and re-layouts, apply_blocks(): mixed = jnp.concatenate([total[:, :, :count], total[:, :, count:]], axis=-1)  7.04 us
  transfers between devices with their start and end apart: 9, of which 5 were waited for; matrix products, arithmetic and copies ran while one was open for 5% of the time, Pallas kernels for 0%

commit v1 on v0

v1 whole, which is shorter than its diff:
```python
import functools

import jax
import jax.numpy as jnp
from jax import lax
from jax.experimental import pallas as pl
from jax.experimental.pallas import tpu as pltpu
from jax.sharding import PartitionSpec as P

LY = 4
LZ = 2
STEPS = 4
PIECES = 2

diagonal_shift = 1.5
center_value = 1.5
half_width = 1.0

WHOLE = pl.BlockSpec(memory_space=pltpu.VMEM)
VMEM_LIMIT = 32 * 1024 * 1024


def in_vmem(value):
    return pltpu.with_memory_space_constraint(value, pltpu.VMEM)


def coefficients():
    ratio = half_width / center_value
    out = []
    for _ in range(STEPS - 1):
        ratio_next = 1.0 / (2.0 * center_value / half_width - ratio)
        out.append((ratio_next * ratio, 2.0 * ratio_next / half_width))
        ratio = ratio_next
    return out


def call(kernel, outs, operands, flops, name, aliases=None, out_specs=None, in_specs=None, grid=()):
    nbytes = sum(o.size * o.dtype.itemsize for o in operands)
    in_specs = in_specs or [WHOLE] * len(operands)
    out_specs = out_specs or [WHOLE] * len(outs)
    operands = [in_vmem(o) if s is WHOLE else o for o, s in zip(operands, in_specs)]
    return pl.pallas_call(
        kernel,
        out_shape=outs,
        grid=grid,
        in_specs=in_specs,
        out_specs=out_specs,
        input_output_aliases=aliases or {},
        compiler_params=pltpu.CompilerParams(vmem_limit_bytes=VMEM_LIMIT),
        cost_estimate=pl.CostEstimate(flops=flops, bytes_accessed=nbytes, transcendentals=0),
        name=name,
    )(*operands)


def real_form(block):
    block = block.astype(jnp.float32)
    half = block.shape[-1] // 2
    lane = lax.broadcasted_iota(jnp.int32, block.shape, 1)
    upper = jnp.where(lane < half, block, -block)
    lower = pltpu.roll(block, half, 1)
    return jnp.concatenate([upper, lower], axis=0)


def prep_kernel(plane_sites, place, self_ref, hop_ref, local_ref, time_ref):
    parity = place[1]
    per = self_ref.shape[1]
    width = self_ref.shape[3]
    step = pl.program_id(0)
    for j in range(per):
        site = step * per + j
        plane = site // plane_sites
        hop = lambda m: real_form(hop_ref[0, j, m])
        parts = [
            real_form(self_ref[0, j]),
            hop(plane),
            hop(2),
            hop(3),
            hop(4) + hop(5),
            hop(1 - plane),
        ]
        for k, part in enumerate(parts):
            local_ref[site, :, k * width : (k + 1) * width] = part.astype(jnp.bfloat16)
        time_ref[site, :, :width] = hop(6 + parity).astype(jnp.bfloat16)
        time_ref[site, :, width:] = hop(7 - parity).astype(jnp.bfloat16)


def prep(self_block, hop_blocks, sites, plane_sites):
    place = jnp.stack([lax.axis_index("group"), lax.axis_index("site") % 2]).astype(jnp.int32)
    comps, width = self_block.shape[2:]
    per = 2
    grid_spec = pltpu.PrefetchScalarGridSpec(
        num_scalar_prefetch=1,
        grid=(sites // per,),
        in_specs=[
            pl.BlockSpec((1, per, comps, width), lambda i, p: (0, p[0] * (sites // per) + i, 0, 0)),
            pl.BlockSpec(
                (1, per, 8, comps, width), lambda i, p: (0, p[0] * (sites // per) + i, 0, 0, 0)
            ),
        ],
        out_specs=[WHOLE, WHOLE],
    )
    return pl.pallas_call(
        functools.partial(prep_kernel, plane_sites),
        out_shape=[
            pltpu.VMEM((sites, width, 6 * width), jnp.bfloat16),
            pltpu.VMEM((sites, width, 2 * width), jnp.bfloat16),
        ],
        grid_spec=grid_spec,
        compiler_params=pltpu.CompilerParams(vmem_limit_bytes=VMEM_LIMIT),
        name="prep",
    )(place, self_block, hop_blocks)


def times(vector, weight):
    return lax.dot_general(
        vector, weight, (((1,), (1,)), ((), ())), preferred_element_type=jnp.float32
    )


def local_kernel(plane, plane_sites, pieces, first, *refs):
    sent = refs[:pieces]
    halo, residual, weight = refs[pieces : pieces + 3]
    per = sent[0].shape[0]

    def at(site):
        return sent[site // per][site % per]

    acc = refs[pieces + 3]
    base = plane * plane_sites
    for s in range(plane_sites):
        y, z = s // LZ, s % LZ
        own = at(base + s)
        around = jnp.concatenate(
            [
                own,
                at((1 - plane) * plane_sites + s),
                at(base + (y + 1) % LY * LZ + z),
                at(base + (y - 1) % LY * LZ + z),
                at(base + y * LZ + 1 - z),
                halo[s],
            ],
            axis=1,
        )
        now = residual[0, base + s].astype(jnp.float32) if first else residual[s]
        acc[s] = now - diagonal_shift * own.astype(jnp.float32) - times(around, weight[base + s])


def time_kernel(offset, mode, scale, *refs):
    if mode == "last":
        acc, partner, other, weight, out = refs[:4] + refs[-1:]
    else:
        acc, partner, other, weight, direction, correction = refs[:6]
        out, direction_out, correction_out, sent_out = refs[6:]
    per = partner.shape[0]
    plane_offset = offset % acc.shape[0]
    for s in range(per):
        around = jnp.concatenate([partner[s], other[s]], axis=1)
        now = acc[plane_offset + s] - times(around, weight[offset + s])
        out[s] = now
        if mode != "last":
            if mode == "first":
                old = direction[0, offset + s].astype(jnp.float32) * (half_width / center_value)
                total = old
            else:
                old = direction[s]
                total = correction[s]
            new = scale[0] * old + scale[1] * now
            direction_out[s] = new
            correction_out[s] = total + new
            sent_out[s] = new.astype(jnp.bfloat16)


def body(residual_in, self_block, hop_blocks):
    _, sites, count, width = residual_in.shape
    plane_sites = LY * LZ
    groups, slices = lax.axis_size("group"), lax.axis_size("site")
    assert sites == 2 * plane_sites and slices % 2 == 0
    per = sites // PIECES
    per_plane = PIECES // 2
    swap = [(i, i ^ 1) for i in range(slices)]
    relay = [(i, (i + 2 - 4 * (i % 2)) % slices) for i in range(slices)]
    up = [(i, (i + 1) % groups) for i in range(groups)]
    down = [(j, i) for i, j in up]

    weight_local, weight_time = prep(self_block, hop_blocks, sites, plane_sites)
    scales = coefficients()
    block = (count, width)
    f32, bf16 = jnp.float32, jnp.bfloat16

    start = (residual_in[0].astype(f32) * (half_width / center_value)).astype(bf16)
    sent = [start[i * per : (i + 1) * per] for i in range(PIECES)]
    residual = [None] * PIECES
    direction = [None] * PIECES
    correction = [None] * PIECES
    mac = 2 * count * width * width
    for number in range(STEPS):
        halo = []
        for plane, pairs in ((0, up), (1, down)):
            far = sent[(1 - plane) * per_plane : (2 - plane) * per_plane]
            far = far[0] if per_plane == 1 else jnp.concatenate(far, axis=0)
            halo.append(lax.ppermute(far, "group", pairs))
        partner = [lax.ppermute(v, "site", swap) for v in sent]
        other = [lax.ppermute(v, "site", relay) for v in partner]
        acc = []
        for plane in range(2):
            if number == 0:
                now = residual_in
            else:
                now = residual[plane * per_plane : (plane + 1) * per_plane]
                now = now[0] if per_plane == 1 else jnp.concatenate(now, axis=0)
            acc.append(
                call(
                    functools.partial(local_kernel, plane, plane_sites, PIECES, number == 0),
                    [pltpu.VMEM((plane_sites,) + block, f32)],
                    [*sent, halo[plane], now, weight_local],
                    plane_sites * 6 * mac,
                    "local_terms",
                )[0]
            )
        last = number == STEPS - 1
        result = None
        new_sent = []
        for i in range(PIECES):
            mode = "first" if number == 0 else "last" if last else "middle"
            operands = [acc[i // per_plane], partner[i], other[i], weight_time]
            flops = per * 2 * mac
            kernel = functools.partial(
                time_kernel, i * per, mode, None if last else scales[number]
            )
            if last:
                spec = pl.BlockSpec((per,) + block, lambda _, i=i: (i, 0, 0))
                extra = [] if result is None else [result]
                result = call(
                    kernel,
                    [jax.ShapeDtypeStruct((sites,) + block, f32)],
                    operands + extra,
                    flops,
                    "time_terms_last",
                    aliases={4: 0} if extra else None,
                    grid=(1,),
                    out_specs=[spec],
                    in_specs=[WHOLE] * 4 + [pl.BlockSpec(memory_space=pltpu.HBM)] * len(extra),
                )[0]
                continue
            old = [residual_in, residual_in] if number == 0 else [direction[i], correction[i]]
            residual[i], direction[i], correction[i], new = call(
                kernel,
                [pltpu.VMEM((per,) + block, f32)] * 3 + [pltpu.VMEM((per,) + block, bf16)],
                operands + old,
                flops,
                "time_terms",
            )
            new_sent.append(new)
        sent = new_sent
    correction = jnp.concatenate(correction, axis=0)
    return correction[None], result[None]


def solution(mesh):
    return jax.shard_map(
        body,
        mesh=mesh,
        in_specs=(
            P("site", "group", None, None),
            P("site", None, None, None),
            P("site", None, None, None, None),
        ),
        out_specs=(P("site", "group", None, None), P("site", "group", None, None)),
        check_vma=False,
    )
```

time: 231 us -> 90.3 us (0.39)
  matrix products: 56 us -> 0 us
  waiting for transfers between devices: 83.4 us -> 53.6 us
  other arithmetic: 31.2 us -> 2.38 us
  blocking collectives: 24.6 us -> 0 us
  Pallas kernels: 0 us -> 12.3 us
  local copies, waits for them, and re-layouts: 16 us -> 4.65 us
    dot_general x8 -> x0, matrix products: 56 us -> none  [the longest x4 50.4 us: apply_blocks(): jnp.einsum('tsmab,tsmkb->tska', own_hops, paired(around), preferred_eleme...]
    all_to_all x2 -> x0, blocking collectives: 24.6 us -> none  [the longest x1 12.9 us: body(): lax.all_to_all(residual_in, 'group', split_axis=2, concat_axis=1, tiled=T...]
    ppermute x8 -> x24, waiting for transfers between devices: 75.8 us -> 53.6 us  [the longest x8 31.4 us: body(): partner = [lax.ppermute(v, 'site', swap) for v in sent]]
    neg x8 -> x0, other arithmetic: 21.4 us -> none  [paired(): conjugate = jnp.concatenate([real_part, -imag_part], axis=-1)]
    pallas_call x0 -> x17, Pallas kernels: none -> 12.3 us  [the longest x16 10.4 us: call(): pl.pallas_call(kernel, out_shape=outs, grid=grid, in_specs=in_specs, out_...]
    slice x24 -> x1, local copies, waits for them, and re-layouts: 8.79 us -> 0.04 us  [body(): sent = [start[i * per:(i + 1) * per] for i in range(PIECES)]]
    all_to_all x1 -> x0, waiting for transfers between devices: 7.61 us -> none  [body(): lax.all_to_all(residual.astype(jnp.bfloat16), 'group', split_axis=1, conc...]
    convert_element_type x11 -> x1, other arithmetic: 8.78 us -> 1.24 us  [body(): (residual_in[0].astype(f32) * (half_width / center_value)).astype(bf16)]
  transfers between devices with their start and end apart: 9 -> 24, of which waited for: 5 -> 14; matrix products, arithmetic and copies ran while one was open for 5% -> 1% of each run, Pallas kernels for 0% -> 12%
where the time goes in v1:
time: 90.3 us; the launch traced here: 90.1 us
  waiting for transfers between devices  53.6 us (59%)
  starting transfers between devices  16.2 us (18%)
  Pallas kernels  12.3 us (14%)
  local copies, waits for them, and re-layouts  4.65 us (5%)
  other arithmetic  2.38 us (3%)
    ppermute x8, waiting for transfers between devices, body(): partner = [lax.ppermute(v, 'site', swap) for v in sent]  31.4 us
    ppermute x8, waiting for transfers between devices, body(): other = [lax.ppermute(v, 'site', relay) for v in partner]  22.2 us
    pallas_call x16, Pallas kernels, call(): pl.pallas_call(kernel, out_shape=outs, grid=grid, in_specs=in_specs, out_...  10.4 us
    ppermute x8, starting transfers between devices, body(): partner = [lax.ppermute(v, 'site', swap) for v in sent]  8.22 us
    unnamed x6, local copies, waits for them, and re-layouts  4.61 us
    ppermute x8, starting transfers between devices, body(): halo.append(lax.ppermute(far, 'group', pairs))  4.04 us
    ppermute x8, starting transfers between devices, body(): other = [lax.ppermute(v, 'site', relay) for v in partner]  3.98 us
    pallas_call x1, Pallas kernels, prep(): pl.pallas_call(functools.partial(prep_kernel, plane_sites), out_shape=[pl...  1.93 us
  transfers between devices with their start and end apart: 24, of which 14 were waited for; matrix products, arithmetic and copies ran while one was open for 1% of the time, Pallas kernels for 12%

profile of v1, /device:TPU:0, one launch (start us, length us, event | category | flops | bytes accessed | tf_op | source)
XLA Modules:
  0.0 90.1 jit_solution(5337958105786561503)
XLA Ops:
  0.6 1.2 %multiply_convert_fusion = bf16[1,16,128,128]{3,2,1,0:T(8,128)(2,1)S(1)} fusion(bf16[1,16,128,128]{3,2,1,0:T(8,128)(2,1)} %refs_5_.3), kind=kLoop, calls=%fused_computation.1 | loop fusion | flops 786432 | bytes 1048576 | tf_op jit(solution)/shard_map/convert_element_type | solution.py:190
  1.9 3.0 %collective-permute-start.1 = (bf16[8,128,128]{2,1,0:T(8,128)(2,1)S(1)}, bf16[8,128,128]{2,1,0:T(8,128)(2,1)S(1)}, u32[]{:S(2)}, u32[]{:S(2)}) collective-permute-start(bf16[8,128,128]{2,1,0:T(8,128)(2,1)S(1)} %get-tuple-element.51.refs_0_), channel_id=1, source_target_pairs={{0,1},{1,0},{2,3},{3,2},{4,5},{5,4},{6,7},{7,6},{8,9},{9,8},{10,11... | collective-permute-start | bytes 786440 | tf_op jit(solution)/shard_map/ppermute | solution.py:202
  5.0 7.1 %collective-permute-done.1.refs_1_ = bf16[8,128,128]{2,1,0:T(8,128)(2,1)S(1)} collective-permute-done((bf16[8,128,128]{2,1,0:T(8,128)(2,1)S(1)}, bf16[8,128,128]{2,1,0:T(8,128)(2,1)S(1)}, u32[]{:S(2)}, u32[]{:S(2)}) %collective-permute-start.1) | collective-permute-done | bytes 262176 | tf_op jit(solution)/shard_map/ppermute | solution.py:202
  12.1 2.1 %collective-permute-start.2 = (bf16[8,128,128]{2,1,0:T(8,128)(2,1)S(1)}, bf16[8,128,128]{2,1,0:T(8,128)(2,1)S(1)}, u32[]{:S(2)}, u32[]{:S(2)}) collective-permute-start(bf16[8,128,128]{2,1,0:T(8,128)(2,1)S(1)} %collective-permute-done.1.refs_1_), channel_id=1, source_target_pairs={{0,2},{1,7},{2,4},{3,1},{4,6},{5,3},{6,0},{7,5},{8,10},{9,15},{10,... | collective-permute-start | bytes 786440 | tf_op jit(solution)/shard_map/ppermute | solution.py:203
  14.2 2.7 %collective-permute-done.4.refs_1_ = bf16[8,128,128]{2,1,0:T(8,128)(2,1)S(1)} collective-permute-done((bf16[8,128,128]{2,1,0:T(8,128)(2,1)S(1)}, bf16[8,128,128]{2,1,0:T(8,128)(2,1)S(1)}, u32[]{:S(2)}, u32[]{:S(2)}) %collective-permute-start.4) | collective-permute-done | bytes 262176 | tf_op jit(solution)/shard_map/ppermute | solution.py:202
  16.9 1.8 %collective-permute-start.5 = (bf16[8,128,128]{2,1,0:T(8,128)(2,1)S(1)}, bf16[8,128,128]{2,1,0:T(8,128)(2,1)S(1)}, u32[]{:S(2)}, u32[]{:S(2)}) collective-permute-start(bf16[8,128,128]{2,1,0:T(8,128)(2,1)S(1)} %collective-permute-done.4.refs_1_), channel_id=1, source_target_pairs={{0,2},{1,7},{2,4},{3,1},{4,6},{5,3},{6,0},{7,5},{8,10},{9,15},{10,... | collective-permute-start | bytes 786440 | tf_op jit(solution)/shard_map/ppermute | solution.py:203
  18.8 3.4 %copy-done.1 = bf16[1,64,8,64,128]{4,3,2,1,0:T(8,128)(2,1)S(1)} copy-done((bf16[1,64,8,64,128]{4,3,2,1,0:T(8,128)(2,1)S(1)}, bf16[1,64,8,64,128]{4,3,2,1,0:T(8,128)(2,1)}, u32[]{:S(2)}) %copy-start.1) | copy-done | bytes 8388632
  22.1 1.2 %copy-done.2 = bf16[1,64,64,128]{3,2,1,0:T(8,128)(2,1)S(1)} copy-done((bf16[1,64,64,128]{3,2,1,0:T(8,128)(2,1)S(1)}, bf16[1,64,64,128]{3,2,1,0:T(8,128)(2,1)}, u32[]{:S(2)}) %copy-start.2) | copy-done | bytes 1048600
  23.4 1.9 %prep.1 = (bf16[16,128,768]{2,1,0:T(8,128)(2,1)S(1)}, bf16[16,128,256]{2,1,0:T(8,128)(2,1)S(1)}) custom-call(s32[2]{0:T(128)S(1)} %pad_add_fusion.place, bf16[1,64,64,128]{3,2,1,0:T(8,128)(2,1)S(1)} %copy-done.2, bf16[1,64,8,64,128]{4,3,2,1,0:T(8,128)(2,1)S(1)} %copy-done.1), custom_call_target="tpu_custom_call" | custom-call | tf_op jit(solution)/shard_map/prep/pallas_call | solution.py:102
  26.3 3.6 %collective-permute-start.7 = (bf16[8,128,128]{2,1,0:T(8,128)(2,1)S(1)}, bf16[8,128,128]{2,1,0:T(8,128)(2,1)S(1)}, u32[]{:S(2)}, u32[]{:S(2)}) collective-permute-start(bf16[8,128,128]{2,1,0:T(8,128)(2,1)S(1)} %get-tuple-element.28.refs_0_), channel_id=1, source_target_pairs={{0,1},{1,0},{2,3},{3,2},{4,5},{5,4},{6,7},{7,6},{8,9},{9,8},{10,11... | collective-permute-start | bytes 786440 | tf_op jit(solution)/shard_map/ppermute | solution.py:202
  31.4 5.7 %collective-permute-done.7.refs_1_ = bf16[8,128,128]{2,1,0:T(8,128)(2,1)S(1)} collective-permute-done((bf16[8,128,128]{2,1,0:T(8,128)(2,1)S(1)}, bf16[8,128,128]{2,1,0:T(8,128)(2,1)S(1)}, u32[]{:S(2)}, u32[]{:S(2)}) %collective-permute-start.7) | collective-permute-done | bytes 262176 | tf_op jit(solution)/shard_map/ppermute | solution.py:202
  37.1 3.5 %collective-permute-done.10.refs_1_ = bf16[8,128,128]{2,1,0:T(8,128)(2,1)S(1)} collective-permute-done((bf16[8,128,128]{2,1,0:T(8,128)(2,1)S(1)}, bf16[8,128,128]{2,1,0:T(8,128)(2,1)S(1)}, u32[]{:S(2)}, u32[]{:S(2)}) %collective-permute-start.10) | collective-permute-done | bytes 262176 | tf_op jit(solution)/shard_map/ppermute | solution.py:202
  41.8 5.7 %collective-permute-done.8.refs_2_ = bf16[8,128,128]{2,1,0:T(8,128)(2,1)S(1)} collective-permute-done((bf16[8,128,128]{2,1,0:T(8,128)(2,1)S(1)}, bf16[8,128,128]{2,1,0:T(8,128)(2,1)S(1)}, u32[]{:S(2)}, u32[]{:S(2)}) %collective-permute-start.8) | collective-permute-done | bytes 262176 | tf_op jit(solution)/shard_map/ppermute | solution.py:203
  48.6 2.3 %collective-permute-done.11.refs_2_ = bf16[8,128,128]{2,1,0:T(8,128)(2,1)S(1)} collective-permute-done((bf16[8,128,128]{2,1,0:T(8,128)(2,1)S(1)}, bf16[8,128,128]{2,1,0:T(8,128)(2,1)S(1)}, u32[]{:S(2)}, u32[]{:S(2)}) %collective-permute-start.11) | collective-permute-done | bytes 262176 | tf_op jit(solution)/shard_map/ppermute | solution.py:203
  51.5 1.7 %collective-permute-start.15 = (bf16[8,128,128]{2,1,0:T(8,128)(2,1)S(1)}, bf16[8,128,128]{2,1,0:T(8,128)(2,1)S(1)}, u32[]{:S(2)}, u32[]{:S(2)}) collective-permute-start(bf16[8,128,128]{2,1,0:T(8,128)(2,1)S(1)} %get-tuple-element.33.refs_0_), channel_id=1, source_target_pairs={{8,0},{16,8},{24,16},{0,24},{9,1},{17,9},{25,17},{1,25},{10,2},{18... | collective-permute-start | bytes 786440 | tf_op jit(solution)/shard_map/ppermute | solution.py:201
  53.2 3.6 %collective-permute-done.13.refs_1_ = bf16[8,128,128]{2,1,0:T(8,128)(2,1)S(1)} collective-permute-done((bf16[8,128,128]{2,1,0:T(8,128)(2,1)S(1)}, bf16[8,128,128]{2,1,0:T(8,128)(2,1)S(1)}, u32[]{:S(2)}, u32[]{:S(2)}) %collective-permute-start.13) | collective-permute-done | bytes 262176 | tf_op jit(solution)/shard_map/ppermute | solution.py:202
  56.8 3.1 %collective-permute-done.16.refs_1_ = bf16[8,128,128]{2,1,0:T(8,128)(2,1)S(1)} collective-permute-done((bf16[8,128,128]{2,1,0:T(8,128)(2,1)S(1)}, bf16[8,128,128]{2,1,0:T(8,128)(2,1)S(1)}, u32[]{:S(2)}, u32[]{:S(2)}) %collective-permute-start.16) | collective-permute-done | bytes 262176 | tf_op jit(solution)/shard_map/ppermute | solution.py:202
  61.1 6.4 %collective-permute-done.14.refs_2_ = bf16[8,128,128]{2,1,0:T(8,128)(2,1)S(1)} collective-permute-done((bf16[8,128,128]{2,1,0:T(8,128)(2,1)S(1)}, bf16[8,128,128]{2,1,0:T(8,128)(2,1)S(1)}, u32[]{:S(2)}, u32[]{:S(2)}) %collective-permute-start.14) | collective-permute-done | bytes 262176 | tf_op jit(solution)/shard_map/ppermute | solution.py:203
  68.6 1.7 %collective-permute-done.17.refs_2_ = bf16[8,128,128]{2,1,0:T(8,128)(2,1)S(1)} collective-permute-done((bf16[8,128,128]{2,1,0:T(8,128)(2,1)S(1)}, bf16[8,128,128]{2,1,0:T(8,128)(2,1)S(1)}, u32[]{:S(2)}, u32[]{:S(2)}) %collective-permute-start.17) | collective-permute-done | bytes 262176 | tf_op jit(solution)/shard_map/ppermute | solution.py:203
  71.7 1.7 %collective-permute-start.18 = (bf16[8,128,128]{2,1,0:T(8,128)(2,1)S(1)}, bf16[8,128,128]{2,1,0:T(8,128)(2,1)S(1)}, u32[]{:S(2)}, u32[]{:S(2)}) collective-permute-start(bf16[8,128,128]{2,1,0:T(8,128)(2,1)S(1)} %get-tuple-element.46.refs_0_), channel_id=1, source_target_pairs={{8,0},{16,8},{24,16},{0,24},{9,1},{17,9},{25,17},{1,25},{10,2},{18... | collective-permute-start | bytes 786440 | tf_op jit(solution)/shard_map/ppermute | solution.py:201
  73.5 3.1 %collective-permute-done.22.refs_1_ = bf16[8,128,128]{2,1,0:T(8,128)(2,1)S(1)} collective-permute-done((bf16[8,128,128]{2,1,0:T(8,128)(2,1)S(1)}, bf16[8,128,128]{2,1,0:T(8,128)(2,1)S(1)}, u32[]{:S(2)}, u32[]{:S(2)}) %collective-permute-start.22) | collective-permute-done | bytes 262176 | tf_op jit(solution)/shard_map/ppermute | solution.py:202
  76.6 2.8 %collective-permute-done.19.refs_1_ = bf16[8,128,128]{2,1,0:T(8,128)(2,1)S(1)} collective-permute-done((bf16[8,128,128]{2,1,0:T(8,128)(2,1)S(1)}, bf16[8,128,128]{2,1,0:T(8,128)(2,1)S(1)}, u32[]{:S(2)}, u32[]{:S(2)}) %collective-permute-start.19) | collective-permute-done | bytes 262176 | tf_op jit(solution)/shard_map/ppermute | solution.py:202
  81.6 4.5 %collective-permute-done.23.refs_2_ = bf16[8,128,128]{2,1,0:T(8,128)(2,1)S(1)} collective-permute-done((bf16[8,128,128]{2,1,0:T(8,128)(2,1)S(1)}, bf16[8,128,128]{2,1,0:T(8,128)(2,1)S(1)}, u32[]{:S(2)}, u32[]{:S(2)}) %collective-permute-start.23) | collective-permute-done | bytes 262176 | tf_op jit(solution)/shard_map/ppermute | solution.py:203
  87.3 1.7 %collective-permute-done.20.refs_2_ = bf16[8,128,128]{2,1,0:T(8,128)(2,1)S(1)} collective-permute-done((bf16[8,128,128]{2,1,0:T(8,128)(2,1)S(1)}, bf16[8,128,128]{2,1,0:T(8,128)(2,1)S(1)}, u32[]{:S(2)}, u32[]{:S(2)}) %collective-permute-start.20) | collective-permute-done | bytes 262176 | tf_op jit(solution)/shard_map/ppermute | solution.py:203
  (51 shorter events, 13.8 us)
Async XLA Ops:
  1.9 10.2 %collective-permute-start.1 = (bf16[8,128,128]{2,1,0:T(8,128)(2,1)S(1)}, bf16[8,128,128]{2,1,0:T(8,128)(2,1)S(1)}, u32[]{:S(2)}, u32[]{:S(2)}) collective-permute-start(bf16[8,128,128]{2,1,0:T(8,128)(2,1)S(1)} %get-tuple-element.51.refs_0_), channel_id=1, source_target_pairs={{0,1},{1,0},{2,3},{3,2},{4,5},{5,4},{6,7},{7,6},{8,9},{9,8},{10,11... | collective-permute-start | bytes 786440 | tf_op jit(solution)/shard_map/ppermute | solution.py:202
  5.0 11.9 %collective-permute-start.4 = (bf16[8,128,128]{2,1,0:T(8,128)(2,1)S(1)}, bf16[8,128,128]{2,1,0:T(8,128)(2,1)S(1)}, u32[]{:S(2)}, u32[]{:S(2)}) collective-permute-start(bf16[8,128,128]{2,1,0:T(8,128)(2,1)S(1)} %get-tuple-element.50.refs_1_), channel_id=1, source_target_pairs={{0,1},{1,0},{2,3},{3,2},{4,5},{5,4},{6,7},{7,6},{8,9},{9,8},{10,11... | collective-permute-start | bytes 786440 | tf_op jit(solution)/shard_map/ppermute | solution.py:202
  5.0 20.3 %collective-permute-start = (bf16[8,128,128]{2,1,0:T(8,128)(2,1)S(1)}, bf16[8,128,128]{2,1,0:T(8,128)(2,1)S(1)}, u32[]{:S(2)}, u32[]{:S(2)}) collective-permute-start(bf16[8,128,128]{2,1,0:T(8,128)(2,1)S(1)} %get-tuple-element.50.refs_1_), channel_id=1, source_target_pairs={{0,8},{8,16},{16,24},{24,0},{1,9},{9,17},{17,25},{25,1},{2,10},{10... | collective-permute-start | bytes 786440 | tf_op jit(solution)/shard_map/ppermute | solution.py:201
  12.1 13.8 %collective-permute-start.2 = (bf16[8,128,128]{2,1,0:T(8,128)(2,1)S(1)}, bf16[8,128,128]{2,1,0:T(8,128)(2,1)S(1)}, u32[]{:S(2)}, u32[]{:S(2)}) collective-permute-start(bf16[8,128,128]{2,1,0:T(8,128)(2,1)S(1)} %collective-permute-done.1.refs_1_), channel_id=1, source_target_pairs={{0,2},{1,7},{2,4},{3,1},{4,6},{5,3},{6,0},{7,5},{8,10},{9,15},{10,... | collective-permute-start | bytes 786440 | tf_op jit(solution)/shard_map/ppermute | solution.py:203
  14.2 15.7 %collective-permute-start.3 = (bf16[8,128,128]{2,1,0:T(8,128)(2,1)S(1)}, bf16[8,128,128]{2,1,0:T(8,128)(2,1)S(1)}, u32[]{:S(2)}, u32[]{:S(2)}) collective-permute-start(bf16[8,128,128]{2,1,0:T(8,128)(2,1)S(1)} %get-tuple-element.51.refs_0_), channel_id=1, source_target_pairs={{8,0},{16,8},{24,16},{0,24},{9,1},{17,9},{25,17},{1,25},{10,2},{18... | collective-permute-start | bytes 786440 | tf_op jit(solution)/shard_map/ppermute | solution.py:201
  16.9 13.6 %collective-permute-start.5 = (bf16[8,128,128]{2,1,0:T(8,128)(2,1)S(1)}, bf16[8,128,128]{2,1,0:T(8,128)(2,1)S(1)}, u32[]{:S(2)}, u32[]{:S(2)}) collective-permute-start(bf16[8,128,128]{2,1,0:T(8,128)(2,1)S(1)} %collective-permute-done.4.refs_1_), channel_id=1, source_target_pairs={{0,2},{1,7},{2,4},{3,1},{4,6},{5,3},{6,0},{7,5},{8,10},{9,15},{10,... | collective-permute-start | bytes 786440 | tf_op jit(solution)/shard_map/ppermute | solution.py:203
  26.3 10.8 %collective-permute-start.7 = (bf16[8,128,128]{2,1,0:T(8,128)(2,1)S(1)}, bf16[8,128,128]{2,1,0:T(8,128)(2,1)S(1)}, u32[]{:S(2)}, u32[]{:S(2)}) collective-permute-start(bf16[8,128,128]{2,1,0:T(8,128)(2,1)S(1)} %get-tuple-element.28.refs_0_), channel_id=1, source_target_pairs={{0,1},{1,0},{2,3},{3,2},{4,5},{5,4},{6,7},{7,6},{8,9},{9,8},{10,11... | collective-permute-start | bytes 786440 | tf_op jit(solution)/shard_map/ppermute | solution.py:202
  30.8 9.8 %collective-permute-start.10 = (bf16[8,128,128]{2,1,0:T(8,128)(2,1)S(1)}, bf16[8,128,128]{2,1,0:T(8,128)(2,1)S(1)}, u32[]{:S(2)}, u32[]{:S(2)}) collective-permute-start(bf16[8,128,128]{2,1,0:T(8,128)(2,1)S(1)} %get-tuple-element.29.refs_1_), channel_id=1, source_target_pairs={{0,1},{1,0},{2,3},{3,2},{4,5},{5,4},{6,7},{7,6},{8,9},{9,8},{10,11... | collective-permute-start | bytes 786440 | tf_op jit(solution)/shard_map/ppermute | solution.py:202
  30.9 9.8 %collective-permute-start.9 = (bf16[8,128,128]{2,1,0:T(8,128)(2,1)S(1)}, bf16[8,128,128]{2,1,0:T(8,128)(2,1)S(1)}, u32[]{:S(2)}, u32[]{:S(2)}) collective-permute-start(bf16[8,128,128]{2,1,0:T(8,128)(2,1)S(1)} %get-tuple-element.28.refs_0_), channel_id=1, source_target_pairs={{8,0},{16,8},{24,16},{0,24},{9,1},{17,9},{25,17},{1,25},{10,2},{18... | collective-permute-start | bytes 786440 | tf_op jit(solution)/shard_map/ppermute | solution.py:201
  30.9 10.3 %collective-permute-start.6 = (bf16[8,128,128]{2,1,0:T(8,128)(2,1)S(1)}, bf16[8,128,128]{2,1,0:T(8,128)(2,1)S(1)}, u32[]{:S(2)}, u32[]{:S(2)}) collective-permute-start(bf16[8,128,128]{2,1,0:T(8,128)(2,1)S(1)} %get-tuple-element.29.refs_1_), channel_id=1, source_target_pairs={{0,8},{8,16},{16,24},{24,0},{1,9},{9,17},{17,25},{25,1},{2,10},{10... | collective-permute-start | bytes 786440 | tf_op jit(solution)/shard_map/ppermute | solution.py:201
  37.1 10.4 %collective-permute-start.8 = (bf16[8,128,128]{2,1,0:T(8,128)(2,1)S(1)}, bf16[8,128,128]{2,1,0:T(8,128)(2,1)S(1)}, u32[]{:S(2)}, u32[]{:S(2)}) collective-permute-start(bf16[8,128,128]{2,1,0:T(8,128)(2,1)S(1)} %collective-permute-done.7.refs_1_), channel_id=1, source_target_pairs={{0,2},{1,7},{2,4},{3,1},{4,6},{5,3},{6,0},{7,5},{8,10},{9,15},{10,... | collective-permute-start | bytes 786440 | tf_op jit(solution)/shard_map/ppermute | solution.py:203
  40.6 10.2 %collective-permute-start.11 = (bf16[8,128,128]{2,1,0:T(8,128)(2,1)S(1)}, bf16[8,128,128]{2,1,0:T(8,128)(2,1)S(1)}, u32[]{:S(2)}, u32[]{:S(2)}) collective-permute-start(bf16[8,128,128]{2,1,0:T(8,128)(2,1)S(1)} %collective-permute-done.10.refs_1_), channel_id=1, source_target_pairs={{0,2},{1,7},{2,4},{3,1},{4,6},{5,3},{6,0},{7,5},{8,10},{9,15},{10,... | collective-permute-start | bytes 786440 | tf_op jit(solution)/shard_map/ppermute | solution.py:203
  47.8 9.0 %collective-permute-start.13 = (bf16[8,128,128]{2,1,0:T(8,128)(2,1)S(1)}, bf16[8,128,128]{2,1,0:T(8,128)(2,1)S(1)}, u32[]{:S(2)}, u32[]{:S(2)}) collective-permute-start(bf16[8,128,128]{2,1,0:T(8,128)(2,1)S(1)} %get-tuple-element.33.refs_0_), channel_id=1, source_target_pairs={{0,1},{1,0},{2,3},{3,2},{4,5},{5,4},{6,7},{7,6},{8,9},{9,8},{10,11... | collective-permute-start | bytes 786440 | tf_op jit(solution)/shard_map/ppermute | solution.py:202
  51.2 8.7 %collective-permute-start.16 = (bf16[8,128,128]{2,1,0:T(8,128)(2,1)S(1)}, bf16[8,128,128]{2,1,0:T(8,128)(2,1)S(1)}, u32[]{:S(2)}, u32[]{:S(2)}) collective-permute-start(bf16[8,128,128]{2,1,0:T(8,128)(2,1)S(1)} %get-tuple-element.37.refs_1_), channel_id=1, source_target_pairs={{0,1},{1,0},{2,3},{3,2},{4,5},{5,4},{6,7},{7,6},{8,9},{9,8},{10,11... | collective-permute-start | bytes 786440 | tf_op jit(solution)/shard_map/ppermute | solution.py:202
  51.5 8.4 %collective-permute-start.12 = (bf16[8,128,128]{2,1,0:T(8,128)(2,1)S(1)}, bf16[8,128,128]{2,1,0:T(8,128)(2,1)S(1)}, u32[]{:S(2)}, u32[]{:S(2)}) collective-permute-start(bf16[8,128,128]{2,1,0:T(8,128)(2,1)S(1)} %get-tuple-element.37.refs_1_), channel_id=1, source_target_pairs={{0,8},{8,16},{16,24},{24,0},{1,9},{9,17},{17,25},{25,1},{2,10},{10... | collective-permute-start | bytes 786440 | tf_op jit(solution)/shard_map/ppermute | solution.py:201
  51.5 9.0 %collective-permute-start.15 = (bf16[8,128,128]{2,1,0:T(8,128)(2,1)S(1)}, bf16[8,128,128]{2,1,0:T(8,128)(2,1)S(1)}, u32[]{:S(2)}, u32[]{:S(2)}) collective-permute-start(bf16[8,128,128]{2,1,0:T(8,128)(2,1)S(1)} %get-tuple-element.33.refs_0_), channel_id=1, source_target_pairs={{8,0},{16,8},{24,16},{0,24},{9,1},{17,9},{25,17},{1,25},{10,2},{18... | collective-permute-start | bytes 786440 | tf_op jit(solution)/shard_map/ppermute | solution.py:201
  56.8 10.6 %collective-permute-start.14 = (bf16[8,128,128]{2,1,0:T(8,128)(2,1)S(1)}, bf16[8,128,128]{2,1,0:T(8,128)(2,1)S(1)}, u32[]{:S(2)}, u32[]{:S(2)}) collective-permute-start(bf16[8,128,128]{2,1,0:T(8,128)(2,1)S(1)} %collective-permute-done.13.refs_1_), channel_id=1, source_target_pairs={{0,2},{1,7},{2,4},{3,1},{4,6},{5,3},{6,0},{7,5},{8,10},{9,15},{10,... | collective-permute-start | bytes 786440 | tf_op jit(solution)/shard_map/ppermute | solution.py:203
  59.9 10.4 %collective-permute-start.17 = (bf16[8,128,128]{2,1,0:T(8,128)(2,1)S(1)}, bf16[8,128,128]{2,1,0:T(8,128)(2,1)S(1)}, u32[]{:S(2)}, u32[]{:S(2)}) collective-permute-start(bf16[8,128,128]{2,1,0:T(8,128)(2,1)S(1)} %collective-permute-done.16.refs_1_), channel_id=1, source_target_pairs={{0,2},{1,7},{2,4},{3,1},{4,6},{5,3},{6,0},{7,5},{8,10},{9,15},{10,... | collective-permute-start | bytes 786440 | tf_op jit(solution)/shard_map/ppermute | solution.py:203
  68.6 8.0 %collective-permute-start.22 = (bf16[8,128,128]{2,1,0:T(8,128)(2,1)S(1)}, bf16[8,128,128]{2,1,0:T(8,128)(2,1)S(1)}, u32[]{:S(2)}, u32[]{:S(2)}) collective-permute-start(bf16[8,128,128]{2,1,0:T(8,128)(2,1)S(1)} %get-tuple-element.46.refs_0_), channel_id=1, source_target_pairs={{0,1},{1,0},{2,3},{3,2},{4,5},{5,4},{6,7},{7,6},{8,9},{9,8},{10,11... | collective-permute-start | bytes 786440 | tf_op jit(solution)/shard_map/ppermute | solution.py:202
  71.4 8.0 %collective-permute-start.19 = (bf16[8,128,128]{2,1,0:T(8,128)(2,1)S(1)}, bf16[8,128,128]{2,1,0:T(8,128)(2,1)S(1)}, u32[]{:S(2)}, u32[]{:S(2)}) collective-permute-start(bf16[8,128,128]{2,1,0:T(8,128)(2,1)S(1)} %get-tuple-element.47.refs_1_), channel_id=1, source_target_pairs={{0,1},{1,0},{2,3},{3,2},{4,5},{5,4},{6,7},{7,6},{8,9},{9,8},{10,11... | collective-permute-start | bytes 786440 | tf_op jit(solution)/shard_map/ppermute | solution.py:202
  71.7 8.7 %collective-permute-start.21 = (bf16[8,128,128]{2,1,0:T(8,128)(2,1)S(1)}, bf16[8,128,128]{2,1,0:T(8,128)(2,1)S(1)}, u32[]{:S(2)}, u32[]{:S(2)}) collective-permute-start(bf16[8,128,128]{2,1,0:T(8,128)(2,1)S(1)} %get-tuple-element.47.refs_1_), channel_id=1, source_target_pairs={{0,8},{8,16},{16,24},{24,0},{1,9},{9,17},{17,25},{25,1},{2,10},{10... | collective-permute-start | bytes 786440 | tf_op jit(solution)/shard_map/ppermute | solution.py:201
  71.7 9.3 %collective-permute-start.18 = (bf16[8,128,128]{2,1,0:T(8,128)(2,1)S(1)}, bf16[8,128,128]{2,1,0:T(8,128)(2,1)S(1)}, u32[]{:S(2)}, u32[]{:S(2)}) collective-permute-start(bf16[8,128,128]{2,1,0:T(8,128)(2,1)S(1)} %get-tuple-element.46.refs_0_), channel_id=1, source_target_pairs={{8,0},{16,8},{24,16},{0,24},{9,1},{17,9},{25,17},{1,25},{10,2},{18... | collective-permute-start | bytes 786440 | tf_op jit(solution)/shard_map/ppermute | solution.py:201
  76.6 9.6 %collective-permute-start.23 = (bf16[8,128,128]{2,1,0:T(8,128)(2,1)S(1)}, bf16[8,128,128]{2,1,0:T(8,128)(2,1)S(1)}, u32[]{:S(2)}, u32[]{:S(2)}) collective-permute-start(bf16[8,128,128]{2,1,0:T(8,128)(2,1)S(1)} %collective-permute-done.22.refs_1_), channel_id=1, source_target_pairs={{0,2},{1,7},{2,4},{3,1},{4,6},{5,3},{6,0},{7,5},{8,10},{9,15},{10,... | collective-permute-start | bytes 786440 | tf_op jit(solution)/shard_map/ppermute | solution.py:203
  79.4 9.6 %collective-permute-start.20 = (bf16[8,128,128]{2,1,0:T(8,128)(2,1)S(1)}, bf16[8,128,128]{2,1,0:T(8,128)(2,1)S(1)}, u32[]{:S(2)}, u32[]{:S(2)}) collective-permute-start(bf16[8,128,128]{2,1,0:T(8,128)(2,1)S(1)} %collective-permute-done.19.refs_1_), channel_id=1, source_target_pairs={{0,2},{1,7},{2,4},{3,1},{4,6},{5,3},{6,0},{7,5},{8,10},{9,15},{10,... | collective-permute-start | bytes 786440 | tf_op jit(solution)/shard_map/ppermute | solution.py:203
  (3 other events, 29.3 us)

commit v2 on v0

v2 whole, which is shorter than its diff:
```python
import functools

import jax
import jax.numpy as jnp
from jax import lax
from jax.experimental import pallas as pl
from jax.experimental.pallas import tpu as pltpu
from jax.sharding import PartitionSpec as P

LY = 4
LZ = 2
STEPS = 4
PIECES = 2

diagonal_shift = 1.5
center_value = 1.5
half_width = 1.0

F32, BF16 = jnp.float32, jnp.bfloat16
WHOLE = pl.BlockSpec(memory_space=pltpu.VMEM)
VMEM_LIMIT = 32 * 1024 * 1024


def coefficients():
    ratio = half_width / center_value
    out = []
    for _ in range(STEPS - 1):
        ratio_next = 1.0 / (2.0 * center_value / half_width - ratio)
        out.append((ratio_next * ratio, 2.0 * ratio_next / half_width))
        ratio = ratio_next
    return out


def call(kernel, outs, operands, flops, name, aliases=None, out_specs=None, in_specs=None, scratch=()):
    nbytes = sum(o.size * o.dtype.itemsize for o in operands)
    in_specs = in_specs or [WHOLE] * len(operands)
    out_specs = out_specs or [WHOLE] * len(outs)
    operands = [
        pltpu.with_memory_space_constraint(o, pltpu.VMEM) if s is WHOLE else o
        for o, s in zip(operands, in_specs)
    ]
    return pl.pallas_call(
        kernel,
        out_shape=outs,
        in_specs=in_specs,
        out_specs=out_specs,
        input_output_aliases=aliases or {},
        scratch_shapes=scratch,
        compiler_params=pltpu.CompilerParams(vmem_limit_bytes=VMEM_LIMIT),
        cost_estimate=pl.CostEstimate(flops=flops, bytes_accessed=nbytes, transcendentals=0),
        name=name,
    )(*operands)


def real_form(block):
    block = block.astype(F32)
    half = block.shape[-1] // 2
    lane = lax.broadcasted_iota(jnp.int32, block.shape, 1)
    upper = jnp.where(lane < half, block, -block)
    lower = pltpu.roll(block, half, 1)
    return jnp.concatenate([upper, lower], axis=0)


def gather_kernel(hop_hbm, out, sem):
    sites = out.shape[0]
    base = pl.multiple_of(lax.axis_index("group") * sites, sites)
    copy = pltpu.make_async_copy(hop_hbm.at[0, pl.ds(base, sites), pl.ds(6, 2)], out, sem)
    copy.start()
    copy.wait()


def gather_time(hop_blocks, sites):
    comps, width = hop_blocks.shape[3:]
    return call(
        gather_kernel,
        [pltpu.VMEM((sites, 2, comps, width), BF16)],
        [pltpu.with_memory_space_constraint(hop_blocks, pltpu.HBM)],
        0,
        "time_blocks",
        in_specs=[pl.BlockSpec(memory_space=pltpu.HBM)],
        scratch=[pltpu.SemaphoreType.DMA],
    )[0]


def prep_time_kernel(blocks, time_ref):
    sites, width = time_ref.shape[:2]
    parity = (lax.axis_index("site") + lax.axis_index("group")) % 2
    for site in range(sites):
        time_ref[site, :, :width] = real_form(blocks[site, parity]).astype(BF16)
        time_ref[site, :, width:] = real_form(blocks[site, 1 - parity]).astype(BF16)


def prep_kernel(plane_sites, batch, self_hbm, hop_hbm, local_ref, self_ref, hop_ref, sems):
    sites, width = local_ref.shape[:2]
    base = pl.multiple_of(lax.axis_index("group") * sites, sites)
    copies = []
    for i in range(sites // batch):
        there, here = pl.ds(base + i * batch, batch), pl.ds(i * batch, batch)
        copies.append(
            (
                pltpu.make_async_copy(
                    hop_hbm.at[0, there, pl.ds(0, 6)], hop_ref.at[here], sems.at[0, i]
                ),
                pltpu.make_async_copy(self_hbm.at[0, there], self_ref.at[here], sems.at[1, i]),
            )
        )
        for copy in copies[i]:
            copy.start()
    for site in range(sites):
        if site % batch == 0:
            for copy in copies[site // batch]:
                copy.wait()
        plane = site // plane_sites
        hop = lambda m: real_form(hop_ref[site, m])
        parts = [
            real_form(self_ref[site]),
            hop(plane),
            hop(2),
            hop(3),
            hop(4) + hop(5),
            hop(1 - plane),
        ]
        for k, part in enumerate(parts):
            local_ref[site, :, k * width : (k + 1) * width] = part.astype(BF16)


def prep(self_block, hop_blocks, sites, plane_sites):
    comps, width = self_block.shape[2:]
    batch = 2
    in_hbm = pl.BlockSpec(memory_space=pltpu.HBM)
    return call(
        functools.partial(prep_kernel, plane_sites, batch),
        [pltpu.VMEM((sites, width, 6 * width), BF16)],
        [
            pltpu.with_memory_space_constraint(self_block, pltpu.HBM),
            pltpu.with_memory_space_constraint(hop_blocks, pltpu.HBM),
        ],
        0,
        "prep",
        in_specs=[in_hbm, in_hbm],
        scratch=[
            pltpu.VMEM((sites, comps, width), BF16),
            pltpu.VMEM((sites, 6, comps, width), BF16),
            pltpu.SemaphoreType.DMA((2, sites // batch)),
        ],
    )[0]


def times(vector, weight):
    return lax.dot_general(
        vector, weight, (((1,), (1,)), ((), ())), preferred_element_type=F32
    )


def store_edges(offset, size, plane_sites, sent_out, core_out, chip_out):
    odd = lax.axis_index("group") % 2
    for plane in range(2):
        low = max(offset, plane * plane_sites)
        high = min(offset + size, (plane + 1) * plane_sites)
        if low >= high:
            continue
        here = pl.ds(low - offset, high - low)
        there = pl.ds(low - plane * plane_sites, high - low)

        @pl.when(odd == 1 - plane)
        def _():
            core_out[there] = sent_out[here]

        @pl.when(odd == plane)
        def _():
            chip_out[there] = sent_out[here]


def init_kernel(offset, plane_sites, size, residual, *refs):
    sent_out, core_out, chip_out = refs[-3:]
    for s in range(size):
        new = residual[0, offset + s].astype(F32) * (half_width / center_value)
        sent_out[s] = new.astype(BF16)
    store_edges(offset, size, plane_sites, sent_out, core_out, chip_out)


def local_kernel(plane_sites, offsets, first, *refs):
    pieces = len(offsets) - 1
    sent = refs[:pieces]
    core_halo, chip_halo, weight = refs[pieces : pieces + 3]
    residual = refs[pieces + 3 : -1]
    acc = refs[-1]

    def at(of, site):
        piece = max(i for i in range(pieces) if offsets[i] <= site)
        return of[piece][site - offsets[piece]]

    odd = lax.axis_index("group") % 2
    for plane in range(2):
        base = plane * plane_sites
        by_core = odd == 1 - plane
        for s in range(plane_sites):
            y, z = s // LZ, s % LZ
            own = at(sent, base + s)
            around = jnp.concatenate(
                [
                    own,
                    at(sent, (1 - plane) * plane_sites + s),
                    at(sent, base + (y + 1) % LY * LZ + z),
                    at(sent, base + (y - 1) % LY * LZ + z),
                    at(sent, base + y * LZ + 1 - z),
                    jnp.where(by_core, core_halo[s], chip_halo[s]),
                ],
                axis=1,
            )
            now = residual[0][0, base + s].astype(F32) if first else at(residual, base + s)
            acc[base + s] = (
                now - diagonal_shift * own.astype(F32) - times(around, weight[base + s])
            )


def middle_kernel(offset, size, near, own, weight, out):
    odd = lax.axis_index("group") % 2

    @pl.when(odd == 0)
    def _():
        out[...] = near[...]

    @pl.when(odd == 1)
    def _():
        for s in range(size):
            around = jnp.concatenate([own[s], near[s]], axis=1)
            out[s] = times(around, weight[offset + s]).astype(BF16)


def time_kernel(offset, size, plane_sites, mode, scale, *refs):
    acc, near, far, weight = refs[:4]
    if mode == "last":
        whole, out, sems = refs[-3:]
        copies = [
            pltpu.make_async_copy(out.at[s], whole.at[0, offset + s], sems.at[s])
            for s in range(size)
        ]
    else:
        direction = refs[4]
        out, direction_out, sent_out, core_out, chip_out = refs[-5:]

    def finish(s, now):
        out[s] = now
        if mode == "last":
            return
        if mode == "first":
            old = direction[0, offset + s].astype(F32) * (half_width / center_value)
        else:
            old = direction[s]
        new = scale[0] * old + scale[1] * now
        direction_out[s] = new
        sent_out[s] = new.astype(BF16)

    odd = lax.axis_index("group") % 2

    @pl.when(odd == 0)
    def _():
        for s in range(size):
            around = jnp.concatenate([near[s], far[s]], axis=1)
            finish(s, acc[offset + s] - times(around, weight[offset + s]))

    @pl.when(odd == 1)
    def _():
        for s in range(size):
            finish(s, acc[offset + s] - far[s].astype(F32))

    if mode == "last":
        for copy in copies:
            copy.start()
        for copy in copies:
            copy.wait()
    else:
        store_edges(offset, size, plane_sites, sent_out, core_out, chip_out)


def sum_kernel(offsets, residual, *refs):
    out = refs[-1]
    pieces = len(offsets) - 1
    for i in range(pieces):
        for s in range(offsets[i + 1] - offsets[i]):
            site = offsets[i] + s
            total = residual[0, site].astype(F32) * (half_width / center_value)
            for k in range(STEPS - 1):
                total = total + refs[k * pieces + i][s]
            out[0, site] = total


def body(residual_in, self_block, hop_blocks):
    _, sites, count, width = residual_in.shape
    plane_sites = LY * LZ
    groups, slices = lax.axis_size("group"), lax.axis_size("site")
    assert sites == 2 * plane_sites and slices % 2 == 0 and groups % 2 == 0
    offsets = [-(-i * sites // PIECES) for i in range(PIECES + 1)]
    sizes = [b - a for a, b in zip(offsets, offsets[1:])]
    swap = lambda t: t ^ 1
    relay = lambda t: (t + 2 - 4 * (t % 2)) % slices
    shift = lambda t: (t - 2 + 4 * (t % 2)) % slices
    every = lambda even, odd: [
        (g * slices + t, g * slices + (odd if g % 2 else even)(t))
        for g in range(groups)
        for t in range(slices)
    ]
    exchange = every(lambda t: t, swap)
    first_hop, second_hop = every(swap, shift), every(relay, swap)
    axes = ("group", "site")
    cores = [(i, i ^ 1) for i in range(groups)]
    chips = [(i, (i - 1 + 2 * (i % 2)) % groups) for i in range(groups)]

    block = (count, width)
    mac = 2 * count * width * width
    scales = coefficients()
    edge = pltpu.VMEM((plane_sites,) + block, BF16)

    residual_in = pltpu.with_memory_space_constraint(residual_in, pltpu.VMEM)
    sent = [None] * PIECES
    edges = []
    for i in range(PIECES):
        sent[i], *edges = call(
            functools.partial(init_kernel, offsets[i], plane_sites, sizes[i]),
            [pltpu.VMEM((sizes[i],) + block, BF16), edge, edge],
            [residual_in, *edges],
            0,
            "first_direction",
            aliases={1: 1, 2: 2} if edges else None,
        )
    time_blocks = lax.ppermute(gather_time(hop_blocks, sites), axes, exchange)
    weight_time = call(
        prep_time_kernel, [pltpu.VMEM((sites, width, 2 * width), BF16)], [time_blocks], 0, "prep_time"
    )[0]
    weight_local = prep(self_block, hop_blocks, sites, plane_sites)
    residual = [residual_in]
    direction = [residual_in] * PIECES
    directions = []
    for number in range(STEPS):
        first, last = number == 0, number == STEPS - 1
        near = [lax.ppermute(v, axes, first_hop) for v in sent]
        core_halo = lax.ppermute(edges[0], "group", cores)
        chip_halo = lax.ppermute(edges[1], "group", chips)
        far = [
            lax.ppermute(
                call(
                    functools.partial(middle_kernel, offsets[i], sizes[i]),
                    [pltpu.VMEM((sizes[i],) + block, BF16)],
                    [near[i], sent[i], weight_time],
                    sizes[i] * 2 * mac,
                    "second_message",
                )[0],
                axes,
                second_hop,
            )
            for i in range(PIECES)
        ]
        acc = call(
            functools.partial(local_kernel, plane_sites, offsets, first),
            [pltpu.VMEM((sites,) + block, F32)],
            [*sent, core_halo, chip_halo, weight_local, *residual],
            sites * 6 * mac,
            "local_terms",
        )[0]
        mode = "first" if first else "last" if last else "middle"
        edges = []
        result = []
        residual = [None] * PIECES
        if last:
            correction = call(
                functools.partial(sum_kernel, offsets),
                [jax.ShapeDtypeStruct((1, sites) + block, F32)],
                [residual_in, *sum(directions, [])],
                0,
                "correction",
            )[0]
        for i in range(PIECES):
            scale = None if last else scales[number]
            kernel = functools.partial(
                time_kernel, offsets[i], sizes[i], plane_sites, mode, scale
            )
            operands = [acc, near[i], far[i], weight_time]
            flops = sizes[i] * 2 * mac
            if last:
                in_hbm = pl.BlockSpec(memory_space=pltpu.HBM)
                result = call(
                    kernel,
                    [jax.ShapeDtypeStruct((1, sites) + block, F32)],
                    [*operands, *result],
                    flops,
                    "time_terms_last",
                    aliases={4: 0} if result else None,
                    in_specs=[WHOLE] * 4 + [in_hbm] * len(result),
                    out_specs=[in_hbm],
                    scratch=[
                        pltpu.VMEM((sizes[i],) + block, F32),
                        pltpu.SemaphoreType.DMA((sizes[i],)),
                    ],
                )
                continue
            piece = lambda kind: pltpu.VMEM((sizes[i],) + block, kind)
            residual[i], direction[i], sent[i], *edges = call(
                kernel,
                [piece(F32), piece(F32), piece(BF16), edge, edge],
                operands + [direction[i], *edges],
                flops,
                "time_terms",
                aliases={5: 3, 6: 4} if edges else None,
            )
        directions.append(list(direction))
    return correction, result[0]


def solution(mesh):
    return jax.shard_map(
        body,
        mesh=mesh,
        in_specs=(
            P("site", "group", None, None),
            P("site", None, None, None),
            P("site", None, None, None, None),
        ),
        out_specs=(P("site", "group", None, None), P("site", "group", None, None)),
        check_vma=False,
    )
```

time: 231 us -> 81.7 us (0.35)
  matrix products: 56 us -> 0 us
  waiting for transfers between devices: 83.4 us -> 39.7 us
  other arithmetic: 31.2 us -> 0 us
  blocking collectives: 24.6 us -> 0 us
  local copies, waits for them, and re-layouts: 16 us -> 0.01 us
  Pallas kernels: 0 us -> 13.2 us
  starting transfers between devices: 18 us -> 27.6 us
    dot_general x8 -> x0, matrix products: 56 us -> none  [the longest x4 50.4 us: apply_blocks(): jnp.einsum('tsmab,tsmkb->tska', own_hops, paired(around), preferred_eleme...]
    ppermute x8 -> x25, waiting for transfers between devices: 75.8 us -> 39.7 us  [the longest x8 16.7 us: body(): near = [lax.ppermute(v, axes, first_hop) for v in sent]]
    all_to_all x2 -> x0, blocking collectives: 24.6 us -> none  [the longest x1 12.9 us: body(): lax.all_to_all(residual_in, 'group', split_axis=2, concat_axis=1, tiled=T...]
    neg x8 -> x0, other arithmetic: 21.4 us -> none  [paired(): conjugate = jnp.concatenate([real_part, -imag_part], axis=-1)]
    pallas_call x0 -> x26, Pallas kernels: none -> 13.2 us  [call(): pl.pallas_call(kernel, out_shape=outs, in_specs=in_specs, out_specs=out_s...]
    ppermute x8 -> x25, starting transfers between devices: 14.6 us -> 27.6 us  [the longest x4 9.69 us: body(): core_halo = lax.ppermute(edges[0], 'group', cores)]
    slice x24 -> x0, local copies, waits for them, and re-layouts: 8.79 us -> none  [the longest x4 7.04 us: apply_blocks(): mixed = jnp.concatenate([total[:, :, :count], total[:, :, count:]], axis=-1)]
    convert_element_type x11 -> x0, other arithmetic: 8.78 us -> none  [the longest x8 6.75 us: body(): sent = direction.astype(jnp.bfloat16)]
  transfers between devices with their start and end apart: 9 -> 25, of which waited for: 5 -> 13; matrix products, arithmetic and copies ran while one was open for 5% -> 0% of each run, Pallas kernels for 0% -> 13%
where the time goes in v2:
time: 81.7 us; the launch traced here: 81.5 us
  waiting for transfers between devices  39.7 us (49%)
  starting transfers between devices  27.6 us (34%)
  Pallas kernels  13.2 us (16%)
  between operations  0.98 us (1%)
    ppermute x8, waiting for transfers between devices, body(): near = [lax.ppermute(v, axes, first_hop) for v in sent]  16.7 us
    ppermute x8, waiting for transfers between devices, body(): lax.ppermute(call(functools.partial(middle_kernel, offsets[i], sizes[i]),...  13.7 us
    pallas_call x26, Pallas kernels, call(): pl.pallas_call(kernel, out_shape=outs, in_specs=in_specs, out_specs=out_s...  13.2 us
    ppermute x4, starting transfers between devices, body(): core_halo = lax.ppermute(edges[0], 'group', cores)  9.69 us
    ppermute x4, waiting for transfers between devices, body(): chip_halo = lax.ppermute(edges[1], 'group', chips)  9.33 us
    ppermute x8, starting transfers between devices, body(): near = [lax.ppermute(v, axes, first_hop) for v in sent]  7.24 us
    ppermute x8, starting transfers between devices, body(): lax.ppermute(call(functools.partial(middle_kernel, offsets[i], sizes[i]),...  5.06 us
    ppermute x4, starting transfers between devices, body(): chip_halo = lax.ppermute(edges[1], 'group', chips)  4.87 us
  transfers between devices with their start and end apart: 25, of which 13 were waited for; matrix products, arithmetic and copies ran while one was open for 0% of the time, Pallas kernels for 13%

profile of v2, /device:TPU:0, one launch (start us, length us, event | category | flops | bytes accessed | tf_op | source)
XLA Modules:
  0.0 81.5 jit_solution(13932970481577769627)
XLA Ops:
  0.6 1.1 %time_blocks.1 = bf16[16,2,64,128]{3,2,1,0:T(8,128)(2,1)S(1)} custom-call(bf16[1,64,8,64,128]{4,3,2,1,0:T(8,128)(2,1)} %hop_hbm.3), custom_call_target="tpu_custom_call" | custom-call | bytes 8388608 | tf_op jit(solution)/shard_map/time_blocks/pallas_call | solution.py:42
  2.5 3.0 %collective-permute-start.2 = (bf16[8,128,128]{2,1,0:T(8,128)(2,1)S(1)}, bf16[8,128,128]{2,1,0:T(8,128)(2,1)S(1)}, u32[]{:S(2)}, u32[]{:S(2)}) collective-permute-start(bf16[8,128,128]{2,1,0:T(8,128)(2,1)S(1)} %get-tuple-element.38.refs_0_.own), channel_id=1, source_target_pairs={{0,1},{1,0},{2,3},{3,2},{4,5},{5,4},{6,7},{7,6},{8,14},{9,11},{10,... | collective-permute-start | bytes 786440 | tf_op jit(solution)/shard_map/ppermute | solution.py:337
  5.7 4.2 %collective-permute-start = (bf16[8,128,128]{2,1,0:T(8,128)(2,1)S(1)}, bf16[8,128,128]{2,1,0:T(8,128)(2,1)S(1)}, u32[]{:S(2)}, u32[]{:S(2)}) collective-permute-start(bf16[8,128,128]{2,1,0:T(8,128)(2,1)S(1)} %get-tuple-element.42), channel_id=1, source_target_pairs={{0,8},{8,0},{16,24},{24,16},{1,9},{9,1},{17,25},{25,17},{2,10},{10... | collective-permute-start | bytes 786440 | tf_op jit(solution)/shard_map/ppermute | solution.py:338
  9.9 1.1 %collective-permute-start.1 = (bf16[8,128,128]{2,1,0:T(8,128)(2,1)S(1)}, bf16[8,128,128]{2,1,0:T(8,128)(2,1)S(1)}, u32[]{:S(2)}, u32[]{:S(2)}) collective-permute-start(bf16[8,128,128]{2,1,0:T(8,128)(2,1)S(1)} %get-tuple-element.43), channel_id=1, source_target_pairs={{0,24},{8,16},{16,8},{24,0},{1,25},{9,17},{17,9},{25,1},{2,26},{10... | collective-permute-start | bytes 786440 | tf_op jit(solution)/shard_map/ppermute | solution.py:339
  11.3 1.2 %collective-permute-done.2.near.refs_1_ = bf16[8,128,128]{2,1,0:T(8,128)(2,1)S(1)} collective-permute-done((bf16[8,128,128]{2,1,0:T(8,128)(2,1)S(1)}, bf16[8,128,128]{2,1,0:T(8,128)(2,1)S(1)}, u32[]{:S(2)}, u32[]{:S(2)}) %collective-permute-start.2) | collective-permute-done | bytes 262176 | tf_op jit(solution)/shard_map/ppermute | solution.py:337
  12.5 2.3 %collective-permute-start.4 = (bf16[8,128,128]{2,1,0:T(8,128)(2,1)S(1)}, bf16[8,128,128]{2,1,0:T(8,128)(2,1)S(1)}, u32[]{:S(2)}, u32[]{:S(2)}) collective-permute-start(bf16[8,128,128]{2,1,0:T(8,128)(2,1)S(1)} %second_message.8), channel_id=1, source_target_pairs={{0,2},{1,7},{2,4},{3,1},{4,6},{5,3},{6,0},{7,5},{8,9},{9,8},{10,11... | collective-permute-start | bytes 786440 | tf_op jit(solution)/shard_map/ppermute | solution.py:341
  14.9 3.2 %collective-permute-done.5.near.refs_1_ = bf16[8,128,128]{2,1,0:T(8,128)(2,1)S(1)} collective-permute-done((bf16[8,128,128]{2,1,0:T(8,128)(2,1)S(1)}, bf16[8,128,128]{2,1,0:T(8,128)(2,1)S(1)}, u32[]{:S(2)}, u32[]{:S(2)}) %collective-permute-start.5) | collective-permute-done | bytes 262176 | tf_op jit(solution)/shard_map/ppermute | solution.py:337
  18.2 2.3 %collective-permute-start.6 = (bf16[8,128,128]{2,1,0:T(8,128)(2,1)S(1)}, bf16[8,128,128]{2,1,0:T(8,128)(2,1)S(1)}, u32[]{:S(2)}, u32[]{:S(2)}) collective-permute-start(bf16[8,128,128]{2,1,0:T(8,128)(2,1)S(1)} %second_message.9), channel_id=1, source_target_pairs={{0,2},{1,7},{2,4},{3,1},{4,6},{5,3},{6,0},{7,5},{8,9},{9,8},{10,11... | collective-permute-start | bytes 786440 | tf_op jit(solution)/shard_map/ppermute | solution.py:341
  20.4 2.2 %prep.1.refs_4_ = bf16[16,128,768]{2,1,0:T(8,128)(2,1)S(1)} custom-call(bf16[1,64,64,128]{3,2,1,0:T(8,128)(2,1)} %self_hbm.1, bf16[1,64,8,64,128]{4,3,2,1,0:T(8,128)(2,1)} %hop_hbm.3), custom_call_target="tpu_custom_call" | custom-call | bytes 9437184 | tf_op jit(solution)/shard_map/prep/pallas_call | solution.py:42
  24.0 3.6 %collective-permute-start.9 = (bf16[8,128,128]{2,1,0:T(8,128)(2,1)S(1)}, bf16[8,128,128]{2,1,0:T(8,128)(2,1)S(1)}, u32[]{:S(2)}, u32[]{:S(2)}) collective-permute-start(bf16[8,128,128]{2,1,0:T(8,128)(2,1)S(1)} %get-tuple-element.48.refs_0_.own), channel_id=1, source_target_pairs={{0,1},{1,0},{2,3},{3,2},{4,5},{5,4},{6,7},{7,6},{8,14},{9,11},{10,... | collective-permute-start | bytes 786440 | tf_op jit(solution)/shard_map/ppermute | solution.py:337
  28.2 4.6 %collective-permute-start.7 = (bf16[8,128,128]{2,1,0:T(8,128)(2,1)S(1)}, bf16[8,128,128]{2,1,0:T(8,128)(2,1)S(1)}, u32[]{:S(2)}, u32[]{:S(2)}) collective-permute-start(bf16[8,128,128]{2,1,0:T(8,128)(2,1)S(1)} %get-tuple-element.50), channel_id=1, source_target_pairs={{0,8},{8,0},{16,24},{24,16},{1,9},{9,1},{17,25},{25,17},{2,10},{10... | collective-permute-start | bytes 786440 | tf_op jit(solution)/shard_map/ppermute | solution.py:338
  34.9 6.3 %collective-permute-done.8.refs_3_ = bf16[8,128,128]{2,1,0:T(8,128)(2,1)S(1)} collective-permute-done((bf16[8,128,128]{2,1,0:T(8,128)(2,1)S(1)}, bf16[8,128,128]{2,1,0:T(8,128)(2,1)S(1)}, u32[]{:S(2)}, u32[]{:S(2)}) %collective-permute-start.8) | collective-permute-done | bytes 262176 | tf_op jit(solution)/shard_map/ppermute | solution.py:339
  41.3 1.0 %local_terms.5.refs_0_ = f32[16,128,128]{2,1,0:T(8,128)S(1)} custom-call(bf16[8,128,128]{2,1,0:T(8,128)(2,1)S(1)} %get-tuple-element.48.refs_0_.own, bf16[8,128,128]{2,1,0:T(8,128)(2,1)S(1)} %get-tuple-element.49.refs_1_.own, bf16[8,128,128]{2,1,0:T(8,128)(2,1)S(1)} %collective-permute-done.7.refs_2_, ...), custom_call_target="tpu_custom_call" | custom-call | flops 402653184 | bytes 5242880 | tf_op jit(solution)/shard_map/local_terms/pallas_call | solution.py:42
  42.7 2.9 %collective-permute-done.12.refs_2_ = bf16[8,128,128]{2,1,0:T(8,128)(2,1)S(1)} collective-permute-done((bf16[8,128,128]{2,1,0:T(8,128)(2,1)S(1)}, bf16[8,128,128]{2,1,0:T(8,128)(2,1)S(1)}, u32[]{:S(2)}, u32[]{:S(2)}) %collective-permute-start.12) | collective-permute-done | bytes 262176 | tf_op jit(solution)/shard_map/ppermute | solution.py:341
  46.7 2.2 %collective-permute-start.14 = (bf16[8,128,128]{2,1,0:T(8,128)(2,1)S(1)}, bf16[8,128,128]{2,1,0:T(8,128)(2,1)S(1)}, u32[]{:S(2)}, u32[]{:S(2)}) collective-permute-start(bf16[8,128,128]{2,1,0:T(8,128)(2,1)S(1)} %get-tuple-element.61), channel_id=1, source_target_pairs={{0,24},{8,16},{16,8},{24,0},{1,25},{9,17},{17,9},{25,1},{2,26},{10... | collective-permute-start | bytes 786440 | tf_op jit(solution)/shard_map/ppermute | solution.py:339
  49.1 3.2 %collective-permute-done.17.near.refs_1_ = bf16[8,128,128]{2,1,0:T(8,128)(2,1)S(1)} collective-permute-done((bf16[8,128,128]{2,1,0:T(8,128)(2,1)S(1)}, bf16[8,128,128]{2,1,0:T(8,128)(2,1)S(1)}, u32[]{:S(2)}, u32[]{:S(2)}) %collective-permute-start.17) | collective-permute-done | bytes 262176 | tf_op jit(solution)/shard_map/ppermute | solution.py:337
  52.4 3.0 %collective-permute-done.14.refs_3_ = bf16[8,128,128]{2,1,0:T(8,128)(2,1)S(1)} collective-permute-done((bf16[8,128,128]{2,1,0:T(8,128)(2,1)S(1)}, bf16[8,128,128]{2,1,0:T(8,128)(2,1)S(1)}, u32[]{:S(2)}, u32[]{:S(2)}) %collective-permute-start.14) | collective-permute-done | bytes 262176 | tf_op jit(solution)/shard_map/ppermute | solution.py:339
  57.7 5.1 %collective-permute-done.18.refs_2_ = bf16[8,128,128]{2,1,0:T(8,128)(2,1)S(1)} collective-permute-done((bf16[8,128,128]{2,1,0:T(8,128)(2,1)S(1)}, bf16[8,128,128]{2,1,0:T(8,128)(2,1)S(1)}, u32[]{:S(2)}, u32[]{:S(2)}) %collective-permute-start.18) | collective-permute-done | bytes 262176 | tf_op jit(solution)/shard_map/ppermute | solution.py:341
  64.2 7.9 %collective-permute-done.21.near.refs_1_ = bf16[8,128,128]{2,1,0:T(8,128)(2,1)S(1)} collective-permute-done((bf16[8,128,128]{2,1,0:T(8,128)(2,1)S(1)}, bf16[8,128,128]{2,1,0:T(8,128)(2,1)S(1)}, u32[]{:S(2)}, u32[]{:S(2)}) %collective-permute-start.21) | collective-permute-done | bytes 262176 | tf_op jit(solution)/shard_map/ppermute | solution.py:337
  72.2 1.2 %correction.1 = f32[1,16,128,128]{3,2,1,0:T(8,128)} custom-call(bf16[1,16,128,128]{3,2,1,0:T(8,128)(2,1)S(1)} %copy-done, f32[8,128,128]{2,1,0:T(8,128)S(1)} %get-tuple-element.44.refs_4_.refs_0_, f32[8,128,128]{2,1,0:T(8,128)S(1)} %get-tuple-element.47.refs_4_.refs_1_, f32[8,128,128]{2,1,0:T(8,128)S(1)} %get-tuple-element.54.refs_4_.refs_2_, ...), custom_call_target="tpu_custom_call" | custom-call | bytes 3670016 | tf_op jit(solution)/shard_map/correction/pallas_call | solution.py:42
  73.4 1.0 %local_terms.7.refs_0_ = f32[16,128,128]{2,1,0:T(8,128)S(1)} custom-call(bf16[8,128,128]{2,1,0:T(8,128)(2,1)S(1)} %get-tuple-element.68.refs_0_.own, bf16[8,128,128]{2,1,0:T(8,128)(2,1)S(1)} %get-tuple-element.69.refs_1_.own, bf16[8,128,128]{2,1,0:T(8,128)(2,1)S(1)} %collective-permute-done.19.refs_2_, ...), custom_call_target="tpu_custom_call" | custom-call | flops 402653184 | bytes 5242880 | tf_op jit(solution)/shard_map/local_terms/pallas_call | solution.py:42
  74.4 1.2 %time_terms_last.2.refs_4_ = f32[1,16,128,128]{3,2,1,0:T(8,128)} custom-call(f32[16,128,128]{2,1,0:T(8,128)S(1)} %local_terms.7.refs_0_, bf16[8,128,128]{2,1,0:T(8,128)(2,1)S(1)} %collective-permute-done.23.near.refs_1_, bf16[8,128,128]{2,1,0:T(8,128)(2,1)S(1)} %collective-permute-done.24.refs_2_, bf16[16,128,256]{2,1,0:T(8,128)(2,1)S(1)} %prep_time.1.weight.refs_3_), custom_call_target="tpu_custom_call" | custom-call | flops 67108864 | bytes 2621440 | tf_op jit(solution)/shard_map/time_terms_last/pallas_call | solution.py:42
  75.5 4.8 %collective-permute-done.22.refs_2_ = bf16[8,128,128]{2,1,0:T(8,128)(2,1)S(1)} collective-permute-done((bf16[8,128,128]{2,1,0:T(8,128)(2,1)S(1)}, bf16[8,128,128]{2,1,0:T(8,128)(2,1)S(1)}, u32[]{:S(2)}, u32[]{:S(2)}) %collective-permute-start.22) | collective-permute-done | bytes 262176 | tf_op jit(solution)/shard_map/ppermute | solution.py:341
  80.3 1.1 %time_terms_last.3 = f32[1,16,128,128]{3,2,1,0:T(8,128)} custom-call(f32[16,128,128]{2,1,0:T(8,128)S(1)} %local_terms.7.refs_0_, bf16[8,128,128]{2,1,0:T(8,128)(2,1)S(1)} %collective-permute-done.21.near.refs_1_, bf16[8,128,128]{2,1,0:T(8,128)(2,1)S(1)} %collective-permute-done.22.refs_2_, ...), custom_call_target="tpu_custom_call", output_to_operand_aliasing={{}: (4, {})} | custom-call | flops 67108864 | bytes 3670016 | tf_op jit(solution)/shard_map/time_terms_last/pallas_call | solution.py:42
  (54 shorter events, 10.7 us)
Async XLA Ops:
  1.8 9.3 %collective-permute-start.3 = (bf16[16,2,64,128]{3,2,1,0:T(8,128)(2,1)S(1)}, bf16[16,2,64,128]{3,2,1,0:T(8,128)(2,1)S(1)}, u32[]{:S(2)}, u32[]{:S(2)}) collective-permute-start(bf16[16,2,64,128]{3,2,1,0:T(8,128)(2,1)S(1)} %time_blocks.1), channel_id=1, source_target_pairs={{0,0},{1,1},{2,2},{3,3},{4,4},{5,5},{6,6},{7,7},{8,9},{9,8},{10,11... | collective-permute-start | bytes 1572872 | tf_op jit(solution)/shard_map/ppermute | solution.py:327
  2.5 10.0 %collective-permute-start.2 = (bf16[8,128,128]{2,1,0:T(8,128)(2,1)S(1)}, bf16[8,128,128]{2,1,0:T(8,128)(2,1)S(1)}, u32[]{:S(2)}, u32[]{:S(2)}) collective-permute-start(bf16[8,128,128]{2,1,0:T(8,128)(2,1)S(1)} %get-tuple-element.38.refs_0_.own), channel_id=1, source_target_pairs={{0,1},{1,0},{2,3},{3,2},{4,5},{5,4},{6,7},{7,6},{8,14},{9,11},{10,... | collective-permute-start | bytes 786440 | tf_op jit(solution)/shard_map/ppermute | solution.py:337
  5.6 12.5 %collective-permute-start.5 = (bf16[8,128,128]{2,1,0:T(8,128)(2,1)S(1)}, bf16[8,128,128]{2,1,0:T(8,128)(2,1)S(1)}, u32[]{:S(2)}, u32[]{:S(2)}) collective-permute-start(bf16[8,128,128]{2,1,0:T(8,128)(2,1)S(1)} %get-tuple-element.41.refs_1_.own), channel_id=1, source_target_pairs={{0,1},{1,0},{2,3},{3,2},{4,5},{5,4},{6,7},{7,6},{8,14},{9,11},{10,... | collective-permute-start | bytes 786440 | tf_op jit(solution)/shard_map/ppermute | solution.py:337
  5.7 16.9 %collective-permute-start = (bf16[8,128,128]{2,1,0:T(8,128)(2,1)S(1)}, bf16[8,128,128]{2,1,0:T(8,128)(2,1)S(1)}, u32[]{:S(2)}, u32[]{:S(2)}) collective-permute-start(bf16[8,128,128]{2,1,0:T(8,128)(2,1)S(1)} %get-tuple-element.42), channel_id=1, source_target_pairs={{0,8},{8,0},{16,24},{24,16},{1,9},{9,1},{17,25},{25,17},{2,10},{10... | collective-permute-start | bytes 786440 | tf_op jit(solution)/shard_map/ppermute | solution.py:338
  9.9 12.7 %collective-permute-start.1 = (bf16[8,128,128]{2,1,0:T(8,128)(2,1)S(1)}, bf16[8,128,128]{2,1,0:T(8,128)(2,1)S(1)}, u32[]{:S(2)}, u32[]{:S(2)}) collective-permute-start(bf16[8,128,128]{2,1,0:T(8,128)(2,1)S(1)} %get-tuple-element.43), channel_id=1, source_target_pairs={{0,24},{8,16},{16,8},{24,0},{1,25},{9,17},{17,9},{25,1},{2,26},{10... | collective-permute-start | bytes 786440 | tf_op jit(solution)/shard_map/ppermute | solution.py:339
  12.5 11.1 %collective-permute-start.4 = (bf16[8,128,128]{2,1,0:T(8,128)(2,1)S(1)}, bf16[8,128,128]{2,1,0:T(8,128)(2,1)S(1)}, u32[]{:S(2)}, u32[]{:S(2)}) collective-permute-start(bf16[8,128,128]{2,1,0:T(8,128)(2,1)S(1)} %second_message.8), channel_id=1, source_target_pairs={{0,2},{1,7},{2,4},{3,1},{4,6},{5,3},{6,0},{7,5},{8,9},{9,8},{10,11... | collective-permute-start | bytes 786440 | tf_op jit(solution)/shard_map/ppermute | solution.py:341
  18.2 9.4 %collective-permute-start.6 = (bf16[8,128,128]{2,1,0:T(8,128)(2,1)S(1)}, bf16[8,128,128]{2,1,0:T(8,128)(2,1)S(1)}, u32[]{:S(2)}, u32[]{:S(2)}) collective-permute-start(bf16[8,128,128]{2,1,0:T(8,128)(2,1)S(1)} %second_message.9), channel_id=1, source_target_pairs={{0,2},{1,7},{2,4},{3,1},{4,6},{5,3},{6,0},{7,5},{8,9},{9,8},{10,11... | collective-permute-start | bytes 786440 | tf_op jit(solution)/shard_map/ppermute | solution.py:341
  24.0 9.8 %collective-permute-start.9 = (bf16[8,128,128]{2,1,0:T(8,128)(2,1)S(1)}, bf16[8,128,128]{2,1,0:T(8,128)(2,1)S(1)}, u32[]{:S(2)}, u32[]{:S(2)}) collective-permute-start(bf16[8,128,128]{2,1,0:T(8,128)(2,1)S(1)} %get-tuple-element.48.refs_0_.own), channel_id=1, source_target_pairs={{0,1},{1,0},{2,3},{3,2},{4,5},{5,4},{6,7},{7,6},{8,14},{9,11},{10,... | collective-permute-start | bytes 786440 | tf_op jit(solution)/shard_map/ppermute | solution.py:337
  27.9 6.8 %collective-permute-start.11 = (bf16[8,128,128]{2,1,0:T(8,128)(2,1)S(1)}, bf16[8,128,128]{2,1,0:T(8,128)(2,1)S(1)}, u32[]{:S(2)}, u32[]{:S(2)}) collective-permute-start(bf16[8,128,128]{2,1,0:T(8,128)(2,1)S(1)} %get-tuple-element.49.refs_1_.own), channel_id=1, source_target_pairs={{0,1},{1,0},{2,3},{3,2},{4,5},{5,4},{6,7},{7,6},{8,14},{9,11},{10,... | collective-permute-start | bytes 786440 | tf_op jit(solution)/shard_map/ppermute | solution.py:337
  28.2 6.7 %collective-permute-start.7 = (bf16[8,128,128]{2,1,0:T(8,128)(2,1)S(1)}, bf16[8,128,128]{2,1,0:T(8,128)(2,1)S(1)}, u32[]{:S(2)}, u32[]{:S(2)}) collective-permute-start(bf16[8,128,128]{2,1,0:T(8,128)(2,1)S(1)} %get-tuple-element.50), channel_id=1, source_target_pairs={{0,8},{8,0},{16,24},{24,16},{1,9},{9,1},{17,25},{25,17},{2,10},{10... | collective-permute-start | bytes 786440 | tf_op jit(solution)/shard_map/ppermute | solution.py:338
  32.9 8.4 %collective-permute-start.8 = (bf16[8,128,128]{2,1,0:T(8,128)(2,1)S(1)}, bf16[8,128,128]{2,1,0:T(8,128)(2,1)S(1)}, u32[]{:S(2)}, u32[]{:S(2)}) collective-permute-start(bf16[8,128,128]{2,1,0:T(8,128)(2,1)S(1)} %get-tuple-element.51), channel_id=1, source_target_pairs={{0,24},{8,16},{16,8},{24,0},{1,25},{9,17},{17,9},{25,1},{2,26},{10... | collective-permute-start | bytes 786440 | tf_op jit(solution)/shard_map/ppermute | solution.py:339
  33.8 8.5 %collective-permute-start.10 = (bf16[8,128,128]{2,1,0:T(8,128)(2,1)S(1)}, bf16[8,128,128]{2,1,0:T(8,128)(2,1)S(1)}, u32[]{:S(2)}, u32[]{:S(2)}) collective-permute-start(bf16[8,128,128]{2,1,0:T(8,128)(2,1)S(1)} %second_message.10), channel_id=1, source_target_pairs={{0,2},{1,7},{2,4},{3,1},{4,6},{5,3},{6,0},{7,5},{8,9},{9,8},{10,11... | collective-permute-start | bytes 786440 | tf_op jit(solution)/shard_map/ppermute | solution.py:341
  34.8 10.8 %collective-permute-start.12 = (bf16[8,128,128]{2,1,0:T(8,128)(2,1)S(1)}, bf16[8,128,128]{2,1,0:T(8,128)(2,1)S(1)}, u32[]{:S(2)}, u32[]{:S(2)}) collective-permute-start(bf16[8,128,128]{2,1,0:T(8,128)(2,1)S(1)} %second_message.11), channel_id=1, source_target_pairs={{0,2},{1,7},{2,4},{3,1},{4,6},{5,3},{6,0},{7,5},{8,9},{9,8},{10,11... | collective-permute-start | bytes 786440 | tf_op jit(solution)/shard_map/ppermute | solution.py:341
  42.6 6.4 %collective-permute-start.15 = (bf16[8,128,128]{2,1,0:T(8,128)(2,1)S(1)}, bf16[8,128,128]{2,1,0:T(8,128)(2,1)S(1)}, u32[]{:S(2)}, u32[]{:S(2)}) collective-permute-start(bf16[8,128,128]{2,1,0:T(8,128)(2,1)S(1)} %get-tuple-element.58.refs_0_.own), channel_id=1, source_target_pairs={{0,1},{1,0},{2,3},{3,2},{4,5},{5,4},{6,7},{7,6},{8,14},{9,11},{10,... | collective-permute-start | bytes 786440 | tf_op jit(solution)/shard_map/ppermute | solution.py:337
  45.9 6.4 %collective-permute-start.17 = (bf16[8,128,128]{2,1,0:T(8,128)(2,1)S(1)}, bf16[8,128,128]{2,1,0:T(8,128)(2,1)S(1)}, u32[]{:S(2)}, u32[]{:S(2)}) collective-permute-start(bf16[8,128,128]{2,1,0:T(8,128)(2,1)S(1)} %get-tuple-element.59.refs_1_.own), channel_id=1, source_target_pairs={{0,1},{1,0},{2,3},{3,2},{4,5},{5,4},{6,7},{7,6},{8,14},{9,11},{10,... | collective-permute-start | bytes 786440 | tf_op jit(solution)/shard_map/ppermute | solution.py:337
  46.0 6.5 %collective-permute-start.13 = (bf16[8,128,128]{2,1,0:T(8,128)(2,1)S(1)}, bf16[8,128,128]{2,1,0:T(8,128)(2,1)S(1)}, u32[]{:S(2)}, u32[]{:S(2)}) collective-permute-start(bf16[8,128,128]{2,1,0:T(8,128)(2,1)S(1)} %get-tuple-element.60), channel_id=1, source_target_pairs={{0,8},{8,0},{16,24},{24,16},{1,9},{9,1},{17,25},{25,17},{2,10},{10... | collective-permute-start | bytes 786440 | tf_op jit(solution)/shard_map/ppermute | solution.py:338
  46.7 8.7 %collective-permute-start.14 = (bf16[8,128,128]{2,1,0:T(8,128)(2,1)S(1)}, bf16[8,128,128]{2,1,0:T(8,128)(2,1)S(1)}, u32[]{:S(2)}, u32[]{:S(2)}) collective-permute-start(bf16[8,128,128]{2,1,0:T(8,128)(2,1)S(1)} %get-tuple-element.61), channel_id=1, source_target_pairs={{0,24},{8,16},{16,8},{24,0},{1,25},{9,17},{17,9},{25,1},{2,26},{10... | collective-permute-start | bytes 786440 | tf_op jit(solution)/shard_map/ppermute | solution.py:339
  49.1 8.2 %collective-permute-start.16 = (bf16[8,128,128]{2,1,0:T(8,128)(2,1)S(1)}, bf16[8,128,128]{2,1,0:T(8,128)(2,1)S(1)}, u32[]{:S(2)}, u32[]{:S(2)}) collective-permute-start(bf16[8,128,128]{2,1,0:T(8,128)(2,1)S(1)} %second_message.12), channel_id=1, source_target_pairs={{0,2},{1,7},{2,4},{3,1},{4,6},{5,3},{6,0},{7,5},{8,9},{9,8},{10,11... | collective-permute-start | bytes 786440 | tf_op jit(solution)/shard_map/ppermute | solution.py:341
  52.4 10.5 %collective-permute-start.18 = (bf16[8,128,128]{2,1,0:T(8,128)(2,1)S(1)}, bf16[8,128,128]{2,1,0:T(8,128)(2,1)S(1)}, u32[]{:S(2)}, u32[]{:S(2)}) collective-permute-start(bf16[8,128,128]{2,1,0:T(8,128)(2,1)S(1)} %second_message.13), channel_id=1, source_target_pairs={{0,2},{1,7},{2,4},{3,1},{4,6},{5,3},{6,0},{7,5},{8,9},{9,8},{10,11... | collective-permute-start | bytes 786440 | tf_op jit(solution)/shard_map/ppermute | solution.py:341
  63.2 8.9 %collective-permute-start.21 = (bf16[8,128,128]{2,1,0:T(8,128)(2,1)S(1)}, bf16[8,128,128]{2,1,0:T(8,128)(2,1)S(1)}, u32[]{:S(2)}, u32[]{:S(2)}) collective-permute-start(bf16[8,128,128]{2,1,0:T(8,128)(2,1)S(1)} %get-tuple-element.69.refs_1_.own), channel_id=1, source_target_pairs={{0,1},{1,0},{2,3},{3,2},{4,5},{5,4},{6,7},{7,6},{8,14},{9,11},{10,... | collective-permute-start | bytes 786440 | tf_op jit(solution)/shard_map/ppermute | solution.py:337
  63.2 10.1 %collective-permute-start.19 = (bf16[8,128,128]{2,1,0:T(8,128)(2,1)S(1)}, bf16[8,128,128]{2,1,0:T(8,128)(2,1)S(1)}, u32[]{:S(2)}, u32[]{:S(2)}) collective-permute-start(bf16[8,128,128]{2,1,0:T(8,128)(2,1)S(1)} %get-tuple-element.70), channel_id=1, source_target_pairs={{0,8},{8,0},{16,24},{24,16},{1,9},{9,1},{17,25},{25,17},{2,10},{10... | collective-permute-start | bytes 786440 | tf_op jit(solution)/shard_map/ppermute | solution.py:338
  63.3 10.0 %collective-permute-start.20 = (bf16[8,128,128]{2,1,0:T(8,128)(2,1)S(1)}, bf16[8,128,128]{2,1,0:T(8,128)(2,1)S(1)}, u32[]{:S(2)}, u32[]{:S(2)}) collective-permute-start(bf16[8,128,128]{2,1,0:T(8,128)(2,1)S(1)} %get-tuple-element.71), channel_id=1, source_target_pairs={{0,24},{8,16},{16,8},{24,0},{1,25},{9,17},{17,9},{25,1},{2,26},{10... | collective-permute-start | bytes 786440 | tf_op jit(solution)/shard_map/ppermute | solution.py:339
  64.1 10.2 %collective-permute-start.24 = (bf16[8,128,128]{2,1,0:T(8,128)(2,1)S(1)}, bf16[8,128,128]{2,1,0:T(8,128)(2,1)S(1)}, u32[]{:S(2)}, u32[]{:S(2)}) collective-permute-start(bf16[8,128,128]{2,1,0:T(8,128)(2,1)S(1)} %second_message.15), channel_id=1, source_target_pairs={{0,2},{1,7},{2,4},{3,1},{4,6},{5,3},{6,0},{7,5},{8,9},{9,8},{10,11... | collective-permute-start | bytes 786440 | tf_op jit(solution)/shard_map/ppermute | solution.py:341
  72.1 8.2 %collective-permute-start.22 = (bf16[8,128,128]{2,1,0:T(8,128)(2,1)S(1)}, bf16[8,128,128]{2,1,0:T(8,128)(2,1)S(1)}, u32[]{:S(2)}, u32[]{:S(2)}) collective-permute-start(bf16[8,128,128]{2,1,0:T(8,128)(2,1)S(1)} %second_message.14), channel_id=1, source_target_pairs={{0,2},{1,7},{2,4},{3,1},{4,6},{5,3},{6,0},{7,5},{8,9},{9,8},{10,11... | collective-permute-start | bytes 786440 | tf_op jit(solution)/shard_map/ppermute | solution.py:341
  (2 other events, 8.3 us)

commit v3 on v0

v3 whole, which is shorter than its diff:
```python
import functools

import jax
import jax.numpy as jnp
from jax import lax
from jax.experimental import pallas as pl
from jax.experimental.pallas import tpu as pltpu
from jax.sharding import PartitionSpec as P

LY = 4
LZ = 2
STEPS = 4
PLANE = LY * LZ

diagonal_shift = 1.5
center_value = 1.5
half_width = 1.0

F32, BF16 = jnp.float32, jnp.bfloat16
WHOLE = pl.BlockSpec(memory_space=pltpu.VMEM)
IN_HBM = pl.BlockSpec(memory_space=pltpu.HBM)
VMEM_LIMIT = 32 * 1024 * 1024


def coefficients():
    ratio = half_width / center_value
    out = []
    for _ in range(STEPS - 1):
        ratio_next = 1.0 / (2.0 * center_value / half_width - ratio)
        out.append((ratio_next * ratio, 2.0 * ratio_next / half_width))
        ratio = ratio_next
    return out


def call(kernel, outs, operands, flops, name, aliases=None, out_specs=None, in_specs=None, scratch=()):
    nbytes = sum(o.size * o.dtype.itemsize for o in operands)
    in_specs = in_specs or [WHOLE] * len(operands)
    out_specs = out_specs or [WHOLE] * len(outs)
    operands = [
        pltpu.with_memory_space_constraint(o, pltpu.VMEM if s is WHOLE else pltpu.HBM)
        for o, s in zip(operands, in_specs)
    ]
    return pl.pallas_call(
        kernel,
        out_shape=outs,
        in_specs=in_specs,
        out_specs=out_specs,
        input_output_aliases=aliases or {},
        scratch_shapes=scratch,
        compiler_params=pltpu.CompilerParams(vmem_limit_bytes=VMEM_LIMIT),
        cost_estimate=pl.CostEstimate(flops=flops, bytes_accessed=nbytes, transcendentals=0),
        name=name,
    )(*operands)


def odd_group():
    return lax.axis_index("group") % 2


def plane_of(piece):
    return (piece + odd_group()) % 2


def plane_sites(piece):
    return pl.ds(pl.multiple_of(plane_of(piece) * PLANE, PLANE), PLANE)


def real_form(block):
    block = block.astype(F32)
    half = block.shape[-1] // 2
    lane = lax.broadcasted_iota(jnp.int32, block.shape, 1)
    upper = jnp.where(lane < half, block, -block)
    lower = pltpu.roll(block, half, 1)
    return jnp.concatenate([upper, lower], axis=0)


def prep_kernel(batch, self_hbm, hop_hbm, *refs):
    local_refs, time_refs, (self_ref, hop_ref, sems) = refs[:2], refs[2:4], refs[4:]
    sites = hop_ref.shape[0]
    width = local_refs[0].shape[1]
    parity = lax.axis_index("site") % 2
    copies = []
    for i in range(sites // batch):
        piece, offset = divmod(i * batch, PLANE)
        base = lax.axis_index("group") * sites + plane_of(piece) * PLANE + offset
        there, here = pl.ds(pl.multiple_of(base, batch), batch), pl.ds(i * batch, batch)
        copies.append(
            (
                pltpu.make_async_copy(hop_hbm.at[0, there], hop_ref.at[here], sems.at[0, i]),
                pltpu.make_async_copy(self_hbm.at[0, there], self_ref.at[here], sems.at[1, i]),
            )
        )
        for copy in copies[i]:
            copy.start()
    for site in range(sites):
        if site % batch == 0:
            for copy in copies[site // batch]:
                copy.wait()
        piece, own = divmod(site, PLANE)
        plane = plane_of(piece)
        hop = lambda m: real_form(hop_ref[site, m])
        parts = [
            real_form(self_ref[site]),
            hop(plane),
            hop(2),
            hop(3),
            hop(4) + hop(5),
            hop(1 - plane),
        ]
        for k, part in enumerate(parts):
            local_refs[piece][own, :, k * width : (k + 1) * width] = part.astype(BF16)
        time_refs[piece][own, :, :width] = hop(6 + parity).astype(BF16)
        time_refs[piece][own, :, width:] = hop(7 - parity).astype(BF16)


def prep(self_block, hop_blocks, sites):
    comps, width = self_block.shape[2:]
    batch = 2
    weight = lambda parts: pltpu.VMEM((PLANE, width, parts * width), BF16)
    outs = call(
        functools.partial(prep_kernel, batch),
        [weight(6)] * 2 + [weight(2)] * 2,
        [self_block, hop_blocks],
        0,
        "prep",
        in_specs=[IN_HBM, IN_HBM],
        scratch=[
            pltpu.VMEM((sites, comps, width), BF16),
            pltpu.VMEM((sites, 8, comps, width), BF16),
            pltpu.SemaphoreType.DMA((2, sites // batch)),
        ],
    )
    return outs[:2], outs[2:4]


def times(vector, weight):
    return lax.dot_general(
        vector, weight, (((1,), (1,)), ((), ())), preferred_element_type=F32
    )


def first_kernel(piece, residual_hbm, *refs):
    residual, sent_out, sems = refs[-3:]
    base = plane_of(piece) * PLANE
    copies = [
        pltpu.make_async_copy(residual_hbm.at[0, base + s], residual.at[s], sems.at[s])
        for s in range(PLANE)
    ]
    for copy in copies:
        copy.start()
    for s in range(PLANE):
        copies[s].wait()
        sent_out[s] = (residual[s].astype(F32) * (half_width / center_value)).astype(BF16)


def local_kernel(this, that, halo, weight, residual, acc):
    for s in range(PLANE):
        y, z = s // LZ, s % LZ
        own = this[s]
        around = jnp.concatenate(
            [
                own,
                that[s],
                this[(y + 1) % LY * LZ + z],
                this[(y - 1) % LY * LZ + z],
                this[y * LZ + 1 - z],
                halo[s],
            ],
            axis=1,
        )
        acc[s] = (
            residual[s].astype(F32) - diagonal_shift * own.astype(F32) - times(around, weight[s])
        )


def time_kernel(piece, mode, scale, *refs):
    acc, near, far, weight = refs[:4]
    if mode == "last":
        whole, out, sems = refs[-3:]
        base = plane_of(piece) * PLANE
        copies = [
            pltpu.make_async_copy(out.at[s], whole.at[0, base + s], sems.at[s]) for s in range(PLANE)
        ]
    else:
        direction = refs[4]
        out, direction_out, sent_out = refs[-3:]

    for s in range(PLANE):
        around = jnp.concatenate([near[s], far[s]], axis=1)
        now = acc[s] - times(around, weight[s])
        out[s] = now
        if mode == "last":
            copies[s].start()
            continue
        old = direction[s].astype(F32)
        if mode == "first":
            old = old * (half_width / center_value)
        new = scale[0] * old + scale[1] * now
        direction_out[s] = new
        sent_out[s] = new.astype(BF16)
    if mode == "last":
        for copy in copies:
            copy.wait()


def sum_kernel(residual_a, residual_b, *refs):
    out = refs[-1]
    for piece, residual in enumerate((residual_a, residual_b)):
        total = residual[...].astype(F32) * (half_width / center_value)
        for ref in refs[piece:-1:2]:
            total = total + ref[...]
        out[0, plane_sites(piece)] = total


def body(residual_in, self_block, hop_blocks):
    _, sites, count, width = residual_in.shape
    groups, slices = lax.axis_size("group"), lax.axis_size("site")
    assert sites == 2 * PLANE and slices % 2 == 0 and groups % 2 == 0
    swap = [(t, t ^ 1) for t in range(slices)]
    relay = [(t, (t + 2 - 4 * (t % 2)) % slices) for t in range(slices)]
    cores = [(i, i ^ 1) for i in range(groups)]
    chips = [(i, (i - 1 + 2 * (i % 2)) % groups) for i in range(groups)]

    block = (count, width)
    piece = lambda kind: pltpu.VMEM((PLANE,) + block, kind)
    whole = jax.ShapeDtypeStruct((1, sites) + block, F32)
    flops = 2 * PLANE * count * width * width
    scales = coefficients()

    weight_local, weight_time = prep(self_block, hop_blocks, sites)
    start, sent = zip(
        *[
            call(
                functools.partial(first_kernel, i),
                [piece(BF16), piece(BF16)],
                [residual_in] + [weight_local[0]] * i,
                0,
                "first_direction",
                in_specs=[IN_HBM] + [WHOLE] * i,
                scratch=[pltpu.SemaphoreType.DMA((PLANE,))],
            )
            for i in range(2)
        ]
    )
    residual, direction = start, start
    directions = []
    for number in range(STEPS):
        first, last = number == 0, number == STEPS - 1
        near = [lax.ppermute(v, "site", swap) for v in sent]
        halo = [lax.ppermute(sent[0], "group", chips), lax.ppermute(sent[1], "group", cores)]
        far = [lax.ppermute(v, "site", relay) for v in near]
        acc = [
            call(
                local_kernel,
                [piece(F32)],
                [sent[i], sent[1 - i], halo[i], weight_local[i], residual[i]],
                6 * flops,
                "local_terms",
            )[0]
            for i in range(2)
        ]
        operands = lambda i: [acc[i], near[i], far[i], weight_time[i]]
        if last:
            correction = call(sum_kernel, [whole], [*start, *sum(directions, ())], 0, "correction")[0]
            result = []
            for i in range(2):
                result = call(
                    functools.partial(time_kernel, i, "last", None),
                    [whole],
                    [*operands(i), *result],
                    2 * flops,
                    "time_terms_last",
                    aliases={4: 0} if result else None,
                    in_specs=[WHOLE] * 4 + [IN_HBM] * len(result),
                    out_specs=[IN_HBM],
                    scratch=[piece(F32), pltpu.SemaphoreType.DMA((PLANE,))],
                )
            return correction, result[0]
        mode = "first" if first else "middle"
        residual, direction, sent = zip(
            *[
                call(
                    functools.partial(time_kernel, i, mode, scales[number]),
                    [piece(F32), piece(F32), piece(BF16)],
                    [*operands(i), direction[i]],
                    2 * flops,
                    "time_terms",
                )
                for i in range(2)
            ]
        )
        directions.append(direction)


def solution(mesh):
    return jax.shard_map(
        body,
        mesh=mesh,
        in_specs=(
            P("site", "group", None, None),
            P("site", None, None, None),
            P("site", None, None, None, None),
        ),
        out_specs=(P("site", "group", None, None), P("site", "group", None, None)),
        check_vma=False,
    )
```

time: 231 us -> 81.2 us (0.35)
  matrix products: 56 us -> 0 us
  waiting for transfers between devices: 83.4 us -> 47.6 us
  other arithmetic: 31.2 us -> 0 us
  blocking collectives: 24.6 us -> 0 us
  local copies, waits for them, and re-layouts: 16 us -> 0 us
  Pallas kernels: 0 us -> 13.9 us
    dot_general x8 -> x0, matrix products: 56 us -> none  [the longest x4 50.4 us: apply_blocks(): jnp.einsum('tsmab,tsmkb->tska', own_hops, paired(around), preferred_eleme...]
    ppermute x8 -> x24, waiting for transfers between devices: 75.8 us -> 47.6 us  [the longest x8 25.1 us: body(): far = [lax.ppermute(v, 'site', relay) for v in near]]
    all_to_all x2 -> x0, blocking collectives: 24.6 us -> none  [the longest x1 12.9 us: body(): lax.all_to_all(residual_in, 'group', split_axis=2, concat_axis=1, tiled=T...]
    neg x8 -> x0, other arithmetic: 21.4 us -> none  [paired(): conjugate = jnp.concatenate([real_part, -imag_part], axis=-1)]
    pallas_call x0 -> x20, Pallas kernels: none -> 13.9 us  [call(): pl.pallas_call(kernel, out_shape=outs, in_specs=in_specs, out_specs=out_s...]
    slice x24 -> x0, local copies, waits for them, and re-layouts: 8.79 us -> none  [the longest x4 7.04 us: apply_blocks(): mixed = jnp.concatenate([total[:, :, :count], total[:, :, count:]], axis=-1)]
    convert_element_type x11 -> x0, other arithmetic: 8.78 us -> none  [the longest x8 6.75 us: body(): sent = direction.astype(jnp.bfloat16)]
    all_to_all x1 -> x0, waiting for transfers between devices: 7.61 us -> none  [body(): lax.all_to_all(residual.astype(jnp.bfloat16), 'group', split_axis=1, conc...]
  transfers between devices with their start and end apart: 9 -> 24, of which waited for: 5 -> 18; matrix products, arithmetic and copies ran while one was open for 5% -> 0% of each run, Pallas kernels for 0% -> 15%
where the time goes in v3:
time: 81.2 us; the launch traced here: 80.9 us
  waiting for transfers between devices  47.6 us (59%)
  starting transfers between devices  18.6 us (23%)
  Pallas kernels  13.9 us (17%)
  between operations  0.83 us (1%)
    ppermute x8, waiting for transfers between devices, body(): far = [lax.ppermute(v, 'site', relay) for v in near]  25.1 us
    ppermute x8, waiting for transfers between devices, body(): near = [lax.ppermute(v, 'site', swap) for v in sent]  21.5 us
    pallas_call x20, Pallas kernels, call(): pl.pallas_call(kernel, out_shape=outs, in_specs=in_specs, out_specs=out_s...  13.9 us
    ppermute x8, starting transfers between devices, body(): near = [lax.ppermute(v, 'site', swap) for v in sent]  8.42 us
    ppermute x8, starting transfers between devices, body(): far = [lax.ppermute(v, 'site', relay) for v in near]  4.14 us
    ppermute x4, starting transfers between devices, body(): lax.ppermute(sent[0], 'group', chips)  3.1 us
    ppermute x4, starting transfers between devices, body(): lax.ppermute(sent[1], 'group', cores)  2.91 us
  transfers between devices with their start and end apart: 24, of which 18 were waited for; matrix products, arithmetic and copies ran while one was open for 0% of the time, Pallas kernels for 15%

profile of v3, /device:TPU:0, one launch (start us, length us, event | category | flops | bytes accessed | tf_op | source)
XLA Modules:
  0.0 80.9 jit_solution(8148364828131357760)
XLA Ops:
  1.6 3.0 %collective-permute-start.1 = (bf16[8,128,128]{2,1,0:T(8,128)(2,1)S(1)}, bf16[8,128,128]{2,1,0:T(8,128)(2,1)S(1)}, u32[]{:S(2)}, u32[]{:S(2)}) collective-permute-start(bf16[8,128,128]{2,1,0:T(8,128)(2,1)S(1)} %get-tuple-element.31.this.that), channel_id=1, source_target_pairs={{0,1},{1,0},{2,3},{3,2},{4,5},{5,4},{6,7},{7,6},{8,9},{9,8},{10,11... | collective-permute-start | bytes 786440 | tf_op jit(solution)/shard_map/ppermute | solution.py:249
  4.6 2.4 %prep.1 = (bf16[8,128,768]{2,1,0:T(8,128)(2,1)S(1)}, bf16[8,128,768]{2,1,0:T(8,128)(2,1)S(1)}, bf16[8,128,256]{2,1,0:T(8,128)(2,1)S(1)}, bf16[8,128,256]{2,1,0:T(8,128)(2,1)S(1)}) custom-call(bf16[1,64,64,128]{3,2,1,0:T(8,128)(2,1)} %self_hbm.1, bf16[1,64,8,64,128]{4,3,2,1,0:T(8,128)(2,1)} %hop_hbm.1), custom_call_target="tpu_custom_call" | custom-call | bytes 9437184 | tf_op jit(solution)/shard_map/prep/pallas_call | solution.py:43
  9.0 1.2 %collective-permute-start.3 = (bf16[8,128,128]{2,1,0:T(8,128)(2,1)S(1)}, bf16[8,128,128]{2,1,0:T(8,128)(2,1)S(1)}, u32[]{:S(2)}, u32[]{:S(2)}) collective-permute-start(bf16[8,128,128]{2,1,0:T(8,128)(2,1)S(1)} %get-tuple-element.32.that.this), channel_id=1, source_target_pairs={{0,8},{8,0},{16,24},{24,16},{1,9},{9,1},{17,25},{25,17},{2,10},{10... | collective-permute-start | bytes 786440 | tf_op jit(solution)/shard_map/ppermute | solution.py:250
  10.2 1.4 %collective-permute-done.1.refs_1_ = bf16[8,128,128]{2,1,0:T(8,128)(2,1)S(1)} collective-permute-done((bf16[8,128,128]{2,1,0:T(8,128)(2,1)S(1)}, bf16[8,128,128]{2,1,0:T(8,128)(2,1)S(1)}, u32[]{:S(2)}, u32[]{:S(2)}) %collective-permute-start.1) | collective-permute-done | bytes 262176 | tf_op jit(solution)/shard_map/ppermute | solution.py:249
  11.6 2.0 %collective-permute-start.2 = (bf16[8,128,128]{2,1,0:T(8,128)(2,1)S(1)}, bf16[8,128,128]{2,1,0:T(8,128)(2,1)S(1)}, u32[]{:S(2)}, u32[]{:S(2)}) collective-permute-start(bf16[8,128,128]{2,1,0:T(8,128)(2,1)S(1)} %collective-permute-done.1.refs_1_), channel_id=1, source_target_pairs={{0,2},{1,7},{2,4},{3,1},{4,6},{5,3},{6,0},{7,5},{8,10},{9,15},{10,... | collective-permute-start | bytes 786440 | tf_op jit(solution)/shard_map/ppermute | solution.py:251
  13.6 3.0 %collective-permute-done.4.refs_1_ = bf16[8,128,128]{2,1,0:T(8,128)(2,1)S(1)} collective-permute-done((bf16[8,128,128]{2,1,0:T(8,128)(2,1)S(1)}, bf16[8,128,128]{2,1,0:T(8,128)(2,1)S(1)}, u32[]{:S(2)}, u32[]{:S(2)}) %collective-permute-start.4) | collective-permute-done | bytes 262176 | tf_op jit(solution)/shard_map/ppermute | solution.py:249
  16.6 1.8 %collective-permute-start.5 = (bf16[8,128,128]{2,1,0:T(8,128)(2,1)S(1)}, bf16[8,128,128]{2,1,0:T(8,128)(2,1)S(1)}, u32[]{:S(2)}, u32[]{:S(2)}) collective-permute-start(bf16[8,128,128]{2,1,0:T(8,128)(2,1)S(1)} %collective-permute-done.4.refs_1_), channel_id=1, source_target_pairs={{0,2},{1,7},{2,4},{3,1},{4,6},{5,3},{6,0},{7,5},{8,10},{9,15},{10,... | collective-permute-start | bytes 786440 | tf_op jit(solution)/shard_map/ppermute | solution.py:251
  20.6 2.9 %collective-permute-start.7 = (bf16[8,128,128]{2,1,0:T(8,128)(2,1)S(1)}, bf16[8,128,128]{2,1,0:T(8,128)(2,1)S(1)}, u32[]{:S(2)}, u32[]{:S(2)}) collective-permute-start(bf16[8,128,128]{2,1,0:T(8,128)(2,1)S(1)} %get-tuple-element.38.this.that), channel_id=1, source_target_pairs={{0,1},{1,0},{2,3},{3,2},{4,5},{5,4},{6,7},{7,6},{8,9},{9,8},{10,11... | collective-permute-start | bytes 786440 | tf_op jit(solution)/shard_map/ppermute | solution.py:249
  23.5 2.6 %collective-permute-done.5.refs_2_ = bf16[8,128,128]{2,1,0:T(8,128)(2,1)S(1)} collective-permute-done((bf16[8,128,128]{2,1,0:T(8,128)(2,1)S(1)}, bf16[8,128,128]{2,1,0:T(8,128)(2,1)S(1)}, u32[]{:S(2)}, u32[]{:S(2)}) %collective-permute-start.5) | collective-permute-done | bytes 262176 | tf_op jit(solution)/shard_map/ppermute | solution.py:251
  27.3 1.6 %collective-permute-start.6 = (bf16[8,128,128]{2,1,0:T(8,128)(2,1)S(1)}, bf16[8,128,128]{2,1,0:T(8,128)(2,1)S(1)}, u32[]{:S(2)}, u32[]{:S(2)}) collective-permute-start(bf16[8,128,128]{2,1,0:T(8,128)(2,1)S(1)} %get-tuple-element.38.this.that), channel_id=1, source_target_pairs={{0,24},{8,16},{16,8},{24,0},{1,25},{9,17},{17,9},{25,1},{2,26},{10... | collective-permute-start | bytes 786440 | tf_op jit(solution)/shard_map/ppermute | solution.py:250
  30.2 4.1 %collective-permute-done.10.refs_1_ = bf16[8,128,128]{2,1,0:T(8,128)(2,1)S(1)} collective-permute-done((bf16[8,128,128]{2,1,0:T(8,128)(2,1)S(1)}, bf16[8,128,128]{2,1,0:T(8,128)(2,1)S(1)}, u32[]{:S(2)}, u32[]{:S(2)}) %collective-permute-start.10) | collective-permute-done | bytes 262176 | tf_op jit(solution)/shard_map/ppermute | solution.py:249
  35.9 5.0 %collective-permute-done.8.refs_2_ = bf16[8,128,128]{2,1,0:T(8,128)(2,1)S(1)} collective-permute-done((bf16[8,128,128]{2,1,0:T(8,128)(2,1)S(1)}, bf16[8,128,128]{2,1,0:T(8,128)(2,1)S(1)}, u32[]{:S(2)}, u32[]{:S(2)}) %collective-permute-start.8) | collective-permute-done | bytes 262176 | tf_op jit(solution)/shard_map/ppermute | solution.py:251
  41.3 4.0 %collective-permute-done.11.refs_2_ = bf16[8,128,128]{2,1,0:T(8,128)(2,1)S(1)} collective-permute-done((bf16[8,128,128]{2,1,0:T(8,128)(2,1)S(1)}, bf16[8,128,128]{2,1,0:T(8,128)(2,1)S(1)}, u32[]{:S(2)}, u32[]{:S(2)}) %collective-permute-start.11) | collective-permute-done | bytes 262176 | tf_op jit(solution)/shard_map/ppermute | solution.py:251
  46.4 1.6 %collective-permute-done.13.refs_1_ = bf16[8,128,128]{2,1,0:T(8,128)(2,1)S(1)} collective-permute-done((bf16[8,128,128]{2,1,0:T(8,128)(2,1)S(1)}, bf16[8,128,128]{2,1,0:T(8,128)(2,1)S(1)}, u32[]{:S(2)}, u32[]{:S(2)}) %collective-permute-start.13) | collective-permute-done | bytes 262176 | tf_op jit(solution)/shard_map/ppermute | solution.py:249
  48.0 5.2 %collective-permute-done.16.refs_1_ = bf16[8,128,128]{2,1,0:T(8,128)(2,1)S(1)} collective-permute-done((bf16[8,128,128]{2,1,0:T(8,128)(2,1)S(1)}, bf16[8,128,128]{2,1,0:T(8,128)(2,1)S(1)}, u32[]{:S(2)}, u32[]{:S(2)}) %collective-permute-start.16) | collective-permute-done | bytes 262176 | tf_op jit(solution)/shard_map/ppermute | solution.py:249
  54.4 2.4 %collective-permute-done.14.refs_2_ = bf16[8,128,128]{2,1,0:T(8,128)(2,1)S(1)} collective-permute-done((bf16[8,128,128]{2,1,0:T(8,128)(2,1)S(1)}, bf16[8,128,128]{2,1,0:T(8,128)(2,1)S(1)}, u32[]{:S(2)}, u32[]{:S(2)}) %collective-permute-start.14) | collective-permute-done | bytes 262176 | tf_op jit(solution)/shard_map/ppermute | solution.py:251
  57.1 1.2 %collective-permute-start.22 = (bf16[8,128,128]{2,1,0:T(8,128)(2,1)S(1)}, bf16[8,128,128]{2,1,0:T(8,128)(2,1)S(1)}, u32[]{:S(2)}, u32[]{:S(2)}) collective-permute-start(bf16[8,128,128]{2,1,0:T(8,128)(2,1)S(1)} %get-tuple-element.51.that.this), channel_id=1, source_target_pairs={{0,1},{1,0},{2,3},{3,2},{4,5},{5,4},{6,7},{7,6},{8,9},{9,8},{10,11... | collective-permute-start | bytes 786440 | tf_op jit(solution)/shard_map/ppermute | solution.py:249
  58.3 3.8 %collective-permute-done.17.refs_2_ = bf16[8,128,128]{2,1,0:T(8,128)(2,1)S(1)} collective-permute-done((bf16[8,128,128]{2,1,0:T(8,128)(2,1)S(1)}, bf16[8,128,128]{2,1,0:T(8,128)(2,1)S(1)}, u32[]{:S(2)}, u32[]{:S(2)}) %collective-permute-start.17) | collective-permute-done | bytes 262176 | tf_op jit(solution)/shard_map/ppermute | solution.py:251
  62.6 1.6 %collective-permute-start.18 = (bf16[8,128,128]{2,1,0:T(8,128)(2,1)S(1)}, bf16[8,128,128]{2,1,0:T(8,128)(2,1)S(1)}, u32[]{:S(2)}, u32[]{:S(2)}) collective-permute-start(bf16[8,128,128]{2,1,0:T(8,128)(2,1)S(1)} %get-tuple-element.50.this.that), channel_id=1, source_target_pairs={{0,8},{8,0},{16,24},{24,16},{1,9},{9,1},{17,25},{25,17},{2,10},{10... | collective-permute-start | bytes 786440 | tf_op jit(solution)/shard_map/ppermute | solution.py:250
  64.6 4.8 %collective-permute-done.19.refs_1_ = bf16[8,128,128]{2,1,0:T(8,128)(2,1)S(1)} collective-permute-done((bf16[8,128,128]{2,1,0:T(8,128)(2,1)S(1)}, bf16[8,128,128]{2,1,0:T(8,128)(2,1)S(1)}, u32[]{:S(2)}, u32[]{:S(2)}) %collective-permute-start.19) | collective-permute-done | bytes 262176 | tf_op jit(solution)/shard_map/ppermute | solution.py:249
  69.5 1.2 %correction.1 = f32[1,16,128,128]{3,2,1,0:T(8,128)} custom-call(bf16[8,128,128]{2,1,0:T(8,128)(2,1)S(1)} %get-tuple-element.28.residual.refs_4_.residual_a, bf16[8,128,128]{2,1,0:T(8,128)(2,1)S(1)} %get-tuple-element.30.residual.refs_4_.residual_b, f32[8,128,128]{2,1,0:T(8,128)S(1)} %get-tuple-element.34.refs_4_.refs_0_, ...), custom_call_target="tpu_custom_call" | custom-call | bytes 3670016 | tf_op jit(solution)/shard_map/correction/pallas_call | solution.py:43
  72.3 3.4 %collective-permute-done.23.refs_2_ = bf16[8,128,128]{2,1,0:T(8,128)(2,1)S(1)} collective-permute-done((bf16[8,128,128]{2,1,0:T(8,128)(2,1)S(1)}, bf16[8,128,128]{2,1,0:T(8,128)(2,1)S(1)}, u32[]{:S(2)}, u32[]{:S(2)}) %collective-permute-start.23) | collective-permute-done | bytes 262176 | tf_op jit(solution)/shard_map/ppermute | solution.py:251
  76.7 3.1 %collective-permute-done.20.refs_2_ = bf16[8,128,128]{2,1,0:T(8,128)(2,1)S(1)} collective-permute-done((bf16[8,128,128]{2,1,0:T(8,128)(2,1)S(1)}, bf16[8,128,128]{2,1,0:T(8,128)(2,1)S(1)}, u32[]{:S(2)}, u32[]{:S(2)}) %collective-permute-start.20) | collective-permute-done | bytes 262176 | tf_op jit(solution)/shard_map/ppermute | solution.py:251
  79.9 1.0 %time_terms_last.3 = f32[1,16,128,128]{3,2,1,0:T(8,128)} custom-call(f32[8,128,128]{2,1,0:T(8,128)S(1)} %local_terms.14.refs_0_, bf16[8,128,128]{2,1,0:T(8,128)(2,1)S(1)} %collective-permute-done.19.refs_1_, bf16[8,128,128]{2,1,0:T(8,128)(2,1)S(1)} %collective-permute-done.20.refs_2_, ...), custom_call_target="tpu_custom_call", output_to_operand_aliasing={{}: (4, {})} | custom-call | flops 67108864 | bytes 2621440 | tf_op jit(solution)/shard_map/time_terms_last/pallas_call | solution.py:43
  (44 shorter events, 15.6 us)
Async XLA Ops:
  1.6 10.0 %collective-permute-start.1 = (bf16[8,128,128]{2,1,0:T(8,128)(2,1)S(1)}, bf16[8,128,128]{2,1,0:T(8,128)(2,1)S(1)}, u32[]{:S(2)}, u32[]{:S(2)}) collective-permute-start(bf16[8,128,128]{2,1,0:T(8,128)(2,1)S(1)} %get-tuple-element.31.this.that), channel_id=1, source_target_pairs={{0,1},{1,0},{2,3},{3,2},{4,5},{5,4},{6,7},{7,6},{8,9},{9,8},{10,11... | collective-permute-start | bytes 786440 | tf_op jit(solution)/shard_map/ppermute | solution.py:249
  8.0 8.5 %collective-permute-start.4 = (bf16[8,128,128]{2,1,0:T(8,128)(2,1)S(1)}, bf16[8,128,128]{2,1,0:T(8,128)(2,1)S(1)}, u32[]{:S(2)}, u32[]{:S(2)}) collective-permute-start(bf16[8,128,128]{2,1,0:T(8,128)(2,1)S(1)} %get-tuple-element.32.that.this), channel_id=1, source_target_pairs={{0,1},{1,0},{2,3},{3,2},{4,5},{5,4},{6,7},{7,6},{8,9},{9,8},{10,11... | collective-permute-start | bytes 786440 | tf_op jit(solution)/shard_map/ppermute | solution.py:249
  8.1 10.2 %collective-permute-start = (bf16[8,128,128]{2,1,0:T(8,128)(2,1)S(1)}, bf16[8,128,128]{2,1,0:T(8,128)(2,1)S(1)}, u32[]{:S(2)}, u32[]{:S(2)}) collective-permute-start(bf16[8,128,128]{2,1,0:T(8,128)(2,1)S(1)} %get-tuple-element.31.this.that), channel_id=1, source_target_pairs={{0,24},{8,16},{16,8},{24,0},{1,25},{9,17},{17,9},{25,1},{2,26},{10... | collective-permute-start | bytes 786440 | tf_op jit(solution)/shard_map/ppermute | solution.py:250
  9.0 10.0 %collective-permute-start.3 = (bf16[8,128,128]{2,1,0:T(8,128)(2,1)S(1)}, bf16[8,128,128]{2,1,0:T(8,128)(2,1)S(1)}, u32[]{:S(2)}, u32[]{:S(2)}) collective-permute-start(bf16[8,128,128]{2,1,0:T(8,128)(2,1)S(1)} %get-tuple-element.32.that.this), channel_id=1, source_target_pairs={{0,8},{8,0},{16,24},{24,16},{1,9},{9,1},{17,25},{25,17},{2,10},{10... | collective-permute-start | bytes 786440 | tf_op jit(solution)/shard_map/ppermute | solution.py:250
  11.6 8.7 %collective-permute-start.2 = (bf16[8,128,128]{2,1,0:T(8,128)(2,1)S(1)}, bf16[8,128,128]{2,1,0:T(8,128)(2,1)S(1)}, u32[]{:S(2)}, u32[]{:S(2)}) collective-permute-start(bf16[8,128,128]{2,1,0:T(8,128)(2,1)S(1)} %collective-permute-done.1.refs_1_), channel_id=1, source_target_pairs={{0,2},{1,7},{2,4},{3,1},{4,6},{5,3},{6,0},{7,5},{8,10},{9,15},{10,... | collective-permute-start | bytes 786440 | tf_op jit(solution)/shard_map/ppermute | solution.py:251
  16.6 9.5 %collective-permute-start.5 = (bf16[8,128,128]{2,1,0:T(8,128)(2,1)S(1)}, bf16[8,128,128]{2,1,0:T(8,128)(2,1)S(1)}, u32[]{:S(2)}, u32[]{:S(2)}) collective-permute-start(bf16[8,128,128]{2,1,0:T(8,128)(2,1)S(1)} %collective-permute-done.4.refs_1_), channel_id=1, source_target_pairs={{0,2},{1,7},{2,4},{3,1},{4,6},{5,3},{6,0},{7,5},{8,10},{9,15},{10,... | collective-permute-start | bytes 786440 | tf_op jit(solution)/shard_map/ppermute | solution.py:251
  20.6 9.3 %collective-permute-start.7 = (bf16[8,128,128]{2,1,0:T(8,128)(2,1)S(1)}, bf16[8,128,128]{2,1,0:T(8,128)(2,1)S(1)}, u32[]{:S(2)}, u32[]{:S(2)}) collective-permute-start(bf16[8,128,128]{2,1,0:T(8,128)(2,1)S(1)} %get-tuple-element.38.this.that), channel_id=1, source_target_pairs={{0,1},{1,0},{2,3},{3,2},{4,5},{5,4},{6,7},{7,6},{8,9},{9,8},{10,11... | collective-permute-start | bytes 786440 | tf_op jit(solution)/shard_map/ppermute | solution.py:249
  26.4 7.8 %collective-permute-start.10 = (bf16[8,128,128]{2,1,0:T(8,128)(2,1)S(1)}, bf16[8,128,128]{2,1,0:T(8,128)(2,1)S(1)}, u32[]{:S(2)}, u32[]{:S(2)}) collective-permute-start(bf16[8,128,128]{2,1,0:T(8,128)(2,1)S(1)} %get-tuple-element.39.that.this), channel_id=1, source_target_pairs={{0,1},{1,0},{2,3},{3,2},{4,5},{5,4},{6,7},{7,6},{8,9},{9,8},{10,11... | collective-permute-start | bytes 786440 | tf_op jit(solution)/shard_map/ppermute | solution.py:249
  27.3 7.0 %collective-permute-start.9 = (bf16[8,128,128]{2,1,0:T(8,128)(2,1)S(1)}, bf16[8,128,128]{2,1,0:T(8,128)(2,1)S(1)}, u32[]{:S(2)}, u32[]{:S(2)}) collective-permute-start(bf16[8,128,128]{2,1,0:T(8,128)(2,1)S(1)} %get-tuple-element.39.that.this), channel_id=1, source_target_pairs={{0,8},{8,0},{16,24},{24,16},{1,9},{9,1},{17,25},{25,17},{2,10},{10... | collective-permute-start | bytes 786440 | tf_op jit(solution)/shard_map/ppermute | solution.py:250
  27.3 8.0 %collective-permute-start.6 = (bf16[8,128,128]{2,1,0:T(8,128)(2,1)S(1)}, bf16[8,128,128]{2,1,0:T(8,128)(2,1)S(1)}, u32[]{:S(2)}, u32[]{:S(2)}) collective-permute-start(bf16[8,128,128]{2,1,0:T(8,128)(2,1)S(1)} %get-tuple-element.38.this.that), channel_id=1, source_target_pairs={{0,24},{8,16},{16,8},{24,0},{1,25},{9,17},{17,9},{25,1},{2,26},{10... | collective-permute-start | bytes 786440 | tf_op jit(solution)/shard_map/ppermute | solution.py:250
  29.9 11.0 %collective-permute-start.8 = (bf16[8,128,128]{2,1,0:T(8,128)(2,1)S(1)}, bf16[8,128,128]{2,1,0:T(8,128)(2,1)S(1)}, u32[]{:S(2)}, u32[]{:S(2)}) collective-permute-start(bf16[8,128,128]{2,1,0:T(8,128)(2,1)S(1)} %collective-permute-done.7.refs_1_), channel_id=1, source_target_pairs={{0,2},{1,7},{2,4},{3,1},{4,6},{5,3},{6,0},{7,5},{8,10},{9,15},{10,... | collective-permute-start | bytes 786440 | tf_op jit(solution)/shard_map/ppermute | solution.py:251
  34.2 11.1 %collective-permute-start.11 = (bf16[8,128,128]{2,1,0:T(8,128)(2,1)S(1)}, bf16[8,128,128]{2,1,0:T(8,128)(2,1)S(1)}, u32[]{:S(2)}, u32[]{:S(2)}) collective-permute-start(bf16[8,128,128]{2,1,0:T(8,128)(2,1)S(1)} %collective-permute-done.10.refs_1_), channel_id=1, source_target_pairs={{0,2},{1,7},{2,4},{3,1},{4,6},{5,3},{6,0},{7,5},{8,10},{9,15},{10,... | collective-permute-start | bytes 786440 | tf_op jit(solution)/shard_map/ppermute | solution.py:251
  41.2 6.8 %collective-permute-start.13 = (bf16[8,128,128]{2,1,0:T(8,128)(2,1)S(1)}, bf16[8,128,128]{2,1,0:T(8,128)(2,1)S(1)}, u32[]{:S(2)}, u32[]{:S(2)}) collective-permute-start(bf16[8,128,128]{2,1,0:T(8,128)(2,1)S(1)} %get-tuple-element.44.this.that), channel_id=1, source_target_pairs={{0,1},{1,0},{2,3},{3,2},{4,5},{5,4},{6,7},{7,6},{8,9},{9,8},{10,11... | collective-permute-start | bytes 786440 | tf_op jit(solution)/shard_map/ppermute | solution.py:249
  45.6 7.6 %collective-permute-start.16 = (bf16[8,128,128]{2,1,0:T(8,128)(2,1)S(1)}, bf16[8,128,128]{2,1,0:T(8,128)(2,1)S(1)}, u32[]{:S(2)}, u32[]{:S(2)}) collective-permute-start(bf16[8,128,128]{2,1,0:T(8,128)(2,1)S(1)} %get-tuple-element.45.that.this), channel_id=1, source_target_pairs={{0,1},{1,0},{2,3},{3,2},{4,5},{5,4},{6,7},{7,6},{8,9},{9,8},{10,11... | collective-permute-start | bytes 786440 | tf_op jit(solution)/shard_map/ppermute | solution.py:249
  45.7 7.6 %collective-permute-start.15 = (bf16[8,128,128]{2,1,0:T(8,128)(2,1)S(1)}, bf16[8,128,128]{2,1,0:T(8,128)(2,1)S(1)}, u32[]{:S(2)}, u32[]{:S(2)}) collective-permute-start(bf16[8,128,128]{2,1,0:T(8,128)(2,1)S(1)} %get-tuple-element.45.that.this), channel_id=1, source_target_pairs={{0,8},{8,0},{16,24},{24,16},{1,9},{9,1},{17,25},{25,17},{2,10},{10... | collective-permute-start | bytes 786440 | tf_op jit(solution)/shard_map/ppermute | solution.py:250
  45.8 8.1 %collective-permute-start.12 = (bf16[8,128,128]{2,1,0:T(8,128)(2,1)S(1)}, bf16[8,128,128]{2,1,0:T(8,128)(2,1)S(1)}, u32[]{:S(2)}, u32[]{:S(2)}) collective-permute-start(bf16[8,128,128]{2,1,0:T(8,128)(2,1)S(1)} %get-tuple-element.44.this.that), channel_id=1, source_target_pairs={{0,24},{8,16},{16,8},{24,0},{1,25},{9,17},{17,9},{25,1},{2,26},{10... | collective-permute-start | bytes 786440 | tf_op jit(solution)/shard_map/ppermute | solution.py:250
  48.0 8.8 %collective-permute-start.14 = (bf16[8,128,128]{2,1,0:T(8,128)(2,1)S(1)}, bf16[8,128,128]{2,1,0:T(8,128)(2,1)S(1)}, u32[]{:S(2)}, u32[]{:S(2)}) collective-permute-start(bf16[8,128,128]{2,1,0:T(8,128)(2,1)S(1)} %collective-permute-done.13.refs_1_), channel_id=1, source_target_pairs={{0,2},{1,7},{2,4},{3,1},{4,6},{5,3},{6,0},{7,5},{8,10},{9,15},{10,... | collective-permute-start | bytes 786440 | tf_op jit(solution)/shard_map/ppermute | solution.py:251
  53.2 8.9 %collective-permute-start.17 = (bf16[8,128,128]{2,1,0:T(8,128)(2,1)S(1)}, bf16[8,128,128]{2,1,0:T(8,128)(2,1)S(1)}, u32[]{:S(2)}, u32[]{:S(2)}) collective-permute-start(bf16[8,128,128]{2,1,0:T(8,128)(2,1)S(1)} %collective-permute-done.16.refs_1_), channel_id=1, source_target_pairs={{0,2},{1,7},{2,4},{3,1},{4,6},{5,3},{6,0},{7,5},{8,10},{9,15},{10,... | collective-permute-start | bytes 786440 | tf_op jit(solution)/shard_map/ppermute | solution.py:251
  57.1 7.5 %collective-permute-start.22 = (bf16[8,128,128]{2,1,0:T(8,128)(2,1)S(1)}, bf16[8,128,128]{2,1,0:T(8,128)(2,1)S(1)}, u32[]{:S(2)}, u32[]{:S(2)}) collective-permute-start(bf16[8,128,128]{2,1,0:T(8,128)(2,1)S(1)} %get-tuple-element.51.that.this), channel_id=1, source_target_pairs={{0,1},{1,0},{2,3},{3,2},{4,5},{5,4},{6,7},{7,6},{8,9},{9,8},{10,11... | collective-permute-start | bytes 786440 | tf_op jit(solution)/shard_map/ppermute | solution.py:249
  62.4 7.1 %collective-permute-start.19 = (bf16[8,128,128]{2,1,0:T(8,128)(2,1)S(1)}, bf16[8,128,128]{2,1,0:T(8,128)(2,1)S(1)}, u32[]{:S(2)}, u32[]{:S(2)}) collective-permute-start(bf16[8,128,128]{2,1,0:T(8,128)(2,1)S(1)} %get-tuple-element.50.this.that), channel_id=1, source_target_pairs={{0,1},{1,0},{2,3},{3,2},{4,5},{5,4},{6,7},{7,6},{8,9},{9,8},{10,11... | collective-permute-start | bytes 786440 | tf_op jit(solution)/shard_map/ppermute | solution.py:249
  62.6 8.6 %collective-permute-start.21 = (bf16[8,128,128]{2,1,0:T(8,128)(2,1)S(1)}, bf16[8,128,128]{2,1,0:T(8,128)(2,1)S(1)}, u32[]{:S(2)}, u32[]{:S(2)}) collective-permute-start(bf16[8,128,128]{2,1,0:T(8,128)(2,1)S(1)} %get-tuple-element.51.that.this), channel_id=1, source_target_pairs={{0,24},{8,16},{16,8},{24,0},{1,25},{9,17},{17,9},{25,1},{2,26},{10... | collective-permute-start | bytes 786440 | tf_op jit(solution)/shard_map/ppermute | solution.py:250
  62.6 9.1 %collective-permute-start.18 = (bf16[8,128,128]{2,1,0:T(8,128)(2,1)S(1)}, bf16[8,128,128]{2,1,0:T(8,128)(2,1)S(1)}, u32[]{:S(2)}, u32[]{:S(2)}) collective-permute-start(bf16[8,128,128]{2,1,0:T(8,128)(2,1)S(1)} %get-tuple-element.50.this.that), channel_id=1, source_target_pairs={{0,8},{8,0},{16,24},{24,16},{1,9},{9,1},{17,25},{25,17},{2,10},{10... | collective-permute-start | bytes 786440 | tf_op jit(solution)/shard_map/ppermute | solution.py:250
  64.6 11.1 %collective-permute-start.23 = (bf16[8,128,128]{2,1,0:T(8,128)(2,1)S(1)}, bf16[8,128,128]{2,1,0:T(8,128)(2,1)S(1)}, u32[]{:S(2)}, u32[]{:S(2)}) collective-permute-start(bf16[8,128,128]{2,1,0:T(8,128)(2,1)S(1)} %collective-permute-done.22.refs_1_), channel_id=1, source_target_pairs={{0,2},{1,7},{2,4},{3,1},{4,6},{5,3},{6,0},{7,5},{8,10},{9,15},{10,... | collective-permute-start | bytes 786440 | tf_op jit(solution)/shard_map/ppermute | solution.py:251
  69.5 10.4 %collective-permute-start.20 = (bf16[8,128,128]{2,1,0:T(8,128)(2,1)S(1)}, bf16[8,128,128]{2,1,0:T(8,128)(2,1)S(1)}, u32[]{:S(2)}, u32[]{:S(2)}) collective-permute-start(bf16[8,128,128]{2,1,0:T(8,128)(2,1)S(1)} %collective-permute-done.19.refs_1_), channel_id=1, source_target_pairs={{0,2},{1,7},{2,4},{3,1},{4,6},{5,3},{6,0},{7,5},{8,10},{9,15},{10,... | collective-permute-start | bytes 786440 | tf_op jit(solution)/shard_map/ppermute | solution.py:251

commit v4 on v3

--- a/solution.py
+++ b/solution.py
@@ -75,9 +75,9 @@
 
 
 def prep_kernel(batch, self_hbm, hop_hbm, *refs):
-    local_refs, time_refs, (self_ref, hop_ref, sems) = refs[:2], refs[2:4], refs[4:]
+    local_refs, time_ref, (self_ref, hop_ref, sems) = refs[:2], refs[2], refs[3:]
     sites = hop_ref.shape[0]
-    width = local_refs[0].shape[1]
+    width = time_ref.shape[1]
     parity = lax.axis_index("site") % 2
     copies = []
     for i in range(sites // batch):
@@ -109,8 +109,9 @@
         ]
         for k, part in enumerate(parts):
             local_refs[piece][own, :, k * width : (k + 1) * width] = part.astype(BF16)
-        time_refs[piece][own, :, :width] = hop(6 + parity).astype(BF16)
-        time_refs[piece][own, :, width:] = hop(7 - parity).astype(BF16)
+        if piece == 1:
+            time_ref[own, :, :width] = hop(6 + parity).astype(BF16)
+            time_ref[own, :, width:] = hop(7 - parity).astype(BF16)
 
 
 def prep(self_block, hop_blocks, sites):
@@ -119,7 +120,7 @@
     weight = lambda parts: pltpu.VMEM((PLANE, width, parts * width), BF16)
     outs = call(
         functools.partial(prep_kernel, batch),
-        [weight(6)] * 2 + [weight(2)] * 2,
+        [weight(6), weight(6), weight(2)],
         [self_block, hop_blocks],
         0,
         "prep",
@@ -130,7 +131,22 @@
             pltpu.SemaphoreType.DMA((2, sites // batch)),
         ],
     )
-    return outs[:2], outs[2:4]
+    return outs[:2], outs[2]
+
+
+def partner_kernel(blocks, time_ref):
+    width = time_ref.shape[1]
+    parity = (lax.axis_index("site") + 1) % 2
+    for s in range(PLANE):
+        time_ref[s, :, :width] = real_form(blocks[s, parity]).astype(BF16)
+        time_ref[s, :, width:] = real_form(blocks[s, 1 - parity]).astype(BF16)
+
+
+def middle_kernel(near, own, weight, *refs):
+    out = refs[-1]
+    for s in range(PLANE):
+        around = jnp.concatenate([own[s], near[s]], axis=1)
+        out[s] = times(around, weight[s]).astype(BF16)
 
 
 def times(vector, weight):
@@ -139,9 +155,15 @@
     )
 
 
-def first_kernel(piece, residual_hbm, *refs):
-    residual, sent_out, sems = refs[-3:]
+def first_kernel(piece, sites, residual_hbm, other, *refs):
     base = plane_of(piece) * PLANE
+    if piece == 0:
+        residual, sent_out, blocks, sems, sem = refs
+        there = pl.ds(pl.multiple_of(lax.axis_index("group") * sites + base, PLANE), PLANE)
+        last = pltpu.make_async_copy(other.at[0, there, pl.ds(6, 2)], blocks, sem)
+        last.start()
+    else:
+        residual, sent_out, sems = refs
     copies = [
         pltpu.make_async_copy(residual_hbm.at[0, base + s], residual.at[s], sems.at[s])
         for s in range(PLANE)
@@ -151,6 +173,8 @@
     for s in range(PLANE):
         copies[s].wait()
         sent_out[s] = (residual[s].astype(F32) * (half_width / center_value)).astype(BF16)
+    if piece == 0:
+        last.wait()
 
 
 def local_kernel(this, that, halo, weight, residual, acc):
@@ -174,7 +198,7 @@
 
 
 def time_kernel(piece, mode, scale, *refs):
-    acc, near, far, weight = refs[:4]
+    acc, far = refs[:2]
     if mode == "last":
         whole, out, sems = refs[-3:]
         base = plane_of(piece) * PLANE
@@ -182,12 +206,16 @@
             pltpu.make_async_copy(out.at[s], whole.at[0, base + s], sems.at[s]) for s in range(PLANE)
         ]
     else:
-        direction = refs[4]
+        direction = refs[2]
         out, direction_out, sent_out = refs[-3:]
 
     for s in range(PLANE):
-        around = jnp.concatenate([near[s], far[s]], axis=1)
-        now = acc[s] - times(around, weight[s])
+        if piece == 1:
+            near, weight = refs[-5:-3] if mode == "last" else refs[3:5]
+            around = jnp.concatenate([near[s], far[s]], axis=1)
+            now = acc[s] - times(around, weight[s])
+        else:
+            now = acc[s] - far[s].astype(F32)
         out[s] = now
         if mode == "last":
             copies[s].start()
@@ -218,6 +246,7 @@
     assert sites == 2 * PLANE and slices % 2 == 0 and groups % 2 == 0
     swap = [(t, t ^ 1) for t in range(slices)]
     relay = [(t, (t + 2 - 4 * (t % 2)) % slices) for t in range(slices)]
+    shift = [(b, a) for a, b in relay]
     cores = [(i, i ^ 1) for i in range(groups)]
     chips = [(i, (i - 1 + 2 * (i % 2)) % groups) for i in range(groups)]
 
@@ -227,28 +256,49 @@
     flops = 2 * PLANE * count * width * width
     scales = coefficients()
 
+    comps = width // 2
     weight_local, weight_time = prep(self_block, hop_blocks, sites)
-    start, sent = zip(
-        *[
-            call(
-                functools.partial(first_kernel, i),
-                [piece(BF16), piece(BF16)],
-                [residual_in] + [weight_local[0]] * i,
-                0,
-                "first_direction",
-                in_specs=[IN_HBM] + [WHOLE] * i,
-                scratch=[pltpu.SemaphoreType.DMA((PLANE,))],
-            )
-            for i in range(2)
-        ]
-    )
+    sems = pltpu.SemaphoreType.DMA((PLANE,))
+    start_0, sent_0, blocks = call(
+        functools.partial(first_kernel, 0, sites),
+        [piece(BF16), piece(BF16), pltpu.VMEM((PLANE, 2, comps, width), BF16)],
+        [residual_in, hop_blocks],
+        0,
+        "first_direction",
+        in_specs=[IN_HBM] * 2,
+        scratch=[sems, pltpu.SemaphoreType.DMA],
+    )
+    start_1, sent_1 = call(
+        functools.partial(first_kernel, 1, sites),
+        [piece(BF16), piece(BF16)],
+        [residual_in, sent_0],
+        0,
+        "first_direction",
+        in_specs=[IN_HBM, WHOLE],
+        scratch=[sems],
+    )
+    start, sent = [start_0, start_1], [sent_0, sent_1]
+    weight_partner = call(
+        partner_kernel,
+        [pltpu.VMEM((PLANE, width, 2 * width), BF16)],
+        [lax.ppermute(blocks, "site", swap)],
+        0,
+        "partner_weights",
+    )[0]
     residual, direction = start, start
     directions = []
     for number in range(STEPS):
         first, last = number == 0, number == STEPS - 1
-        near = [lax.ppermute(v, "site", swap) for v in sent]
+        near = [lax.ppermute(sent[0], "site", shift), lax.ppermute(sent[1], "site", swap)]
         halo = [lax.ppermute(sent[0], "group", chips), lax.ppermute(sent[1], "group", cores)]
-        far = [lax.ppermute(v, "site", relay) for v in near]
+        terms = call(
+            middle_kernel,
+            [piece(BF16)],
+            [near[0], sent[0], weight_partner] + ([weight_local[0]] if first else []),
+            2 * flops,
+            "partner_terms",
+        )[0]
+        far = [lax.ppermute(terms, "site", swap), lax.ppermute(near[1], "site", relay)]
         acc = [
             call(
                 local_kernel,
@@ -259,7 +309,8 @@
             )[0]
             for i in range(2)
         ]
-        operands = lambda i: [acc[i], near[i], far[i], weight_time[i]]
+        operands = lambda i: [acc[i], far[i]]
+        extra = [[], [near[1], weight_time]]
         if last:
             correction = call(sum_kernel, [whole], [*start, *sum(directions, ())], 0, "correction")[0]
             result = []
@@ -267,11 +318,11 @@
                 result = call(
                     functools.partial(time_kernel, i, "last", None),
                     [whole],
-                    [*operands(i), *result],
+                    [*operands(i), *result, *extra[i]],
                     2 * flops,
                     "time_terms_last",
-                    aliases={4: 0} if result else None,
-                    in_specs=[WHOLE] * 4 + [IN_HBM] * len(result),
+                    aliases={2: 0} if result else None,
+                    in_specs=[WHOLE] * 2 + [IN_HBM] * len(result) + [WHOLE] * len(extra[i]),
                     out_specs=[IN_HBM],
                     scratch=[piece(F32), pltpu.SemaphoreType.DMA((PLANE,))],
                 )
@@ -282,7 +333,7 @@
                 call(
                     functools.partial(time_kernel, i, mode, scales[number]),
                     [piece(F32), piece(F32), piece(BF16)],
-                    [*operands(i), direction[i]],
+                    [*operands(i), direction[i], *extra[i]],
                     2 * flops,
                     "time_terms",
                 )

time: 81.2 us -> 80.5 us (level)
  waiting for transfers between devices: 47.6 us -> 31.4 us
  starting transfers between devices: 18.6 us -> 33.4 us
    ppermute x16 -> x17, waiting for transfers between devices: 46.7 us -> 24.8 us  [the longest x4 9.02 us: body(): lax.ppermute(sent[0], 'site', shift)]
    ppermute x16 -> x17, starting transfers between devices: 12.6 us -> 31 us  [the longest x4 14 us: body(): lax.ppermute(sent[0], 'site', shift)]
    ppermute x4, waiting for transfers between devices: 0.93 us -> 6.58 us  [body(): lax.ppermute(sent[0], 'group', chips)]
    ppermute x4, starting transfers between devices: 3.1 us -> 0.44 us  [body(): lax.ppermute(sent[0], 'group', chips)]
    ppermute x4, starting transfers between devices: 2.91 us -> 1.93 us  [body(): lax.ppermute(sent[1], 'group', cores)]
    pallas_call x20 -> x25, Pallas kernels: 13.9 us -> 14.6 us  [call(): pl.pallas_call(kernel, out_shape=outs, in_specs=in_specs, out_specs=out_s...]
  transfers between devices with their start and end apart: 24 -> 25, of which waited for: 18 -> 17; matrix products, arithmetic and copies ran while one was open for 0% -> 0% of each run, Pallas kernels for 15% -> 15%
where the time goes in v4:
time: 80.5 us; the launch traced here: 80.3 us
  starting transfers between devices  33.4 us (41%)
  waiting for transfers between devices  31.4 us (39%)
  Pallas kernels  14.6 us (18%)
  between operations  0.84 us (1%)
    pallas_call x25, Pallas kernels, call(): pl.pallas_call(kernel, out_shape=outs, in_specs=in_specs, out_specs=out_s...  14.6 us
    ppermute x4, starting transfers between devices, body(): lax.ppermute(sent[0], 'site', shift)  14 us
    ppermute x4, waiting for transfers between devices, body(): lax.ppermute(sent[0], 'site', shift)  9.02 us
    ppermute x4, waiting for transfers between devices, body(): lax.ppermute(terms, 'site', swap)  8.8 us
    ppermute x4, waiting for transfers between devices, body(): lax.ppermute(sent[0], 'group', chips)  6.58 us
    ppermute x4, starting transfers between devices, body(): lax.ppermute(terms, 'site', swap)  5.29 us
    ppermute x4, starting transfers between devices, body(): lax.ppermute(sent[1], 'site', swap)  4.79 us
    ppermute x4, starting transfers between devices, body(): lax.ppermute(near[1], 'site', relay)  3.91 us
  transfers between devices with their start and end apart: 25, of which 17 were waited for; matrix products, arithmetic and copies ran while one was open for 0% of the time, Pallas kernels for 15%

profile of v4, /device:TPU:0, one launch (start us, length us, event | category | flops | bytes accessed | tf_op | source)
XLA Modules:
  0.0 80.3 jit_solution(2432644884325494935)
XLA Ops:
  1.8 3.0 %collective-permute-start.2 = (bf16[8,2,64,128]{3,2,1,0:T(8,128)(2,1)S(1)}, bf16[8,2,64,128]{3,2,1,0:T(8,128)(2,1)S(1)}, u32[]{:S(2)}, u32[]{:S(2)}) collective-permute-start(bf16[8,2,64,128]{3,2,1,0:T(8,128)(2,1)S(1)} %get-tuple-element.33), channel_id=1, source_target_pairs={{0,1},{1,0},{2,3},{3,2},{4,5},{5,4},{6,7},{7,6},{8,9},{9,8},{10,11... | collective-permute-start | bytes 786440 | tf_op jit(solution)/shard_map/ppermute | solution.py:284
  4.9 3.6 %collective-permute-start.1 = (bf16[8,128,128]{2,1,0:T(8,128)(2,1)S(1)}, bf16[8,128,128]{2,1,0:T(8,128)(2,1)S(1)}, u32[]{:S(2)}, u32[]{:S(2)}) collective-permute-start(bf16[8,128,128]{2,1,0:T(8,128)(2,1)S(1)} %get-tuple-element.29.other.this.own.that), channel_id=1, source_target_pairs={{2,0},{7,1},{4,2},{1,3},{6,4},{3,5},{0,6},{5,7},{10,8},{15,9},{12,... | collective-permute-start | bytes 786440 | tf_op jit(solution)/shard_map/ppermute | solution.py:292
  9.9 2.3 %prep.1 = (bf16[8,128,768]{2,1,0:T(8,128)(2,1)S(1)}, bf16[8,128,768]{2,1,0:T(8,128)(2,1)S(1)}, bf16[8,128,256]{2,1,0:T(8,128)(2,1)S(1)}) custom-call(bf16[1,64,64,128]{3,2,1,0:T(8,128)(2,1)} %self_hbm.1, bf16[1,64,8,64,128]{4,3,2,1,0:T(8,128)(2,1)} %hop_hbm.1), custom_call_target="tpu_custom_call" | custom-call | bytes 9437184 | tf_op jit(solution)/shard_map/prep/pallas_call | solution.py:43
  12.4 1.3 %collective-permute-done.1.near = bf16[8,128,128]{2,1,0:T(8,128)(2,1)S(1)} collective-permute-done((bf16[8,128,128]{2,1,0:T(8,128)(2,1)S(1)}, bf16[8,128,128]{2,1,0:T(8,128)(2,1)S(1)}, u32[]{:S(2)}, u32[]{:S(2)}) %collective-permute-start.1) | collective-permute-done | bytes 262176 | tf_op jit(solution)/shard_map/ppermute | solution.py:292
  14.0 1.3 %collective-permute-start.3 = (bf16[8,128,128]{2,1,0:T(8,128)(2,1)S(1)}, bf16[8,128,128]{2,1,0:T(8,128)(2,1)S(1)}, u32[]{:S(2)}, u32[]{:S(2)}) collective-permute-start(bf16[8,128,128]{2,1,0:T(8,128)(2,1)S(1)} %partner_terms.4), channel_id=1, source_target_pairs={{0,1},{1,0},{2,3},{3,2},{4,5},{5,4},{6,7},{7,6},{8,9},{9,8},{10,11... | collective-permute-start | bytes 786440 | tf_op jit(solution)/shard_map/ppermute | solution.py:301
  15.7 1.3 %collective-permute-done.5.refs_3_ = bf16[8,128,128]{2,1,0:T(8,128)(2,1)S(1)} collective-permute-done((bf16[8,128,128]{2,1,0:T(8,128)(2,1)S(1)}, bf16[8,128,128]{2,1,0:T(8,128)(2,1)S(1)}, u32[]{:S(2)}, u32[]{:S(2)}) %collective-permute-start.5) | collective-permute-done | bytes 262176 | tf_op jit(solution)/shard_map/ppermute | solution.py:292
  17.0 2.7 %collective-permute-start.6 = (bf16[8,128,128]{2,1,0:T(8,128)(2,1)S(1)}, bf16[8,128,128]{2,1,0:T(8,128)(2,1)S(1)}, u32[]{:S(2)}, u32[]{:S(2)}) collective-permute-start(bf16[8,128,128]{2,1,0:T(8,128)(2,1)S(1)} %collective-permute-done.5.refs_3_), channel_id=1, source_target_pairs={{0,2},{1,7},{2,4},{3,1},{4,6},{5,3},{6,0},{7,5},{8,10},{9,15},{10,... | collective-permute-start | bytes 786440 | tf_op jit(solution)/shard_map/ppermute | solution.py:301
  20.3 2.3 %collective-permute-done.3.refs_1_ = bf16[8,128,128]{2,1,0:T(8,128)(2,1)S(1)} collective-permute-done((bf16[8,128,128]{2,1,0:T(8,128)(2,1)S(1)}, bf16[8,128,128]{2,1,0:T(8,128)(2,1)S(1)}, u32[]{:S(2)}, u32[]{:S(2)}) %collective-permute-start.3) | collective-permute-done | bytes 262176 | tf_op jit(solution)/shard_map/ppermute | solution.py:301
  22.7 3.7 %collective-permute-start.8 = (bf16[8,128,128]{2,1,0:T(8,128)(2,1)S(1)}, bf16[8,128,128]{2,1,0:T(8,128)(2,1)S(1)}, u32[]{:S(2)}, u32[]{:S(2)}) collective-permute-start(bf16[8,128,128]{2,1,0:T(8,128)(2,1)S(1)} %get-tuple-element.38.this.own.that), channel_id=1, source_target_pairs={{2,0},{7,1},{4,2},{1,3},{6,4},{3,5},{0,6},{5,7},{10,8},{15,9},{12,... | collective-permute-start | bytes 786440 | tf_op jit(solution)/shard_map/ppermute | solution.py:292
  27.3 2.5 %collective-permute-start.11 = (bf16[8,128,128]{2,1,0:T(8,128)(2,1)S(1)}, bf16[8,128,128]{2,1,0:T(8,128)(2,1)S(1)}, u32[]{:S(2)}, u32[]{:S(2)}) collective-permute-start(bf16[8,128,128]{2,1,0:T(8,128)(2,1)S(1)} %get-tuple-element.39.that.this), channel_id=1, source_target_pairs={{0,1},{1,0},{2,3},{3,2},{4,5},{5,4},{6,7},{7,6},{8,9},{9,8},{10,11... | collective-permute-start | bytes 786440 | tf_op jit(solution)/shard_map/ppermute | solution.py:292
  29.8 1.9 %collective-permute-done.8.near = bf16[8,128,128]{2,1,0:T(8,128)(2,1)S(1)} collective-permute-done((bf16[8,128,128]{2,1,0:T(8,128)(2,1)S(1)}, bf16[8,128,128]{2,1,0:T(8,128)(2,1)S(1)}, u32[]{:S(2)}, u32[]{:S(2)}) %collective-permute-start.8) | collective-permute-done | bytes 262176 | tf_op jit(solution)/shard_map/ppermute | solution.py:292
  32.0 2.7 %collective-permute-start.9 = (bf16[8,128,128]{2,1,0:T(8,128)(2,1)S(1)}, bf16[8,128,128]{2,1,0:T(8,128)(2,1)S(1)}, u32[]{:S(2)}, u32[]{:S(2)}) collective-permute-start(bf16[8,128,128]{2,1,0:T(8,128)(2,1)S(1)} %partner_terms.5), channel_id=1, source_target_pairs={{0,1},{1,0},{2,3},{3,2},{4,5},{5,4},{6,7},{7,6},{8,9},{9,8},{10,11... | collective-permute-start | bytes 786440 | tf_op jit(solution)/shard_map/ppermute | solution.py:301
  35.6 2.7 %collective-permute-done.7.halo = bf16[8,128,128]{2,1,0:T(8,128)(2,1)S(1)} collective-permute-done((bf16[8,128,128]{2,1,0:T(8,128)(2,1)S(1)}, bf16[8,128,128]{2,1,0:T(8,128)(2,1)S(1)}, u32[]{:S(2)}, u32[]{:S(2)}) %collective-permute-start.7) | collective-permute-done | bytes 262176 | tf_op jit(solution)/shard_map/ppermute | solution.py:293
  40.2 4.2 %collective-permute-start.14 = (bf16[8,128,128]{2,1,0:T(8,128)(2,1)S(1)}, bf16[8,128,128]{2,1,0:T(8,128)(2,1)S(1)}, u32[]{:S(2)}, u32[]{:S(2)}) collective-permute-start(bf16[8,128,128]{2,1,0:T(8,128)(2,1)S(1)} %get-tuple-element.44.this.own.that), channel_id=1, source_target_pairs={{2,0},{7,1},{4,2},{1,3},{6,4},{3,5},{0,6},{5,7},{10,8},{15,9},{12,... | collective-permute-start | bytes 786440 | tf_op jit(solution)/shard_map/ppermute | solution.py:292
  45.6 1.5 %collective-permute-start.17 = (bf16[8,128,128]{2,1,0:T(8,128)(2,1)S(1)}, bf16[8,128,128]{2,1,0:T(8,128)(2,1)S(1)}, u32[]{:S(2)}, u32[]{:S(2)}) collective-permute-start(bf16[8,128,128]{2,1,0:T(8,128)(2,1)S(1)} %get-tuple-element.45.that.this), channel_id=1, source_target_pairs={{0,1},{1,0},{2,3},{3,2},{4,5},{5,4},{6,7},{7,6},{8,9},{9,8},{10,11... | collective-permute-start | bytes 786440 | tf_op jit(solution)/shard_map/ppermute | solution.py:292
  47.1 3.7 %collective-permute-done.14.near = bf16[8,128,128]{2,1,0:T(8,128)(2,1)S(1)} collective-permute-done((bf16[8,128,128]{2,1,0:T(8,128)(2,1)S(1)}, bf16[8,128,128]{2,1,0:T(8,128)(2,1)S(1)}, u32[]{:S(2)}, u32[]{:S(2)}) %collective-permute-start.14) | collective-permute-done | bytes 262176 | tf_op jit(solution)/shard_map/ppermute | solution.py:292
  53.0 2.7 %collective-permute-done.13.halo = bf16[8,128,128]{2,1,0:T(8,128)(2,1)S(1)} collective-permute-done((bf16[8,128,128]{2,1,0:T(8,128)(2,1)S(1)}, bf16[8,128,128]{2,1,0:T(8,128)(2,1)S(1)}, u32[]{:S(2)}, u32[]{:S(2)}) %collective-permute-start.13) | collective-permute-done | bytes 262176 | tf_op jit(solution)/shard_map/ppermute | solution.py:293
  56.3 3.1 %collective-permute-done.15.refs_1_ = bf16[8,128,128]{2,1,0:T(8,128)(2,1)S(1)} collective-permute-done((bf16[8,128,128]{2,1,0:T(8,128)(2,1)S(1)}, bf16[8,128,128]{2,1,0:T(8,128)(2,1)S(1)}, u32[]{:S(2)}, u32[]{:S(2)}) %collective-permute-start.15) | collective-permute-done | bytes 262176 | tf_op jit(solution)/shard_map/ppermute | solution.py:301
  59.5 2.5 %collective-permute-start.23 = (bf16[8,128,128]{2,1,0:T(8,128)(2,1)S(1)}, bf16[8,128,128]{2,1,0:T(8,128)(2,1)S(1)}, u32[]{:S(2)}, u32[]{:S(2)}) collective-permute-start(bf16[8,128,128]{2,1,0:T(8,128)(2,1)S(1)} %get-tuple-element.51.that.this.own), channel_id=1, source_target_pairs={{2,0},{7,1},{4,2},{1,3},{6,4},{3,5},{0,6},{5,7},{10,8},{15,9},{12,... | collective-permute-start | bytes 786440 | tf_op jit(solution)/shard_map/ppermute | solution.py:292
  62.5 1.4 %collective-permute-done.18.refs_1_ = bf16[8,128,128]{2,1,0:T(8,128)(2,1)S(1)} collective-permute-done((bf16[8,128,128]{2,1,0:T(8,128)(2,1)S(1)}, bf16[8,128,128]{2,1,0:T(8,128)(2,1)S(1)}, u32[]{:S(2)}, u32[]{:S(2)}) %collective-permute-start.18) | collective-permute-done | bytes 262176 | tf_op jit(solution)/shard_map/ppermute | solution.py:301
  65.0 1.6 %collective-permute-start.19 = (bf16[8,128,128]{2,1,0:T(8,128)(2,1)S(1)}, bf16[8,128,128]{2,1,0:T(8,128)(2,1)S(1)}, u32[]{:S(2)}, u32[]{:S(2)}) collective-permute-start(bf16[8,128,128]{2,1,0:T(8,128)(2,1)S(1)} %get-tuple-element.50.this.that), channel_id=1, source_target_pairs={{0,8},{8,0},{16,24},{24,16},{1,9},{9,1},{17,25},{25,17},{2,10},{10... | collective-permute-start | bytes 786440 | tf_op jit(solution)/shard_map/ppermute | solution.py:293
  66.6 2.1 %collective-permute-done.23.near = bf16[8,128,128]{2,1,0:T(8,128)(2,1)S(1)} collective-permute-done((bf16[8,128,128]{2,1,0:T(8,128)(2,1)S(1)}, bf16[8,128,128]{2,1,0:T(8,128)(2,1)S(1)}, u32[]{:S(2)}, u32[]{:S(2)}) %collective-permute-start.23) | collective-permute-done | bytes 262176 | tf_op jit(solution)/shard_map/ppermute | solution.py:292
  69.5 1.6 %collective-permute-done.20.refs_3_ = bf16[8,128,128]{2,1,0:T(8,128)(2,1)S(1)} collective-permute-done((bf16[8,128,128]{2,1,0:T(8,128)(2,1)S(1)}, bf16[8,128,128]{2,1,0:T(8,128)(2,1)S(1)}, u32[]{:S(2)}, u32[]{:S(2)}) %collective-permute-start.20) | collective-permute-done | bytes 262176 | tf_op jit(solution)/shard_map/ppermute | solution.py:292
  74.8 2.3 %collective-permute-done.24.refs_1_ = bf16[8,128,128]{2,1,0:T(8,128)(2,1)S(1)} collective-permute-done((bf16[8,128,128]{2,1,0:T(8,128)(2,1)S(1)}, bf16[8,128,128]{2,1,0:T(8,128)(2,1)S(1)}, u32[]{:S(2)}, u32[]{:S(2)}) %collective-permute-start.24) | collective-permute-done | bytes 262176 | tf_op jit(solution)/shard_map/ppermute | solution.py:301
  (51 shorter events, 21.6 us)
Async XLA Ops:
  1.8 10.4 %collective-permute-start.2 = (bf16[8,2,64,128]{3,2,1,0:T(8,128)(2,1)S(1)}, bf16[8,2,64,128]{3,2,1,0:T(8,128)(2,1)S(1)}, u32[]{:S(2)}, u32[]{:S(2)}) collective-permute-start(bf16[8,2,64,128]{3,2,1,0:T(8,128)(2,1)S(1)} %get-tuple-element.33), channel_id=1, source_target_pairs={{0,1},{1,0},{2,3},{3,2},{4,5},{5,4},{6,7},{7,6},{8,9},{9,8},{10,11... | collective-permute-start | bytes 786440 | tf_op jit(solution)/shard_map/ppermute | solution.py:284
  4.9 8.9 %collective-permute-start.1 = (bf16[8,128,128]{2,1,0:T(8,128)(2,1)S(1)}, bf16[8,128,128]{2,1,0:T(8,128)(2,1)S(1)}, u32[]{:S(2)}, u32[]{:S(2)}) collective-permute-start(bf16[8,128,128]{2,1,0:T(8,128)(2,1)S(1)} %get-tuple-element.29.other.this.own.that), channel_id=1, source_target_pairs={{2,0},{7,1},{4,2},{1,3},{6,4},{3,5},{0,6},{5,7},{10,8},{15,9},{12,... | collective-permute-start | bytes 786440 | tf_op jit(solution)/shard_map/ppermute | solution.py:292
  9.4 7.6 %collective-permute-start.5 = (bf16[8,128,128]{2,1,0:T(8,128)(2,1)S(1)}, bf16[8,128,128]{2,1,0:T(8,128)(2,1)S(1)}, u32[]{:S(2)}, u32[]{:S(2)}) collective-permute-start(bf16[8,128,128]{2,1,0:T(8,128)(2,1)S(1)} %get-tuple-element.31.that.this), channel_id=1, source_target_pairs={{0,1},{1,0},{2,3},{3,2},{4,5},{5,4},{6,7},{7,6},{8,9},{9,8},{10,11... | collective-permute-start | bytes 786440 | tf_op jit(solution)/shard_map/ppermute | solution.py:292
  9.5 10.2 %collective-permute-start = (bf16[8,128,128]{2,1,0:T(8,128)(2,1)S(1)}, bf16[8,128,128]{2,1,0:T(8,128)(2,1)S(1)}, u32[]{:S(2)}, u32[]{:S(2)}) collective-permute-start(bf16[8,128,128]{2,1,0:T(8,128)(2,1)S(1)} %get-tuple-element.29.other.this.own.that), channel_id=1, source_target_pairs={{0,24},{8,16},{16,8},{24,0},{1,25},{9,17},{17,9},{25,1},{2,26},{10... | collective-permute-start | bytes 786440 | tf_op jit(solution)/shard_map/ppermute | solution.py:293
  14.0 8.5 %collective-permute-start.3 = (bf16[8,128,128]{2,1,0:T(8,128)(2,1)S(1)}, bf16[8,128,128]{2,1,0:T(8,128)(2,1)S(1)}, u32[]{:S(2)}, u32[]{:S(2)}) collective-permute-start(bf16[8,128,128]{2,1,0:T(8,128)(2,1)S(1)} %partner_terms.4), channel_id=1, source_target_pairs={{0,1},{1,0},{2,3},{3,2},{4,5},{5,4},{6,7},{7,6},{8,9},{9,8},{10,11... | collective-permute-start | bytes 786440 | tf_op jit(solution)/shard_map/ppermute | solution.py:301
  15.4 11.1 %collective-permute-start.4 = (bf16[8,128,128]{2,1,0:T(8,128)(2,1)S(1)}, bf16[8,128,128]{2,1,0:T(8,128)(2,1)S(1)}, u32[]{:S(2)}, u32[]{:S(2)}) collective-permute-start(bf16[8,128,128]{2,1,0:T(8,128)(2,1)S(1)} %get-tuple-element.31.that.this), channel_id=1, source_target_pairs={{0,8},{8,0},{16,24},{24,16},{1,9},{9,1},{17,25},{25,17},{2,10},{10... | collective-permute-start | bytes 786440 | tf_op jit(solution)/shard_map/ppermute | solution.py:293
  17.0 10.0 %collective-permute-start.6 = (bf16[8,128,128]{2,1,0:T(8,128)(2,1)S(1)}, bf16[8,128,128]{2,1,0:T(8,128)(2,1)S(1)}, u32[]{:S(2)}, u32[]{:S(2)}) collective-permute-start(bf16[8,128,128]{2,1,0:T(8,128)(2,1)S(1)} %collective-permute-done.5.refs_3_), channel_id=1, source_target_pairs={{0,2},{1,7},{2,4},{3,1},{4,6},{5,3},{6,0},{7,5},{8,10},{9,15},{10,... | collective-permute-start | bytes 786440 | tf_op jit(solution)/shard_map/ppermute | solution.py:301
  22.7 8.9 %collective-permute-start.8 = (bf16[8,128,128]{2,1,0:T(8,128)(2,1)S(1)}, bf16[8,128,128]{2,1,0:T(8,128)(2,1)S(1)}, u32[]{:S(2)}, u32[]{:S(2)}) collective-permute-start(bf16[8,128,128]{2,1,0:T(8,128)(2,1)S(1)} %get-tuple-element.38.this.own.that), channel_id=1, source_target_pairs={{2,0},{7,1},{4,2},{1,3},{6,4},{3,5},{0,6},{5,7},{10,8},{15,9},{12,... | collective-permute-start | bytes 786440 | tf_op jit(solution)/shard_map/ppermute | solution.py:292
  27.3 7.3 %collective-permute-start.11 = (bf16[8,128,128]{2,1,0:T(8,128)(2,1)S(1)}, bf16[8,128,128]{2,1,0:T(8,128)(2,1)S(1)}, u32[]{:S(2)}, u32[]{:S(2)}) collective-permute-start(bf16[8,128,128]{2,1,0:T(8,128)(2,1)S(1)} %get-tuple-element.39.that.this), channel_id=1, source_target_pairs={{0,1},{1,0},{2,3},{3,2},{4,5},{5,4},{6,7},{7,6},{8,9},{9,8},{10,11... | collective-permute-start | bytes 786440 | tf_op jit(solution)/shard_map/ppermute | solution.py:292
  29.8 8.6 %collective-permute-start.7 = (bf16[8,128,128]{2,1,0:T(8,128)(2,1)S(1)}, bf16[8,128,128]{2,1,0:T(8,128)(2,1)S(1)}, u32[]{:S(2)}, u32[]{:S(2)}) collective-permute-start(bf16[8,128,128]{2,1,0:T(8,128)(2,1)S(1)} %get-tuple-element.38.this.own.that), channel_id=1, source_target_pairs={{0,24},{8,16},{16,8},{24,0},{1,25},{9,17},{17,9},{25,1},{2,26},{10... | collective-permute-start | bytes 786440 | tf_op jit(solution)/shard_map/ppermute | solution.py:293
  32.0 8.1 %collective-permute-start.9 = (bf16[8,128,128]{2,1,0:T(8,128)(2,1)S(1)}, bf16[8,128,128]{2,1,0:T(8,128)(2,1)S(1)}, u32[]{:S(2)}, u32[]{:S(2)}) collective-permute-start(bf16[8,128,128]{2,1,0:T(8,128)(2,1)S(1)} %partner_terms.5), channel_id=1, source_target_pairs={{0,1},{1,0},{2,3},{3,2},{4,5},{5,4},{6,7},{7,6},{8,9},{9,8},{10,11... | collective-permute-start | bytes 786440 | tf_op jit(solution)/shard_map/ppermute | solution.py:301
  34.6 9.8 %collective-permute-start.10 = (bf16[8,128,128]{2,1,0:T(8,128)(2,1)S(1)}, bf16[8,128,128]{2,1,0:T(8,128)(2,1)S(1)}, u32[]{:S(2)}, u32[]{:S(2)}) collective-permute-start(bf16[8,128,128]{2,1,0:T(8,128)(2,1)S(1)} %get-tuple-element.39.that.this), channel_id=1, source_target_pairs={{0,8},{8,0},{16,24},{24,16},{1,9},{9,1},{17,25},{25,17},{2,10},{10... | collective-permute-start | bytes 786440 | tf_op jit(solution)/shard_map/ppermute | solution.py:293
  34.6 10.7 %collective-permute-start.12 = (bf16[8,128,128]{2,1,0:T(8,128)(2,1)S(1)}, bf16[8,128,128]{2,1,0:T(8,128)(2,1)S(1)}, u32[]{:S(2)}, u32[]{:S(2)}) collective-permute-start(bf16[8,128,128]{2,1,0:T(8,128)(2,1)S(1)} %collective-permute-done.11.refs_3_), channel_id=1, source_target_pairs={{0,2},{1,7},{2,4},{3,1},{4,6},{5,3},{6,0},{7,5},{8,10},{9,15},{10,... | collective-permute-start | bytes 786440 | tf_op jit(solution)/shard_map/ppermute | solution.py:301
  40.2 10.6 %collective-permute-start.14 = (bf16[8,128,128]{2,1,0:T(8,128)(2,1)S(1)}, bf16[8,128,128]{2,1,0:T(8,128)(2,1)S(1)}, u32[]{:S(2)}, u32[]{:S(2)}) collective-permute-start(bf16[8,128,128]{2,1,0:T(8,128)(2,1)S(1)} %get-tuple-element.44.this.own.that), channel_id=1, source_target_pairs={{2,0},{7,1},{4,2},{1,3},{6,4},{3,5},{0,6},{5,7},{10,8},{15,9},{12,... | collective-permute-start | bytes 786440 | tf_op jit(solution)/shard_map/ppermute | solution.py:292
  45.6 7.4 %collective-permute-start.17 = (bf16[8,128,128]{2,1,0:T(8,128)(2,1)S(1)}, bf16[8,128,128]{2,1,0:T(8,128)(2,1)S(1)}, u32[]{:S(2)}, u32[]{:S(2)}) collective-permute-start(bf16[8,128,128]{2,1,0:T(8,128)(2,1)S(1)} %get-tuple-element.45.that.this), channel_id=1, source_target_pairs={{0,1},{1,0},{2,3},{3,2},{4,5},{5,4},{6,7},{7,6},{8,9},{9,8},{10,11... | collective-permute-start | bytes 786440 | tf_op jit(solution)/shard_map/ppermute | solution.py:292
  47.1 8.6 %collective-permute-start.13 = (bf16[8,128,128]{2,1,0:T(8,128)(2,1)S(1)}, bf16[8,128,128]{2,1,0:T(8,128)(2,1)S(1)}, u32[]{:S(2)}, u32[]{:S(2)}) collective-permute-start(bf16[8,128,128]{2,1,0:T(8,128)(2,1)S(1)} %get-tuple-element.44.this.own.that), channel_id=1, source_target_pairs={{0,24},{8,16},{16,8},{24,0},{1,25},{9,17},{17,9},{25,1},{2,26},{10... | collective-permute-start | bytes 786440 | tf_op jit(solution)/shard_map/ppermute | solution.py:293
  51.1 8.3 %collective-permute-start.15 = (bf16[8,128,128]{2,1,0:T(8,128)(2,1)S(1)}, bf16[8,128,128]{2,1,0:T(8,128)(2,1)S(1)}, u32[]{:S(2)}, u32[]{:S(2)}) collective-permute-start(bf16[8,128,128]{2,1,0:T(8,128)(2,1)S(1)} %partner_terms.6), channel_id=1, source_target_pairs={{0,1},{1,0},{2,3},{3,2},{4,5},{5,4},{6,7},{7,6},{8,9},{9,8},{10,11... | collective-permute-start | bytes 786440 | tf_op jit(solution)/shard_map/ppermute | solution.py:301
  52.0 9.9 %collective-permute-start.16 = (bf16[8,128,128]{2,1,0:T(8,128)(2,1)S(1)}, bf16[8,128,128]{2,1,0:T(8,128)(2,1)S(1)}, u32[]{:S(2)}, u32[]{:S(2)}) collective-permute-start(bf16[8,128,128]{2,1,0:T(8,128)(2,1)S(1)} %get-tuple-element.45.that.this), channel_id=1, source_target_pairs={{0,8},{8,0},{16,24},{24,16},{1,9},{9,1},{17,25},{25,17},{2,10},{10... | collective-permute-start | bytes 786440 | tf_op jit(solution)/shard_map/ppermute | solution.py:293
  53.0 10.9 %collective-permute-start.18 = (bf16[8,128,128]{2,1,0:T(8,128)(2,1)S(1)}, bf16[8,128,128]{2,1,0:T(8,128)(2,1)S(1)}, u32[]{:S(2)}, u32[]{:S(2)}) collective-permute-start(bf16[8,128,128]{2,1,0:T(8,128)(2,1)S(1)} %collective-permute-done.17.refs_3_), channel_id=1, source_target_pairs={{0,2},{1,7},{2,4},{3,1},{4,6},{5,3},{6,0},{7,5},{8,10},{9,15},{10,... | collective-permute-start | bytes 786440 | tf_op jit(solution)/shard_map/ppermute | solution.py:301
  59.5 9.3 %collective-permute-start.23 = (bf16[8,128,128]{2,1,0:T(8,128)(2,1)S(1)}, bf16[8,128,128]{2,1,0:T(8,128)(2,1)S(1)}, u32[]{:S(2)}, u32[]{:S(2)}) collective-permute-start(bf16[8,128,128]{2,1,0:T(8,128)(2,1)S(1)} %get-tuple-element.51.that.this.own), channel_id=1, source_target_pairs={{2,0},{7,1},{4,2},{1,3},{6,4},{3,5},{0,6},{5,7},{10,8},{15,9},{12,... | collective-permute-start | bytes 786440 | tf_op jit(solution)/shard_map/ppermute | solution.py:292
  65.0 8.6 %collective-permute-start.22 = (bf16[8,128,128]{2,1,0:T(8,128)(2,1)S(1)}, bf16[8,128,128]{2,1,0:T(8,128)(2,1)S(1)}, u32[]{:S(2)}, u32[]{:S(2)}) collective-permute-start(bf16[8,128,128]{2,1,0:T(8,128)(2,1)S(1)} %get-tuple-element.51.that.this.own), channel_id=1, source_target_pairs={{0,24},{8,16},{16,8},{24,0},{1,25},{9,17},{17,9},{25,1},{2,26},{10... | collective-permute-start | bytes 786440 | tf_op jit(solution)/shard_map/ppermute | solution.py:293
  65.0 9.2 %collective-permute-start.19 = (bf16[8,128,128]{2,1,0:T(8,128)(2,1)S(1)}, bf16[8,128,128]{2,1,0:T(8,128)(2,1)S(1)}, u32[]{:S(2)}, u32[]{:S(2)}) collective-permute-start(bf16[8,128,128]{2,1,0:T(8,128)(2,1)S(1)} %get-tuple-element.50.this.that), channel_id=1, source_target_pairs={{0,8},{8,0},{16,24},{24,16},{1,9},{9,1},{17,25},{25,17},{2,10},{10... | collective-permute-start | bytes 786440 | tf_op jit(solution)/shard_map/ppermute | solution.py:293
  69.1 8.0 %collective-permute-start.24 = (bf16[8,128,128]{2,1,0:T(8,128)(2,1)S(1)}, bf16[8,128,128]{2,1,0:T(8,128)(2,1)S(1)}, u32[]{:S(2)}, u32[]{:S(2)}) collective-permute-start(bf16[8,128,128]{2,1,0:T(8,128)(2,1)S(1)} %partner_terms.7), channel_id=1, source_target_pairs={{0,1},{1,0},{2,3},{3,2},{4,5},{5,4},{6,7},{7,6},{8,9},{9,8},{10,11... | collective-permute-start | bytes 786440 | tf_op jit(solution)/shard_map/ppermute | solution.py:301
  71.0 8.2 %collective-permute-start.21 = (bf16[8,128,128]{2,1,0:T(8,128)(2,1)S(1)}, bf16[8,128,128]{2,1,0:T(8,128)(2,1)S(1)}, u32[]{:S(2)}, u32[]{:S(2)}) collective-permute-start(bf16[8,128,128]{2,1,0:T(8,128)(2,1)S(1)} %collective-permute-done.20.refs_3_), channel_id=1, source_target_pairs={{0,2},{1,7},{2,4},{3,1},{4,6},{5,3},{6,0},{7,5},{8,10},{9,15},{10,... | collective-permute-start | bytes 786440 | tf_op jit(solution)/shard_map/ppermute | solution.py:301
  (1 other events, 6.8 us)

commit v5 on v3

--- a/solution.py
+++ b/solution.py
@@ -11,6 +11,7 @@
 LZ = 2
 STEPS = 4
 PLANE = LY * LZ
+PIECES = 3
 
 diagonal_shift = 1.5
 center_value = 1.5
@@ -57,12 +58,12 @@
     return lax.axis_index("group") % 2
 
 
-def plane_of(piece):
-    return (piece + odd_group()) % 2
-
-
-def plane_sites(piece):
-    return pl.ds(pl.multiple_of(plane_of(piece) * PLANE, PLANE), PLANE)
+def plane_of(plane):
+    return (plane + odd_group()) % 2
+
+
+def place_of(site):
+    return plane_of(site // PLANE) * PLANE + site % PLANE
 
 
 def real_form(block):
@@ -139,55 +140,71 @@
     )
 
 
+def planes_in(piece):
+    return sorted({site // PLANE for site in piece})
+
+
+def store_edges(piece, sent_out, edges):
+    for plane, edge in zip(planes_in(piece), edges):
+        mine = [site for site in piece if site // PLANE == plane]
+        edge[pl.ds(mine[0] % PLANE, len(mine))] = sent_out[pl.ds(mine[0] - piece[0], len(mine))]
+
+
 def first_kernel(piece, residual_hbm, *refs):
-    residual, sent_out, sems = refs[-3:]
-    base = plane_of(piece) * PLANE
+    planes = len(planes_in(piece))
+    residual, sent_out, *edges, sems = refs[-3 - planes :]
     copies = [
-        pltpu.make_async_copy(residual_hbm.at[0, base + s], residual.at[s], sems.at[s])
-        for s in range(PLANE)
+        pltpu.make_async_copy(residual_hbm.at[0, place_of(site)], residual.at[s], sems.at[s])
+        for s, site in enumerate(piece)
     ]
     for copy in copies:
         copy.start()
-    for s in range(PLANE):
-        copies[s].wait()
+    for s, copy in enumerate(copies):
+        copy.wait()
         sent_out[s] = (residual[s].astype(F32) * (half_width / center_value)).astype(BF16)
-
-
-def local_kernel(this, that, halo, weight, residual, acc):
+    store_edges(piece, sent_out, edges)
+
+
+def local_kernel(plane, pieces, halo, weight, *refs):
+    count = len(pieces)
+    sent, residual, acc = refs[:count], refs[count : 2 * count], refs[-1]
+
+    def at(of, site):
+        piece = max(i for i in range(count) if pieces[i][0] <= site)
+        return of[piece][site - pieces[piece][0]]
+
     for s in range(PLANE):
         y, z = s // LZ, s % LZ
-        own = this[s]
+        here = lambda y, z: at(sent, plane * PLANE + y % LY * LZ + z)
+        own = here(y, z)
         around = jnp.concatenate(
-            [
-                own,
-                that[s],
-                this[(y + 1) % LY * LZ + z],
-                this[(y - 1) % LY * LZ + z],
-                this[y * LZ + 1 - z],
-                halo[s],
-            ],
+            [own, at(sent, (1 - plane) * PLANE + s), here(y + 1, z), here(y - 1, z), here(y, 1 - z), halo[s]],
             axis=1,
         )
         acc[s] = (
-            residual[s].astype(F32) - diagonal_shift * own.astype(F32) - times(around, weight[s])
+            at(residual, plane * PLANE + s).astype(F32)
+            - diagonal_shift * own.astype(F32)
+            - times(around, weight[s])
         )
 
 
 def time_kernel(piece, mode, scale, *refs):
-    acc, near, far, weight = refs[:4]
+    planes = planes_in(piece)
+    acc, weight = refs[: len(planes)], refs[len(planes) : 2 * len(planes)]
+    near, far, *refs = refs[2 * len(planes) :]
     if mode == "last":
         whole, out, sems = refs[-3:]
-        base = plane_of(piece) * PLANE
         copies = [
-            pltpu.make_async_copy(out.at[s], whole.at[0, base + s], sems.at[s]) for s in range(PLANE)
+            pltpu.make_async_copy(out.at[s], whole.at[0, place_of(site)], sems.at[s])
+            for s, site in enumerate(piece)
         ]
     else:
-        direction = refs[4]
-        out, direction_out, sent_out = refs[-3:]
-
-    for s in range(PLANE):
+        direction = refs[0]
+        out, direction_out, sent_out, *edges = refs[-3 - len(planes) :]
+    for s, site in enumerate(piece):
+        plane = planes.index(site // PLANE)
         around = jnp.concatenate([near[s], far[s]], axis=1)
-        now = acc[s] - times(around, weight[s])
+        now = acc[plane][site % PLANE] - times(around, weight[plane][site % PLANE])
         out[s] = now
         if mode == "last":
             copies[s].start()
@@ -201,15 +218,18 @@
     if mode == "last":
         for copy in copies:
             copy.wait()
-
-
-def sum_kernel(residual_a, residual_b, *refs):
-    out = refs[-1]
-    for piece, residual in enumerate((residual_a, residual_b)):
-        total = residual[...].astype(F32) * (half_width / center_value)
-        for ref in refs[piece:-1:2]:
-            total = total + ref[...]
-        out[0, plane_sites(piece)] = total
+    else:
+        store_edges(piece, sent_out, edges)
+
+
+def sum_kernel(pieces, *refs):
+    out, count = refs[-1], len(pieces)
+    for i, piece in enumerate(pieces):
+        for s, site in enumerate(piece):
+            total = refs[i][s].astype(F32) * (half_width / center_value)
+            for ref in refs[i + count : -1 : count]:
+                total = total + ref[s]
+            out[0, place_of(site)] = total
 
 
 def body(residual_in, self_block, hop_blocks):
@@ -222,73 +242,104 @@
     chips = [(i, (i - 1 + 2 * (i % 2)) % groups) for i in range(groups)]
 
     block = (count, width)
-    piece = lambda kind: pltpu.VMEM((PLANE,) + block, kind)
+    offsets = [-(-i * sites // PIECES) for i in range(PIECES + 1)]
+    pieces = [tuple(range(a, b)) for a, b in zip(offsets, offsets[1:])]
+    vector = lambda piece, kind: pltpu.VMEM((len(piece),) + block, kind)
+    edge = pltpu.VMEM((PLANE,) + block, BF16)
     whole = jax.ShapeDtypeStruct((1, sites) + block, F32)
-    flops = 2 * PLANE * count * width * width
+    flops = 2 * count * width * width
     scales = coefficients()
 
+    def with_edges(kernel, outs, operands, edges, flops, name, **more):
+        piece = kernel.args[0]
+        planes = planes_in(piece)
+        old = [p for p in planes if p in edges]
+        aliases = {len(operands) + i: len(outs) + planes.index(p) for i, p in enumerate(old)}
+        if "in_specs" in more:
+            more["in_specs"] = more["in_specs"] + [WHOLE] * len(old)
+        outs = call(
+            kernel,
+            outs + [edge] * len(planes),
+            operands + [edges[p] for p in old],
+            flops,
+            name,
+            aliases=aliases,
+            **more,
+        )
+        edges.update(zip(planes, outs[-len(planes) :]))
+        return outs[: -len(planes)]
+
     weight_local, weight_time = prep(self_block, hop_blocks, sites)
-    start, sent = zip(
-        *[
-            call(
-                functools.partial(first_kernel, i),
-                [piece(BF16), piece(BF16)],
-                [residual_in] + [weight_local[0]] * i,
-                0,
-                "first_direction",
-                in_specs=[IN_HBM] + [WHOLE] * i,
-                scratch=[pltpu.SemaphoreType.DMA((PLANE,))],
-            )
-            for i in range(2)
-        ]
-    )
+    start, sent, edges = [], [], {}
+    for i, piece in enumerate(pieces):
+        tie = [weight_local[0]] if i == 1 else []
+        outs = with_edges(
+            functools.partial(first_kernel, piece),
+            [vector(piece, BF16)] * 2,
+            [residual_in] + tie,
+            edges,
+            0,
+            "first_direction",
+            in_specs=[IN_HBM] + [WHOLE] * len(tie),
+            scratch=[pltpu.SemaphoreType.DMA((len(piece),))],
+        )
+        start.append(outs[0])
+        sent.append(outs[1])
     residual, direction = start, start
     directions = []
     for number in range(STEPS):
         first, last = number == 0, number == STEPS - 1
         near = [lax.ppermute(v, "site", swap) for v in sent]
-        halo = [lax.ppermute(sent[0], "group", chips), lax.ppermute(sent[1], "group", cores)]
+        halo = [lax.ppermute(edges[0], "group", chips), lax.ppermute(edges[1], "group", cores)]
         far = [lax.ppermute(v, "site", relay) for v in near]
         acc = [
             call(
-                local_kernel,
-                [piece(F32)],
-                [sent[i], sent[1 - i], halo[i], weight_local[i], residual[i]],
-                6 * flops,
+                functools.partial(local_kernel, plane, pieces),
+                [pltpu.VMEM((PLANE,) + block, F32)],
+                [halo[plane], weight_local[plane], *sent, *residual],
+                PLANE * 6 * flops,
                 "local_terms",
             )[0]
-            for i in range(2)
-        ]
-        operands = lambda i: [acc[i], near[i], far[i], weight_time[i]]
+            for plane in range(2)
+        ]
+        operands = lambda i: [
+            *[acc[p] for p in planes_in(pieces[i])],
+            *[weight_time[p] for p in planes_in(pieces[i])],
+            near[i],
+            far[i],
+        ]
         if last:
-            correction = call(sum_kernel, [whole], [*start, *sum(directions, ())], 0, "correction")[0]
+            correction = call(
+                functools.partial(sum_kernel, pieces), [whole], [*start, *sum(directions, [])], 0, "correction"
+            )[0]
             result = []
-            for i in range(2):
+            for i, piece in enumerate(pieces):
+                known = operands(i)
                 result = call(
-                    functools.partial(time_kernel, i, "last", None),
+                    functools.partial(time_kernel, piece, "last", None),
                     [whole],
-                    [*operands(i), *result],
-                    2 * flops,
+                    [*known, *result],
+                    len(piece) * 2 * flops,
                     "time_terms_last",
-                    aliases={4: 0} if result else None,
-                    in_specs=[WHOLE] * 4 + [IN_HBM] * len(result),
+                    aliases={len(known): 0} if result else None,
+                    in_specs=[WHOLE] * len(known) + [IN_HBM] * len(result),
                     out_specs=[IN_HBM],
-                    scratch=[piece(F32), pltpu.SemaphoreType.DMA((PLANE,))],
+                    scratch=[vector(piece, F32), pltpu.SemaphoreType.DMA((len(piece),))],
                 )
             return correction, result[0]
-        mode = "first" if first else "middle"
-        residual, direction, sent = zip(
-            *[
-                call(
-                    functools.partial(time_kernel, i, mode, scales[number]),
-                    [piece(F32), piece(F32), piece(BF16)],
-                    [*operands(i), direction[i]],
-                    2 * flops,
-                    "time_terms",
-                )
-                for i in range(2)
-            ]
-        )
+        edges = {}
+        new = [
+            with_edges(
+                functools.partial(time_kernel, piece, "first" if first else "middle", scales[number]),
+                [vector(piece, F32), vector(piece, F32), vector(piece, BF16)],
+                operands(i) + [direction[i]],
+                edges,
+                len(piece) * 2 * flops,
+                "time_terms",
+            )
+            for i, piece in enumerate(pieces)
+        ]
+        residual, direction, sent = map(list, zip(*new))
         directions.append(direction)
 
 

time: 81.2 us -> 78.2 us (0.963)
  waiting for transfers between devices: 47.6 us -> 38.1 us
  starting transfers between devices: 18.6 us -> 22.7 us
  Pallas kernels: 13.9 us -> 16.2 us
    ppermute x8 -> x12, starting transfers between devices: 8.42 us -> 16.3 us  [body(): near = [lax.ppermute(v, 'site', swap) for v in sent]]
    ppermute x8 -> x12, waiting for transfers between devices: 25.1 us -> 18.3 us  [body(): far = [lax.ppermute(v, 'site', relay) for v in near]]
    ppermute x8, starting transfers between devices: 6 us -> 2.35 us  [the longest x4 1.43 us: body(): lax.ppermute(edges[0], 'group', chips)]
    pallas_call x20 -> x25, Pallas kernels: 13.9 us -> 16.2 us  [call(): pl.pallas_call(kernel, out_shape=outs, in_specs=in_specs, out_specs=out_s...]
    ppermute x8 -> x12, waiting for transfers between devices: 21.5 us -> 19.7 us  [body(): near = [lax.ppermute(v, 'site', swap) for v in sent]]
    ppermute x8, waiting for transfers between devices: 0.94 us -> 0.06 us  [the longest x4 0.05 us: body(): lax.ppermute(edges[0], 'group', chips)]
    ppermute x8 -> x12, starting transfers between devices: 4.14 us -> 4.06 us  [body(): far = [lax.ppermute(v, 'site', relay) for v in near]]
  transfers between devices with their start and end apart: 24 -> 32, of which waited for: 18 -> 20; matrix products, arithmetic and copies ran while one was open for 0% -> 0% of each run, Pallas kernels for 15% -> 18%
where the time goes in v5:
time: 78.2 us; the launch traced here: 77.9 us
  waiting for transfers between devices  38.1 us (49%)
  starting transfers between devices  22.7 us (29%)
  Pallas kernels  16.2 us (21%)
  between operations  0.86 us (1%)
    ppermute x12, waiting for transfers between devices, body(): near = [lax.ppermute(v, 'site', swap) for v in sent]  19.7 us
    ppermute x12, waiting for transfers between devices, body(): far = [lax.ppermute(v, 'site', relay) for v in near]  18.3 us
    ppermute x12, starting transfers between devices, body(): near = [lax.ppermute(v, 'site', swap) for v in sent]  16.3 us
    pallas_call x25, Pallas kernels, call(): pl.pallas_call(kernel, out_shape=outs, in_specs=in_specs, out_specs=out_s...  16.2 us
    ppermute x12, starting transfers between devices, body(): far = [lax.ppermute(v, 'site', relay) for v in near]  4.06 us
  transfers between devices with their start and end apart: 32, of which 20 were waited for; matrix products, arithmetic and copies ran while one was open for 0% of the time, Pallas kernels for 18%

profile of v5, /device:TPU:0, one launch (start us, length us, event | category | flops | bytes accessed | tf_op | source)
XLA Modules:
  0.0 77.9 jit_solution(10258452185270867532)
XLA Ops:
  1.6 3.0 %collective-permute-start.1 = (bf16[6,128,128]{2,1,0:T(8,128)(2,1)S(1)}, bf16[6,128,128]{2,1,0:T(8,128)(2,1)S(1)}, u32[]{:S(2)}, u32[]{:S(2)}) collective-permute-start(bf16[6,128,128]{2,1,0:T(8,128)(2,1)S(1)} %get-tuple-element.62.refs_0_), channel_id=1, source_target_pairs={{0,1},{1,0},{2,3},{3,2},{4,5},{5,4},{6,7},{7,6},{8,9},{9,8},{10,11... | collective-permute-start | bytes 589832 | tf_op jit(solution)/shard_map/ppermute | solution.py:292
  4.6 2.4 %prep.1 = (bf16[8,128,768]{2,1,0:T(8,128)(2,1)S(1)}, bf16[8,128,768]{2,1,0:T(8,128)(2,1)S(1)}, bf16[8,128,256]{2,1,0:T(8,128)(2,1)S(1)}, bf16[8,128,256]{2,1,0:T(8,128)(2,1)S(1)}) custom-call(bf16[1,64,64,128]{3,2,1,0:T(8,128)(2,1)} %self_hbm.1, bf16[1,64,8,64,128]{4,3,2,1,0:T(8,128)(2,1)} %hop_hbm.1), custom_call_target="tpu_custom_call" | custom-call | bytes 9437184 | tf_op jit(solution)/shard_map/prep/pallas_call | solution.py:44
  9.5 1.8 %collective-permute-start.2 = (bf16[6,128,128]{2,1,0:T(8,128)(2,1)S(1)}, bf16[6,128,128]{2,1,0:T(8,128)(2,1)S(1)}, u32[]{:S(2)}, u32[]{:S(2)}) collective-permute-start(bf16[6,128,128]{2,1,0:T(8,128)(2,1)S(1)} %collective-permute-done.1.refs_2_), channel_id=1, source_target_pairs={{0,2},{1,7},{2,4},{3,1},{4,6},{5,3},{6,0},{7,5},{8,10},{9,15},{10,... | collective-permute-start | bytes 589832 | tf_op jit(solution)/shard_map/ppermute | solution.py:294
  12.3 3.6 %collective-permute-start.6 = (bf16[5,128,128]{2,1,0:T(8,128)(2,1)S(1)}, bf16[5,128,128]{2,1,0:T(8,128)(2,1)S(1)}, u32[]{:S(2)}, u32[]{:S(2)}) collective-permute-start(bf16[5,128,128]{2,1,0:T(8,128)(2,1)S(1)} %get-tuple-element.64.refs_2_), channel_id=1, source_target_pairs={{0,1},{1,0},{2,3},{3,2},{4,5},{5,4},{6,7},{7,6},{8,9},{9,8},{10,11... | collective-permute-start | bytes 491528 | tf_op jit(solution)/shard_map/ppermute | solution.py:292
  15.9 1.4 %collective-permute-start.5 = (bf16[5,128,128]{2,1,0:T(8,128)(2,1)S(1)}, bf16[5,128,128]{2,1,0:T(8,128)(2,1)S(1)}, u32[]{:S(2)}, u32[]{:S(2)}) collective-permute-start(bf16[5,128,128]{2,1,0:T(8,128)(2,1)S(1)} %collective-permute-done.4.refs_4_), channel_id=1, source_target_pairs={{0,2},{1,7},{2,4},{3,1},{4,6},{5,3},{6,0},{7,5},{8,10},{9,15},{10,... | collective-permute-start | bytes 491528 | tf_op jit(solution)/shard_map/ppermute | solution.py:294
  18.8 2.0 %collective-permute-start.9 = (bf16[6,128,128]{2,1,0:T(8,128)(2,1)S(1)}, bf16[6,128,128]{2,1,0:T(8,128)(2,1)S(1)}, u32[]{:S(2)}, u32[]{:S(2)}) collective-permute-start(bf16[6,128,128]{2,1,0:T(8,128)(2,1)S(1)} %get-tuple-element.75.refs_0_), channel_id=1, source_target_pairs={{0,1},{1,0},{2,3},{3,2},{4,5},{5,4},{6,7},{7,6},{8,9},{9,8},{10,11... | collective-permute-start | bytes 589832 | tf_op jit(solution)/shard_map/ppermute | solution.py:292
  21.4 2.6 %collective-permute-done.5.refs_5_ = bf16[5,128,128]{2,1,0:T(8,128)(2,1)S(1)} collective-permute-done((bf16[5,128,128]{2,1,0:T(8,128)(2,1)S(1)}, bf16[5,128,128]{2,1,0:T(8,128)(2,1)S(1)}, u32[]{:S(2)}, u32[]{:S(2)}) %collective-permute-start.5) | collective-permute-done | bytes 163872 | tf_op jit(solution)/shard_map/ppermute | solution.py:294
  26.4 2.0 %collective-permute-done.7.refs_3_ = bf16[5,128,128]{2,1,0:T(8,128)(2,1)S(1)} collective-permute-done((bf16[5,128,128]{2,1,0:T(8,128)(2,1)S(1)}, bf16[5,128,128]{2,1,0:T(8,128)(2,1)S(1)}, u32[]{:S(2)}, u32[]{:S(2)}) %collective-permute-start.7) | collective-permute-done | bytes 163872 | tf_op jit(solution)/shard_map/ppermute | solution.py:294
  28.7 1.6 %collective-permute-start.14 = (bf16[5,128,128]{2,1,0:T(8,128)(2,1)S(1)}, bf16[5,128,128]{2,1,0:T(8,128)(2,1)S(1)}, u32[]{:S(2)}, u32[]{:S(2)}) collective-permute-start(bf16[5,128,128]{2,1,0:T(8,128)(2,1)S(1)} %get-tuple-element.77.refs_2_), channel_id=1, source_target_pairs={{0,1},{1,0},{2,3},{3,2},{4,5},{5,4},{6,7},{7,6},{8,9},{9,8},{10,11... | collective-permute-start | bytes 491528 | tf_op jit(solution)/shard_map/ppermute | solution.py:292
  30.3 1.3 %collective-permute-done.12.refs_4_ = bf16[5,128,128]{2,1,0:T(8,128)(2,1)S(1)} collective-permute-done((bf16[5,128,128]{2,1,0:T(8,128)(2,1)S(1)}, bf16[5,128,128]{2,1,0:T(8,128)(2,1)S(1)}, u32[]{:S(2)}, u32[]{:S(2)}) %collective-permute-start.12) | collective-permute-done | bytes 163872 | tf_op jit(solution)/shard_map/ppermute | solution.py:292
  31.6 3.7 %collective-permute-done.14.refs_2_ = bf16[5,128,128]{2,1,0:T(8,128)(2,1)S(1)} collective-permute-done((bf16[5,128,128]{2,1,0:T(8,128)(2,1)S(1)}, bf16[5,128,128]{2,1,0:T(8,128)(2,1)S(1)}, u32[]{:S(2)}, u32[]{:S(2)}) %collective-permute-start.14) | collective-permute-done | bytes 163872 | tf_op jit(solution)/shard_map/ppermute | solution.py:292
  36.2 2.9 %collective-permute-start.17 = (bf16[6,128,128]{2,1,0:T(8,128)(2,1)S(1)}, bf16[6,128,128]{2,1,0:T(8,128)(2,1)S(1)}, u32[]{:S(2)}, u32[]{:S(2)}) collective-permute-start(bf16[6,128,128]{2,1,0:T(8,128)(2,1)S(1)} %get-tuple-element.88.refs_0_), channel_id=1, source_target_pairs={{0,1},{1,0},{2,3},{3,2},{4,5},{5,4},{6,7},{7,6},{8,9},{9,8},{10,11... | collective-permute-start | bytes 589832 | tf_op jit(solution)/shard_map/ppermute | solution.py:292
  40.8 2.5 %collective-permute-done.15.refs_3_ = bf16[5,128,128]{2,1,0:T(8,128)(2,1)S(1)} collective-permute-done((bf16[5,128,128]{2,1,0:T(8,128)(2,1)S(1)}, bf16[5,128,128]{2,1,0:T(8,128)(2,1)S(1)}, u32[]{:S(2)}, u32[]{:S(2)}) %collective-permute-start.15) | collective-permute-done | bytes 163872 | tf_op jit(solution)/shard_map/ppermute | solution.py:294
  43.8 4.1 %collective-permute-done.20.refs_4_ = bf16[5,128,128]{2,1,0:T(8,128)(2,1)S(1)} collective-permute-done((bf16[5,128,128]{2,1,0:T(8,128)(2,1)S(1)}, bf16[5,128,128]{2,1,0:T(8,128)(2,1)S(1)}, u32[]{:S(2)}, u32[]{:S(2)}) %collective-permute-start.20) | collective-permute-done | bytes 163872 | tf_op jit(solution)/shard_map/ppermute | solution.py:292
  47.9 3.4 %collective-permute-done.22.refs_2_ = bf16[5,128,128]{2,1,0:T(8,128)(2,1)S(1)} collective-permute-done((bf16[5,128,128]{2,1,0:T(8,128)(2,1)S(1)}, bf16[5,128,128]{2,1,0:T(8,128)(2,1)S(1)}, u32[]{:S(2)}, u32[]{:S(2)}) %collective-permute-start.22) | collective-permute-done | bytes 163872 | tf_op jit(solution)/shard_map/ppermute | solution.py:292
  51.9 1.4 %collective-permute-done.18.refs_3_ = bf16[6,128,128]{2,1,0:T(8,128)(2,1)S(1)} collective-permute-done((bf16[6,128,128]{2,1,0:T(8,128)(2,1)S(1)}, bf16[6,128,128]{2,1,0:T(8,128)(2,1)S(1)}, u32[]{:S(2)}, u32[]{:S(2)}) %collective-permute-start.18) | collective-permute-done | bytes 196640 | tf_op jit(solution)/shard_map/ppermute | solution.py:294
  53.6 1.9 %collective-permute-start.30 = (bf16[6,128,128]{2,1,0:T(8,128)(2,1)S(1)}, bf16[6,128,128]{2,1,0:T(8,128)(2,1)S(1)}, u32[]{:S(2)}, u32[]{:S(2)}) collective-permute-start(bf16[6,128,128]{2,1,0:T(8,128)(2,1)S(1)} %get-tuple-element.101.refs_0_), channel_id=1, source_target_pairs={{0,1},{1,0},{2,3},{3,2},{4,5},{5,4},{6,7},{7,6},{8,9},{9,8},{10,11... | collective-permute-start | bytes 589832 | tf_op jit(solution)/shard_map/ppermute | solution.py:292
  57.3 2.6 %collective-permute-done.23.refs_3_ = bf16[5,128,128]{2,1,0:T(8,128)(2,1)S(1)} collective-permute-done((bf16[5,128,128]{2,1,0:T(8,128)(2,1)S(1)}, bf16[5,128,128]{2,1,0:T(8,128)(2,1)S(1)}, u32[]{:S(2)}, u32[]{:S(2)}) %collective-permute-start.23) | collective-permute-done | bytes 163872 | tf_op jit(solution)/shard_map/ppermute | solution.py:294
  61.5 3.5 %collective-permute-done.28.refs_4_ = bf16[5,128,128]{2,1,0:T(8,128)(2,1)S(1)} collective-permute-done((bf16[5,128,128]{2,1,0:T(8,128)(2,1)S(1)}, bf16[5,128,128]{2,1,0:T(8,128)(2,1)S(1)}, u32[]{:S(2)}, u32[]{:S(2)}) %collective-permute-start.28) | collective-permute-done | bytes 163872 | tf_op jit(solution)/shard_map/ppermute | solution.py:292
  65.0 2.5 %collective-permute-done.25.refs_2_ = bf16[5,128,128]{2,1,0:T(8,128)(2,1)S(1)} collective-permute-done((bf16[5,128,128]{2,1,0:T(8,128)(2,1)S(1)}, bf16[5,128,128]{2,1,0:T(8,128)(2,1)S(1)}, u32[]{:S(2)}, u32[]{:S(2)}) %collective-permute-start.25) | collective-permute-done | bytes 163872 | tf_op jit(solution)/shard_map/ppermute | solution.py:292
  67.5 1.2 %correction.1 = f32[1,16,128,128]{3,2,1,0:T(8,128)} custom-call(bf16[6,128,128]{2,1,0:T(8,128)(2,1)S(1)} %get-tuple-element.55.refs_3_.refs_4_.refs_0_, bf16[5,128,128]{2,1,0:T(8,128)(2,1)S(1)} %get-tuple-element.58.refs_4_.refs_6_.refs_1_, bf16[5,128,128]{2,1,0:T(8,128)(2,1)S(1)} %get-tuple-element.60.refs_5_.refs_4_.refs_2_, ...), custom_call_target="tpu_custom_call" | custom-call | bytes 3670016 | tf_op jit(solution)/shard_map/correction/pallas_call | solution.py:44
  69.9 1.2 %collective-permute-done.31.refs_3_ = bf16[6,128,128]{2,1,0:T(8,128)(2,1)S(1)} collective-permute-done((bf16[6,128,128]{2,1,0:T(8,128)(2,1)S(1)}, bf16[6,128,128]{2,1,0:T(8,128)(2,1)S(1)}, u32[]{:S(2)}, u32[]{:S(2)}) %collective-permute-start.31) | collective-permute-done | bytes 196640 | tf_op jit(solution)/shard_map/ppermute | solution.py:294
  72.0 2.5 %collective-permute-done.29.refs_5_ = bf16[5,128,128]{2,1,0:T(8,128)(2,1)S(1)} collective-permute-done((bf16[5,128,128]{2,1,0:T(8,128)(2,1)S(1)}, bf16[5,128,128]{2,1,0:T(8,128)(2,1)S(1)}, u32[]{:S(2)}, u32[]{:S(2)}) %collective-permute-start.29) | collective-permute-done | bytes 163872 | tf_op jit(solution)/shard_map/ppermute | solution.py:294
  75.5 1.4 %collective-permute-done.26.refs_3_ = bf16[5,128,128]{2,1,0:T(8,128)(2,1)S(1)} collective-permute-done((bf16[5,128,128]{2,1,0:T(8,128)(2,1)S(1)}, bf16[5,128,128]{2,1,0:T(8,128)(2,1)S(1)}, u32[]{:S(2)}, u32[]{:S(2)}) %collective-permute-start.26) | collective-permute-done | bytes 163872 | tf_op jit(solution)/shard_map/ppermute | solution.py:294
  (65 shorter events, 20.5 us)
Async XLA Ops:
  1.6 7.9 %collective-permute-start.1 = (bf16[6,128,128]{2,1,0:T(8,128)(2,1)S(1)}, bf16[6,128,128]{2,1,0:T(8,128)(2,1)S(1)}, u32[]{:S(2)}, u32[]{:S(2)}) collective-permute-start(bf16[6,128,128]{2,1,0:T(8,128)(2,1)S(1)} %get-tuple-element.62.refs_0_), channel_id=1, source_target_pairs={{0,1},{1,0},{2,3},{3,2},{4,5},{5,4},{6,7},{7,6},{8,9},{9,8},{10,11... | collective-permute-start | bytes 589832 | tf_op jit(solution)/shard_map/ppermute | solution.py:292
  7.9 9.4 %collective-permute-start = (bf16[8,128,128]{2,1,0:T(8,128)(2,1)S(1)}, bf16[8,128,128]{2,1,0:T(8,128)(2,1)S(1)}, u32[]{:S(2)}, u32[]{:S(2)}) collective-permute-start(bf16[8,128,128]{2,1,0:T(8,128)(2,1)S(1)} %get-tuple-element.61), channel_id=1, source_target_pairs={{0,24},{8,16},{16,8},{24,0},{1,25},{9,17},{17,9},{25,1},{2,26},{10... | collective-permute-start | bytes 786440 | tf_op jit(solution)/shard_map/ppermute | solution.py:293
  9.5 9.0 %collective-permute-start.2 = (bf16[6,128,128]{2,1,0:T(8,128)(2,1)S(1)}, bf16[6,128,128]{2,1,0:T(8,128)(2,1)S(1)}, u32[]{:S(2)}, u32[]{:S(2)}) collective-permute-start(bf16[6,128,128]{2,1,0:T(8,128)(2,1)S(1)} %collective-permute-done.1.refs_2_), channel_id=1, source_target_pairs={{0,2},{1,7},{2,4},{3,1},{4,6},{5,3},{6,0},{7,5},{8,10},{9,15},{10,... | collective-permute-start | bytes 589832 | tf_op jit(solution)/shard_map/ppermute | solution.py:294
  12.2 8.6 %collective-permute-start.3 = (bf16[8,128,128]{2,1,0:T(8,128)(2,1)S(1)}, bf16[8,128,128]{2,1,0:T(8,128)(2,1)S(1)}, u32[]{:S(2)}, u32[]{:S(2)}) collective-permute-start(bf16[8,128,128]{2,1,0:T(8,128)(2,1)S(1)} %get-tuple-element.67), channel_id=1, source_target_pairs={{0,8},{8,0},{16,24},{24,16},{1,9},{9,1},{17,25},{25,17},{2,10},{10... | collective-permute-start | bytes 786440 | tf_op jit(solution)/shard_map/ppermute | solution.py:293
  12.3 8.5 %collective-permute-start.6 = (bf16[5,128,128]{2,1,0:T(8,128)(2,1)S(1)}, bf16[5,128,128]{2,1,0:T(8,128)(2,1)S(1)}, u32[]{:S(2)}, u32[]{:S(2)}) collective-permute-start(bf16[5,128,128]{2,1,0:T(8,128)(2,1)S(1)} %get-tuple-element.64.refs_2_), channel_id=1, source_target_pairs={{0,1},{1,0},{2,3},{3,2},{4,5},{5,4},{6,7},{7,6},{8,9},{9,8},{10,11... | collective-permute-start | bytes 491528 | tf_op jit(solution)/shard_map/ppermute | solution.py:292
  15.9 8.1 %collective-permute-start.5 = (bf16[5,128,128]{2,1,0:T(8,128)(2,1)S(1)}, bf16[5,128,128]{2,1,0:T(8,128)(2,1)S(1)}, u32[]{:S(2)}, u32[]{:S(2)}) collective-permute-start(bf16[5,128,128]{2,1,0:T(8,128)(2,1)S(1)} %collective-permute-done.4.refs_4_), channel_id=1, source_target_pairs={{0,2},{1,7},{2,4},{3,1},{4,6},{5,3},{6,0},{7,5},{8,10},{9,15},{10,... | collective-permute-start | bytes 491528 | tf_op jit(solution)/shard_map/ppermute | solution.py:294
  24.2 11.1 %collective-permute-start.8 = (bf16[8,128,128]{2,1,0:T(8,128)(2,1)S(1)}, bf16[8,128,128]{2,1,0:T(8,128)(2,1)S(1)}, u32[]{:S(2)}, u32[]{:S(2)}) collective-permute-start(bf16[8,128,128]{2,1,0:T(8,128)(2,1)S(1)} %get-tuple-element.74), channel_id=1, source_target_pairs={{0,24},{8,16},{16,8},{24,0},{1,25},{9,17},{17,9},{25,1},{2,26},{10... | collective-permute-start | bytes 786440 | tf_op jit(solution)/shard_map/ppermute | solution.py:293
  25.6 10.3 %collective-permute-start.10 = (bf16[6,128,128]{2,1,0:T(8,128)(2,1)S(1)}, bf16[6,128,128]{2,1,0:T(8,128)(2,1)S(1)}, u32[]{:S(2)}, u32[]{:S(2)}) collective-permute-start(bf16[6,128,128]{2,1,0:T(8,128)(2,1)S(1)} %collective-permute-done.9.refs_2_), channel_id=1, source_target_pairs={{0,2},{1,7},{2,4},{3,1},{4,6},{5,3},{6,0},{7,5},{8,10},{9,15},{10,... | collective-permute-start | bytes 589832 | tf_op jit(solution)/shard_map/ppermute | solution.py:294
  30.3 8.8 %collective-permute-start.11 = (bf16[8,128,128]{2,1,0:T(8,128)(2,1)S(1)}, bf16[8,128,128]{2,1,0:T(8,128)(2,1)S(1)}, u32[]{:S(2)}, u32[]{:S(2)}) collective-permute-start(bf16[8,128,128]{2,1,0:T(8,128)(2,1)S(1)} %get-tuple-element.82), channel_id=1, source_target_pairs={{0,8},{8,0},{16,24},{24,16},{1,9},{9,1},{17,25},{25,17},{2,10},{10... | collective-permute-start | bytes 786440 | tf_op jit(solution)/shard_map/ppermute | solution.py:293
  31.6 8.8 %collective-permute-start.13 = (bf16[5,128,128]{2,1,0:T(8,128)(2,1)S(1)}, bf16[5,128,128]{2,1,0:T(8,128)(2,1)S(1)}, u32[]{:S(2)}, u32[]{:S(2)}) collective-permute-start(bf16[5,128,128]{2,1,0:T(8,128)(2,1)S(1)} %collective-permute-done.12.refs_4_), channel_id=1, source_target_pairs={{0,2},{1,7},{2,4},{3,1},{4,6},{5,3},{6,0},{7,5},{8,10},{9,15},{10,... | collective-permute-start | bytes 491528 | tf_op jit(solution)/shard_map/ppermute | solution.py:294
  35.3 8.0 %collective-permute-start.15 = (bf16[5,128,128]{2,1,0:T(8,128)(2,1)S(1)}, bf16[5,128,128]{2,1,0:T(8,128)(2,1)S(1)}, u32[]{:S(2)}, u32[]{:S(2)}) collective-permute-start(bf16[5,128,128]{2,1,0:T(8,128)(2,1)S(1)} %collective-permute-done.14.refs_2_), channel_id=1, source_target_pairs={{0,2},{1,7},{2,4},{3,1},{4,6},{5,3},{6,0},{7,5},{8,10},{9,15},{10,... | collective-permute-start | bytes 491528 | tf_op jit(solution)/shard_map/ppermute | solution.py:294
  40.7 10.7 %collective-permute-start.16 = (bf16[8,128,128]{2,1,0:T(8,128)(2,1)S(1)}, bf16[8,128,128]{2,1,0:T(8,128)(2,1)S(1)}, u32[]{:S(2)}, u32[]{:S(2)}) collective-permute-start(bf16[8,128,128]{2,1,0:T(8,128)(2,1)S(1)} %get-tuple-element.87), channel_id=1, source_target_pairs={{0,24},{8,16},{16,8},{24,0},{1,25},{9,17},{17,9},{25,1},{2,26},{10... | collective-permute-start | bytes 786440 | tf_op jit(solution)/shard_map/ppermute | solution.py:293
  43.6 7.7 %collective-permute-start.22 = (bf16[5,128,128]{2,1,0:T(8,128)(2,1)S(1)}, bf16[5,128,128]{2,1,0:T(8,128)(2,1)S(1)}, u32[]{:S(2)}, u32[]{:S(2)}) collective-permute-start(bf16[5,128,128]{2,1,0:T(8,128)(2,1)S(1)} %get-tuple-element.90.refs_2_), channel_id=1, source_target_pairs={{0,1},{1,0},{2,3},{3,2},{4,5},{5,4},{6,7},{7,6},{8,9},{9,8},{10,11... | collective-permute-start | bytes 491528 | tf_op jit(solution)/shard_map/ppermute | solution.py:292
  43.7 11.9 %collective-permute-start.19 = (bf16[8,128,128]{2,1,0:T(8,128)(2,1)S(1)}, bf16[8,128,128]{2,1,0:T(8,128)(2,1)S(1)}, u32[]{:S(2)}, u32[]{:S(2)}) collective-permute-start(bf16[8,128,128]{2,1,0:T(8,128)(2,1)S(1)} %get-tuple-element.95), channel_id=1, source_target_pairs={{0,8},{8,0},{16,24},{24,16},{1,9},{9,1},{17,25},{25,17},{2,10},{10... | collective-permute-start | bytes 786440 | tf_op jit(solution)/shard_map/ppermute | solution.py:293
  43.8 9.6 %collective-permute-start.18 = (bf16[6,128,128]{2,1,0:T(8,128)(2,1)S(1)}, bf16[6,128,128]{2,1,0:T(8,128)(2,1)S(1)}, u32[]{:S(2)}, u32[]{:S(2)}) collective-permute-start(bf16[6,128,128]{2,1,0:T(8,128)(2,1)S(1)} %collective-permute-done.17.refs_2_), channel_id=1, source_target_pairs={{0,2},{1,7},{2,4},{3,1},{4,6},{5,3},{6,0},{7,5},{8,10},{9,15},{10,... | collective-permute-start | bytes 589832 | tf_op jit(solution)/shard_map/ppermute | solution.py:294
  47.9 8.9 %collective-permute-start.21 = (bf16[5,128,128]{2,1,0:T(8,128)(2,1)S(1)}, bf16[5,128,128]{2,1,0:T(8,128)(2,1)S(1)}, u32[]{:S(2)}, u32[]{:S(2)}) collective-permute-start(bf16[5,128,128]{2,1,0:T(8,128)(2,1)S(1)} %collective-permute-done.20.refs_4_), channel_id=1, source_target_pairs={{0,2},{1,7},{2,4},{3,1},{4,6},{5,3},{6,0},{7,5},{8,10},{9,15},{10,... | collective-permute-start | bytes 491528 | tf_op jit(solution)/shard_map/ppermute | solution.py:294
  51.3 8.5 %collective-permute-start.23 = (bf16[5,128,128]{2,1,0:T(8,128)(2,1)S(1)}, bf16[5,128,128]{2,1,0:T(8,128)(2,1)S(1)}, u32[]{:S(2)}, u32[]{:S(2)}) collective-permute-start(bf16[5,128,128]{2,1,0:T(8,128)(2,1)S(1)} %collective-permute-done.22.refs_2_), channel_id=1, source_target_pairs={{0,2},{1,7},{2,4},{3,1},{4,6},{5,3},{6,0},{7,5},{8,10},{9,15},{10,... | collective-permute-start | bytes 491528 | tf_op jit(solution)/shard_map/ppermute | solution.py:294
  53.6 7.8 %collective-permute-start.30 = (bf16[6,128,128]{2,1,0:T(8,128)(2,1)S(1)}, bf16[6,128,128]{2,1,0:T(8,128)(2,1)S(1)}, u32[]{:S(2)}, u32[]{:S(2)}) collective-permute-start(bf16[6,128,128]{2,1,0:T(8,128)(2,1)S(1)} %get-tuple-element.101.refs_0_), channel_id=1, source_target_pairs={{0,1},{1,0},{2,3},{3,2},{4,5},{5,4},{6,7},{7,6},{8,9},{9,8},{10,11... | collective-permute-start | bytes 589832 | tf_op jit(solution)/shard_map/ppermute | solution.py:292
  57.1 7.9 %collective-permute-start.28 = (bf16[5,128,128]{2,1,0:T(8,128)(2,1)S(1)}, bf16[5,128,128]{2,1,0:T(8,128)(2,1)S(1)}, u32[]{:S(2)}, u32[]{:S(2)}) collective-permute-start(bf16[5,128,128]{2,1,0:T(8,128)(2,1)S(1)} %get-tuple-element.102.refs_1_), channel_id=1, source_target_pairs={{0,1},{1,0},{2,3},{3,2},{4,5},{5,4},{6,7},{7,6},{8,9},{9,8},{10,11... | collective-permute-start | bytes 491528 | tf_op jit(solution)/shard_map/ppermute | solution.py:292
  60.4 8.4 %collective-permute-start.27 = (bf16[8,128,128]{2,1,0:T(8,128)(2,1)S(1)}, bf16[8,128,128]{2,1,0:T(8,128)(2,1)S(1)}, u32[]{:S(2)}, u32[]{:S(2)}) collective-permute-start(bf16[8,128,128]{2,1,0:T(8,128)(2,1)S(1)} %get-tuple-element.107), channel_id=1, source_target_pairs={{0,24},{8,16},{16,8},{24,0},{1,25},{9,17},{17,9},{25,1},{2,26},{10... | collective-permute-start | bytes 786440 | tf_op jit(solution)/shard_map/ppermute | solution.py:293
  60.5 8.8 %collective-permute-start.24 = (bf16[8,128,128]{2,1,0:T(8,128)(2,1)S(1)}, bf16[8,128,128]{2,1,0:T(8,128)(2,1)S(1)}, u32[]{:S(2)}, u32[]{:S(2)}) collective-permute-start(bf16[8,128,128]{2,1,0:T(8,128)(2,1)S(1)} %get-tuple-element.100), channel_id=1, source_target_pairs={{0,8},{8,0},{16,24},{24,16},{1,9},{9,1},{17,25},{25,17},{2,10},{10... | collective-permute-start | bytes 786440 | tf_op jit(solution)/shard_map/ppermute | solution.py:293
  61.5 9.6 %collective-permute-start.31 = (bf16[6,128,128]{2,1,0:T(8,128)(2,1)S(1)}, bf16[6,128,128]{2,1,0:T(8,128)(2,1)S(1)}, u32[]{:S(2)}, u32[]{:S(2)}) collective-permute-start(bf16[6,128,128]{2,1,0:T(8,128)(2,1)S(1)} %collective-permute-done.30.refs_2_), channel_id=1, source_target_pairs={{0,2},{1,7},{2,4},{3,1},{4,6},{5,3},{6,0},{7,5},{8,10},{9,15},{10,... | collective-permute-start | bytes 589832 | tf_op jit(solution)/shard_map/ppermute | solution.py:294
  65.0 9.6 %collective-permute-start.29 = (bf16[5,128,128]{2,1,0:T(8,128)(2,1)S(1)}, bf16[5,128,128]{2,1,0:T(8,128)(2,1)S(1)}, u32[]{:S(2)}, u32[]{:S(2)}) collective-permute-start(bf16[5,128,128]{2,1,0:T(8,128)(2,1)S(1)} %collective-permute-done.28.refs_4_), channel_id=1, source_target_pairs={{0,2},{1,7},{2,4},{3,1},{4,6},{5,3},{6,0},{7,5},{8,10},{9,15},{10,... | collective-permute-start | bytes 491528 | tf_op jit(solution)/shard_map/ppermute | solution.py:294
  67.5 9.4 %collective-permute-start.26 = (bf16[5,128,128]{2,1,0:T(8,128)(2,1)S(1)}, bf16[5,128,128]{2,1,0:T(8,128)(2,1)S(1)}, u32[]{:S(2)}, u32[]{:S(2)}) collective-permute-start(bf16[5,128,128]{2,1,0:T(8,128)(2,1)S(1)} %collective-permute-done.25.refs_2_), channel_id=1, source_target_pairs={{0,2},{1,7},{2,4},{3,1},{4,6},{5,3},{6,0},{7,5},{8,10},{9,15},{10,... | collective-permute-start | bytes 491528 | tf_op jit(solution)/shard_map/ppermute | solution.py:294
  (8 other events, 57.3 us)

commit v6 on v5

--- a/solution.py
+++ b/solution.py
@@ -222,6 +222,10 @@
         store_edges(piece, sent_out, edges)
 
 
+def pass_kernel(*refs):
+    pass
+
+
 def sum_kernel(pieces, *refs):
     out, count = refs[-1], len(pieces)
     for i, piece in enumerate(pieces):
@@ -291,6 +295,19 @@
         first, last = number == 0, number == STEPS - 1
         near = [lax.ppermute(v, "site", swap) for v in sent]
         halo = [lax.ppermute(edges[0], "group", chips), lax.ppermute(edges[1], "group", cores)]
+        if last:
+            correction = call(
+                functools.partial(sum_kernel, pieces), [whole], [*start, *sum(directions, [])], 0, "correction"
+            )[0]
+            near[1] = call(
+                pass_kernel,
+                [vector(pieces[1], BF16)],
+                [near[1], correction],
+                0,
+                "order",
+                aliases={0: 0},
+                in_specs=[WHOLE, IN_HBM],
+            )[0]
         far = [lax.ppermute(v, "site", relay) for v in near]
         acc = [
             call(
@@ -309,9 +326,6 @@
             far[i],
         ]
         if last:
-            correction = call(
-                functools.partial(sum_kernel, pieces), [whole], [*start, *sum(directions, [])], 0, "correction"
-            )[0]
             result = []
             for i, piece in enumerate(pieces):
                 known = operands(i)

time: 78.2 us -> 78.2 us (level)
    ppermute x12, waiting for transfers between devices: 19.7 us -> 18.6 us  [body(): near = [lax.ppermute(v, 'site', swap) for v in sent]]
    ppermute x4, waiting for transfers between devices: 0.05 us -> 1.21 us  [body(): lax.ppermute(edges[0], 'group', chips)]
    pallas_call x25 -> x26, Pallas kernels: 16.2 us -> 16.2 us  [call(): pl.pallas_call(kernel, out_shape=outs, in_specs=in_specs, out_specs=out_s...]
  transfers between devices with their start and end apart: 32 -> 32, of which waited for: 20 -> 21; matrix products, arithmetic and copies ran while one was open for 0% -> 0% of each run, Pallas kernels for 18% -> 18%
where the time goes in v6:
time: 78.2 us; the launch traced here: 77.9 us
  waiting for transfers between devices  38.1 us (49%)
  starting transfers between devices  22.7 us (29%)
  Pallas kernels  16.2 us (21%)
  between operations  0.86 us (1%)
    ppermute x12, waiting for transfers between devices, body(): near = [lax.ppermute(v, 'site', swap) for v in sent]  18.6 us
    ppermute x12, waiting for transfers between devices, body(): far = [lax.ppermute(v, 'site', relay) for v in near]  18.3 us
    ppermute x12, starting transfers between devices, body(): near = [lax.ppermute(v, 'site', swap) for v in sent]  16.3 us
    pallas_call x26, Pallas kernels, call(): pl.pallas_call(kernel, out_shape=outs, in_specs=in_specs, out_specs=out_s...  16.2 us
    ppermute x12, starting transfers between devices, body(): far = [lax.ppermute(v, 'site', relay) for v in near]  4.06 us
  transfers between devices with their start and end apart: 32, of which 21 were waited for; matrix products, arithmetic and copies ran while one was open for 0% of the time, Pallas kernels for 18%

profile of v6, /device:TPU:0, one launch (start us, length us, event | category | flops | bytes accessed | tf_op | source)
XLA Modules:
  0.0 77.9 jit_solution(1719640369111035562)
XLA Ops:
  1.6 3.0 %collective-permute-start.1 = (bf16[6,128,128]{2,1,0:T(8,128)(2,1)S(1)}, bf16[6,128,128]{2,1,0:T(8,128)(2,1)S(1)}, u32[]{:S(2)}, u32[]{:S(2)}) collective-permute-start(bf16[6,128,128]{2,1,0:T(8,128)(2,1)S(1)} %get-tuple-element.62.refs_0_), channel_id=1, source_target_pairs={{0,1},{1,0},{2,3},{3,2},{4,5},{5,4},{6,7},{7,6},{8,9},{9,8},{10,11... | collective-permute-start | bytes 589832 | tf_op jit(solution)/shard_map/ppermute | solution.py:296
  4.6 2.4 %prep.1 = (bf16[8,128,768]{2,1,0:T(8,128)(2,1)S(1)}, bf16[8,128,768]{2,1,0:T(8,128)(2,1)S(1)}, bf16[8,128,256]{2,1,0:T(8,128)(2,1)S(1)}, bf16[8,128,256]{2,1,0:T(8,128)(2,1)S(1)}) custom-call(bf16[1,64,64,128]{3,2,1,0:T(8,128)(2,1)} %self_hbm.1, bf16[1,64,8,64,128]{4,3,2,1,0:T(8,128)(2,1)} %hop_hbm.1), custom_call_target="tpu_custom_call" | custom-call | bytes 9437184 | tf_op jit(solution)/shard_map/prep/pallas_call | solution.py:44
  9.5 1.8 %collective-permute-start.2 = (bf16[6,128,128]{2,1,0:T(8,128)(2,1)S(1)}, bf16[6,128,128]{2,1,0:T(8,128)(2,1)S(1)}, u32[]{:S(2)}, u32[]{:S(2)}) collective-permute-start(bf16[6,128,128]{2,1,0:T(8,128)(2,1)S(1)} %collective-permute-done.1.refs_2_), channel_id=1, source_target_pairs={{0,2},{1,7},{2,4},{3,1},{4,6},{5,3},{6,0},{7,5},{8,10},{9,15},{10,... | collective-permute-start | bytes 589832 | tf_op jit(solution)/shard_map/ppermute | solution.py:311
  12.3 3.6 %collective-permute-start.6 = (bf16[5,128,128]{2,1,0:T(8,128)(2,1)S(1)}, bf16[5,128,128]{2,1,0:T(8,128)(2,1)S(1)}, u32[]{:S(2)}, u32[]{:S(2)}) collective-permute-start(bf16[5,128,128]{2,1,0:T(8,128)(2,1)S(1)} %get-tuple-element.64.refs_2_), channel_id=1, source_target_pairs={{0,1},{1,0},{2,3},{3,2},{4,5},{5,4},{6,7},{7,6},{8,9},{9,8},{10,11... | collective-permute-start | bytes 491528 | tf_op jit(solution)/shard_map/ppermute | solution.py:296
  15.9 1.4 %collective-permute-start.5 = (bf16[5,128,128]{2,1,0:T(8,128)(2,1)S(1)}, bf16[5,128,128]{2,1,0:T(8,128)(2,1)S(1)}, u32[]{:S(2)}, u32[]{:S(2)}) collective-permute-start(bf16[5,128,128]{2,1,0:T(8,128)(2,1)S(1)} %collective-permute-done.4.refs_4_), channel_id=1, source_target_pairs={{0,2},{1,7},{2,4},{3,1},{4,6},{5,3},{6,0},{7,5},{8,10},{9,15},{10,... | collective-permute-start | bytes 491528 | tf_op jit(solution)/shard_map/ppermute | solution.py:311
  18.8 2.0 %collective-permute-start.9 = (bf16[6,128,128]{2,1,0:T(8,128)(2,1)S(1)}, bf16[6,128,128]{2,1,0:T(8,128)(2,1)S(1)}, u32[]{:S(2)}, u32[]{:S(2)}) collective-permute-start(bf16[6,128,128]{2,1,0:T(8,128)(2,1)S(1)} %get-tuple-element.75.refs_0_), channel_id=1, source_target_pairs={{0,1},{1,0},{2,3},{3,2},{4,5},{5,4},{6,7},{7,6},{8,9},{9,8},{10,11... | collective-permute-start | bytes 589832 | tf_op jit(solution)/shard_map/ppermute | solution.py:296
  21.4 2.6 %collective-permute-done.5.refs_5_ = bf16[5,128,128]{2,1,0:T(8,128)(2,1)S(1)} collective-permute-done((bf16[5,128,128]{2,1,0:T(8,128)(2,1)S(1)}, bf16[5,128,128]{2,1,0:T(8,128)(2,1)S(1)}, u32[]{:S(2)}, u32[]{:S(2)}) %collective-permute-start.5) | collective-permute-done | bytes 163872 | tf_op jit(solution)/shard_map/ppermute | solution.py:311
  26.4 2.0 %collective-permute-done.7.refs_3_ = bf16[5,128,128]{2,1,0:T(8,128)(2,1)S(1)} collective-permute-done((bf16[5,128,128]{2,1,0:T(8,128)(2,1)S(1)}, bf16[5,128,128]{2,1,0:T(8,128)(2,1)S(1)}, u32[]{:S(2)}, u32[]{:S(2)}) %collective-permute-start.7) | collective-permute-done | bytes 163872 | tf_op jit(solution)/shard_map/ppermute | solution.py:311
  28.7 1.6 %collective-permute-start.14 = (bf16[5,128,128]{2,1,0:T(8,128)(2,1)S(1)}, bf16[5,128,128]{2,1,0:T(8,128)(2,1)S(1)}, u32[]{:S(2)}, u32[]{:S(2)}) collective-permute-start(bf16[5,128,128]{2,1,0:T(8,128)(2,1)S(1)} %get-tuple-element.77.refs_2_), channel_id=1, source_target_pairs={{0,1},{1,0},{2,3},{3,2},{4,5},{5,4},{6,7},{7,6},{8,9},{9,8},{10,11... | collective-permute-start | bytes 491528 | tf_op jit(solution)/shard_map/ppermute | solution.py:296
  30.3 1.3 %collective-permute-done.12.refs_4_ = bf16[5,128,128]{2,1,0:T(8,128)(2,1)S(1)} collective-permute-done((bf16[5,128,128]{2,1,0:T(8,128)(2,1)S(1)}, bf16[5,128,128]{2,1,0:T(8,128)(2,1)S(1)}, u32[]{:S(2)}, u32[]{:S(2)}) %collective-permute-start.12) | collective-permute-done | bytes 163872 | tf_op jit(solution)/shard_map/ppermute | solution.py:296
  31.6 3.7 %collective-permute-done.14.refs_2_ = bf16[5,128,128]{2,1,0:T(8,128)(2,1)S(1)} collective-permute-done((bf16[5,128,128]{2,1,0:T(8,128)(2,1)S(1)}, bf16[5,128,128]{2,1,0:T(8,128)(2,1)S(1)}, u32[]{:S(2)}, u32[]{:S(2)}) %collective-permute-start.14) | collective-permute-done | bytes 163872 | tf_op jit(solution)/shard_map/ppermute | solution.py:296
  36.2 2.9 %collective-permute-start.17 = (bf16[6,128,128]{2,1,0:T(8,128)(2,1)S(1)}, bf16[6,128,128]{2,1,0:T(8,128)(2,1)S(1)}, u32[]{:S(2)}, u32[]{:S(2)}) collective-permute-start(bf16[6,128,128]{2,1,0:T(8,128)(2,1)S(1)} %get-tuple-element.88.refs_0_), channel_id=1, source_target_pairs={{0,1},{1,0},{2,3},{3,2},{4,5},{5,4},{6,7},{7,6},{8,9},{9,8},{10,11... | collective-permute-start | bytes 589832 | tf_op jit(solution)/shard_map/ppermute | solution.py:296
  40.8 2.5 %collective-permute-done.15.refs_3_ = bf16[5,128,128]{2,1,0:T(8,128)(2,1)S(1)} collective-permute-done((bf16[5,128,128]{2,1,0:T(8,128)(2,1)S(1)}, bf16[5,128,128]{2,1,0:T(8,128)(2,1)S(1)}, u32[]{:S(2)}, u32[]{:S(2)}) %collective-permute-start.15) | collective-permute-done | bytes 163872 | tf_op jit(solution)/shard_map/ppermute | solution.py:311
  43.8 4.1 %collective-permute-done.20.refs_4_ = bf16[5,128,128]{2,1,0:T(8,128)(2,1)S(1)} collective-permute-done((bf16[5,128,128]{2,1,0:T(8,128)(2,1)S(1)}, bf16[5,128,128]{2,1,0:T(8,128)(2,1)S(1)}, u32[]{:S(2)}, u32[]{:S(2)}) %collective-permute-start.20) | collective-permute-done | bytes 163872 | tf_op jit(solution)/shard_map/ppermute | solution.py:296
  47.9 3.4 %collective-permute-done.22.refs_2_ = bf16[5,128,128]{2,1,0:T(8,128)(2,1)S(1)} collective-permute-done((bf16[5,128,128]{2,1,0:T(8,128)(2,1)S(1)}, bf16[5,128,128]{2,1,0:T(8,128)(2,1)S(1)}, u32[]{:S(2)}, u32[]{:S(2)}) %collective-permute-start.22) | collective-permute-done | bytes 163872 | tf_op jit(solution)/shard_map/ppermute | solution.py:296
  51.9 1.4 %collective-permute-done.18.refs_3_ = bf16[6,128,128]{2,1,0:T(8,128)(2,1)S(1)} collective-permute-done((bf16[6,128,128]{2,1,0:T(8,128)(2,1)S(1)}, bf16[6,128,128]{2,1,0:T(8,128)(2,1)S(1)}, u32[]{:S(2)}, u32[]{:S(2)}) %collective-permute-start.18) | collective-permute-done | bytes 196640 | tf_op jit(solution)/shard_map/ppermute | solution.py:311
  53.6 1.9 %collective-permute-start.30 = (bf16[6,128,128]{2,1,0:T(8,128)(2,1)S(1)}, bf16[6,128,128]{2,1,0:T(8,128)(2,1)S(1)}, u32[]{:S(2)}, u32[]{:S(2)}) collective-permute-start(bf16[6,128,128]{2,1,0:T(8,128)(2,1)S(1)} %get-tuple-element.101.refs_0_), channel_id=1, source_target_pairs={{0,1},{1,0},{2,3},{3,2},{4,5},{5,4},{6,7},{7,6},{8,9},{9,8},{10,11... | collective-permute-start | bytes 589832 | tf_op jit(solution)/shard_map/ppermute | solution.py:296
  57.3 2.6 %collective-permute-done.23.refs_3_ = bf16[5,128,128]{2,1,0:T(8,128)(2,1)S(1)} collective-permute-done((bf16[5,128,128]{2,1,0:T(8,128)(2,1)S(1)}, bf16[5,128,128]{2,1,0:T(8,128)(2,1)S(1)}, u32[]{:S(2)}, u32[]{:S(2)}) %collective-permute-start.23) | collective-permute-done | bytes 163872 | tf_op jit(solution)/shard_map/ppermute | solution.py:311
  61.5 1.2 %correction.1.refs_1_ = f32[1,16,128,128]{3,2,1,0:T(8,128)} custom-call(bf16[6,128,128]{2,1,0:T(8,128)(2,1)S(1)} %get-tuple-element.55.refs_3_.refs_4_.refs_0_, bf16[5,128,128]{2,1,0:T(8,128)(2,1)S(1)} %get-tuple-element.58.refs_4_.refs_6_.refs_1_, bf16[5,128,128]{2,1,0:T(8,128)(2,1)S(1)} %get-tuple-element.60.refs_5_.refs_4_.refs_2_, ...), custom_call_target="tpu_custom_call" | custom-call | bytes 3670016 | tf_op jit(solution)/shard_map/correction/pallas_call | solution.py:44
  62.6 2.3 %collective-permute-done.28.refs_0_ = bf16[5,128,128]{2,1,0:T(8,128)(2,1)S(1)} collective-permute-done((bf16[5,128,128]{2,1,0:T(8,128)(2,1)S(1)}, bf16[5,128,128]{2,1,0:T(8,128)(2,1)S(1)}, u32[]{:S(2)}, u32[]{:S(2)}) %collective-permute-start.28) | collective-permute-done | bytes 163872 | tf_op jit(solution)/shard_map/ppermute | solution.py:296
  65.0 2.5 %collective-permute-done.25.refs_2_ = bf16[5,128,128]{2,1,0:T(8,128)(2,1)S(1)} collective-permute-done((bf16[5,128,128]{2,1,0:T(8,128)(2,1)S(1)}, bf16[5,128,128]{2,1,0:T(8,128)(2,1)S(1)}, u32[]{:S(2)}, u32[]{:S(2)}) %collective-permute-start.25) | collective-permute-done | bytes 163872 | tf_op jit(solution)/shard_map/ppermute | solution.py:296
  67.5 1.2 %collective-permute-done.27.halo = bf16[8,128,128]{2,1,0:T(8,128)(2,1)S(1)} collective-permute-done((bf16[8,128,128]{2,1,0:T(8,128)(2,1)S(1)}, bf16[8,128,128]{2,1,0:T(8,128)(2,1)S(1)}, u32[]{:S(2)}, u32[]{:S(2)}) %collective-permute-start.27) | collective-permute-done | bytes 262176 | tf_op jit(solution)/shard_map/ppermute | solution.py:297
  72.0 2.5 %collective-permute-done.29.refs_5_ = bf16[5,128,128]{2,1,0:T(8,128)(2,1)S(1)} collective-permute-done((bf16[5,128,128]{2,1,0:T(8,128)(2,1)S(1)}, bf16[5,128,128]{2,1,0:T(8,128)(2,1)S(1)}, u32[]{:S(2)}, u32[]{:S(2)}) %collective-permute-start.29) | collective-permute-done | bytes 163872 | tf_op jit(solution)/shard_map/ppermute | solution.py:311
  75.5 1.4 %collective-permute-done.26.refs_3_ = bf16[5,128,128]{2,1,0:T(8,128)(2,1)S(1)} collective-permute-done((bf16[5,128,128]{2,1,0:T(8,128)(2,1)S(1)}, bf16[5,128,128]{2,1,0:T(8,128)(2,1)S(1)}, u32[]{:S(2)}, u32[]{:S(2)}) %collective-permute-start.26) | collective-permute-done | bytes 163872 | tf_op jit(solution)/shard_map/ppermute | solution.py:311
  (66 shorter events, 21.6 us)
Async XLA Ops:
  1.6 7.9 %collective-permute-start.1 = (bf16[6,128,128]{2,1,0:T(8,128)(2,1)S(1)}, bf16[6,128,128]{2,1,0:T(8,128)(2,1)S(1)}, u32[]{:S(2)}, u32[]{:S(2)}) collective-permute-start(bf16[6,128,128]{2,1,0:T(8,128)(2,1)S(1)} %get-tuple-element.62.refs_0_), channel_id=1, source_target_pairs={{0,1},{1,0},{2,3},{3,2},{4,5},{5,4},{6,7},{7,6},{8,9},{9,8},{10,11... | collective-permute-start | bytes 589832 | tf_op jit(solution)/shard_map/ppermute | solution.py:296
  7.9 9.4 %collective-permute-start = (bf16[8,128,128]{2,1,0:T(8,128)(2,1)S(1)}, bf16[8,128,128]{2,1,0:T(8,128)(2,1)S(1)}, u32[]{:S(2)}, u32[]{:S(2)}) collective-permute-start(bf16[8,128,128]{2,1,0:T(8,128)(2,1)S(1)} %get-tuple-element.61), channel_id=1, source_target_pairs={{0,24},{8,16},{16,8},{24,0},{1,25},{9,17},{17,9},{25,1},{2,26},{10... | collective-permute-start | bytes 786440 | tf_op jit(solution)/shard_map/ppermute | solution.py:297
  9.5 9.0 %collective-permute-start.2 = (bf16[6,128,128]{2,1,0:T(8,128)(2,1)S(1)}, bf16[6,128,128]{2,1,0:T(8,128)(2,1)S(1)}, u32[]{:S(2)}, u32[]{:S(2)}) collective-permute-start(bf16[6,128,128]{2,1,0:T(8,128)(2,1)S(1)} %collective-permute-done.1.refs_2_), channel_id=1, source_target_pairs={{0,2},{1,7},{2,4},{3,1},{4,6},{5,3},{6,0},{7,5},{8,10},{9,15},{10,... | collective-permute-start | bytes 589832 | tf_op jit(solution)/shard_map/ppermute | solution.py:311
  12.2 8.6 %collective-permute-start.3 = (bf16[8,128,128]{2,1,0:T(8,128)(2,1)S(1)}, bf16[8,128,128]{2,1,0:T(8,128)(2,1)S(1)}, u32[]{:S(2)}, u32[]{:S(2)}) collective-permute-start(bf16[8,128,128]{2,1,0:T(8,128)(2,1)S(1)} %get-tuple-element.67), channel_id=1, source_target_pairs={{0,8},{8,0},{16,24},{24,16},{1,9},{9,1},{17,25},{25,17},{2,10},{10... | collective-permute-start | bytes 786440 | tf_op jit(solution)/shard_map/ppermute | solution.py:297
  12.3 8.5 %collective-permute-start.6 = (bf16[5,128,128]{2,1,0:T(8,128)(2,1)S(1)}, bf16[5,128,128]{2,1,0:T(8,128)(2,1)S(1)}, u32[]{:S(2)}, u32[]{:S(2)}) collective-permute-start(bf16[5,128,128]{2,1,0:T(8,128)(2,1)S(1)} %get-tuple-element.64.refs_2_), channel_id=1, source_target_pairs={{0,1},{1,0},{2,3},{3,2},{4,5},{5,4},{6,7},{7,6},{8,9},{9,8},{10,11... | collective-permute-start | bytes 491528 | tf_op jit(solution)/shard_map/ppermute | solution.py:296
  15.9 8.1 %collective-permute-start.5 = (bf16[5,128,128]{2,1,0:T(8,128)(2,1)S(1)}, bf16[5,128,128]{2,1,0:T(8,128)(2,1)S(1)}, u32[]{:S(2)}, u32[]{:S(2)}) collective-permute-start(bf16[5,128,128]{2,1,0:T(8,128)(2,1)S(1)} %collective-permute-done.4.refs_4_), channel_id=1, source_target_pairs={{0,2},{1,7},{2,4},{3,1},{4,6},{5,3},{6,0},{7,5},{8,10},{9,15},{10,... | collective-permute-start | bytes 491528 | tf_op jit(solution)/shard_map/ppermute | solution.py:311
  24.2 11.1 %collective-permute-start.8 = (bf16[8,128,128]{2,1,0:T(8,128)(2,1)S(1)}, bf16[8,128,128]{2,1,0:T(8,128)(2,1)S(1)}, u32[]{:S(2)}, u32[]{:S(2)}) collective-permute-start(bf16[8,128,128]{2,1,0:T(8,128)(2,1)S(1)} %get-tuple-element.74), channel_id=1, source_target_pairs={{0,24},{8,16},{16,8},{24,0},{1,25},{9,17},{17,9},{25,1},{2,26},{10... | collective-permute-start | bytes 786440 | tf_op jit(solution)/shard_map/ppermute | solution.py:297
  25.6 10.3 %collective-permute-start.10 = (bf16[6,128,128]{2,1,0:T(8,128)(2,1)S(1)}, bf16[6,128,128]{2,1,0:T(8,128)(2,1)S(1)}, u32[]{:S(2)}, u32[]{:S(2)}) collective-permute-start(bf16[6,128,128]{2,1,0:T(8,128)(2,1)S(1)} %collective-permute-done.9.refs_2_), channel_id=1, source_target_pairs={{0,2},{1,7},{2,4},{3,1},{4,6},{5,3},{6,0},{7,5},{8,10},{9,15},{10,... | collective-permute-start | bytes 589832 | tf_op jit(solution)/shard_map/ppermute | solution.py:311
  30.3 8.8 %collective-permute-start.11 = (bf16[8,128,128]{2,1,0:T(8,128)(2,1)S(1)}, bf16[8,128,128]{2,1,0:T(8,128)(2,1)S(1)}, u32[]{:S(2)}, u32[]{:S(2)}) collective-permute-start(bf16[8,128,128]{2,1,0:T(8,128)(2,1)S(1)} %get-tuple-element.82), channel_id=1, source_target_pairs={{0,8},{8,0},{16,24},{24,16},{1,9},{9,1},{17,25},{25,17},{2,10},{10... | collective-permute-start | bytes 786440 | tf_op jit(solution)/shard_map/ppermute | solution.py:297
  31.6 8.8 %collective-permute-start.13 = (bf16[5,128,128]{2,1,0:T(8,128)(2,1)S(1)}, bf16[5,128,128]{2,1,0:T(8,128)(2,1)S(1)}, u32[]{:S(2)}, u32[]{:S(2)}) collective-permute-start(bf16[5,128,128]{2,1,0:T(8,128)(2,1)S(1)} %collective-permute-done.12.refs_4_), channel_id=1, source_target_pairs={{0,2},{1,7},{2,4},{3,1},{4,6},{5,3},{6,0},{7,5},{8,10},{9,15},{10,... | collective-permute-start | bytes 491528 | tf_op jit(solution)/shard_map/ppermute | solution.py:311
  35.3 8.0 %collective-permute-start.15 = (bf16[5,128,128]{2,1,0:T(8,128)(2,1)S(1)}, bf16[5,128,128]{2,1,0:T(8,128)(2,1)S(1)}, u32[]{:S(2)}, u32[]{:S(2)}) collective-permute-start(bf16[5,128,128]{2,1,0:T(8,128)(2,1)S(1)} %collective-permute-done.14.refs_2_), channel_id=1, source_target_pairs={{0,2},{1,7},{2,4},{3,1},{4,6},{5,3},{6,0},{7,5},{8,10},{9,15},{10,... | collective-permute-start | bytes 491528 | tf_op jit(solution)/shard_map/ppermute | solution.py:311
  40.7 10.7 %collective-permute-start.16 = (bf16[8,128,128]{2,1,0:T(8,128)(2,1)S(1)}, bf16[8,128,128]{2,1,0:T(8,128)(2,1)S(1)}, u32[]{:S(2)}, u32[]{:S(2)}) collective-permute-start(bf16[8,128,128]{2,1,0:T(8,128)(2,1)S(1)} %get-tuple-element.87), channel_id=1, source_target_pairs={{0,24},{8,16},{16,8},{24,0},{1,25},{9,17},{17,9},{25,1},{2,26},{10... | collective-permute-start | bytes 786440 | tf_op jit(solution)/shard_map/ppermute | solution.py:297
  43.6 7.7 %collective-permute-start.22 = (bf16[5,128,128]{2,1,0:T(8,128)(2,1)S(1)}, bf16[5,128,128]{2,1,0:T(8,128)(2,1)S(1)}, u32[]{:S(2)}, u32[]{:S(2)}) collective-permute-start(bf16[5,128,128]{2,1,0:T(8,128)(2,1)S(1)} %get-tuple-element.90.refs_2_), channel_id=1, source_target_pairs={{0,1},{1,0},{2,3},{3,2},{4,5},{5,4},{6,7},{7,6},{8,9},{9,8},{10,11... | collective-permute-start | bytes 491528 | tf_op jit(solution)/shard_map/ppermute | solution.py:296
  43.7 11.9 %collective-permute-start.19 = (bf16[8,128,128]{2,1,0:T(8,128)(2,1)S(1)}, bf16[8,128,128]{2,1,0:T(8,128)(2,1)S(1)}, u32[]{:S(2)}, u32[]{:S(2)}) collective-permute-start(bf16[8,128,128]{2,1,0:T(8,128)(2,1)S(1)} %get-tuple-element.95), channel_id=1, source_target_pairs={{0,8},{8,0},{16,24},{24,16},{1,9},{9,1},{17,25},{25,17},{2,10},{10... | collective-permute-start | bytes 786440 | tf_op jit(solution)/shard_map/ppermute | solution.py:297
  43.8 9.6 %collective-permute-start.18 = (bf16[6,128,128]{2,1,0:T(8,128)(2,1)S(1)}, bf16[6,128,128]{2,1,0:T(8,128)(2,1)S(1)}, u32[]{:S(2)}, u32[]{:S(2)}) collective-permute-start(bf16[6,128,128]{2,1,0:T(8,128)(2,1)S(1)} %collective-permute-done.17.refs_2_), channel_id=1, source_target_pairs={{0,2},{1,7},{2,4},{3,1},{4,6},{5,3},{6,0},{7,5},{8,10},{9,15},{10,... | collective-permute-start | bytes 589832 | tf_op jit(solution)/shard_map/ppermute | solution.py:311
  47.9 8.9 %collective-permute-start.21 = (bf16[5,128,128]{2,1,0:T(8,128)(2,1)S(1)}, bf16[5,128,128]{2,1,0:T(8,128)(2,1)S(1)}, u32[]{:S(2)}, u32[]{:S(2)}) collective-permute-start(bf16[5,128,128]{2,1,0:T(8,128)(2,1)S(1)} %collective-permute-done.20.refs_4_), channel_id=1, source_target_pairs={{0,2},{1,7},{2,4},{3,1},{4,6},{5,3},{6,0},{7,5},{8,10},{9,15},{10,... | collective-permute-start | bytes 491528 | tf_op jit(solution)/shard_map/ppermute | solution.py:311
  51.3 8.5 %collective-permute-start.23 = (bf16[5,128,128]{2,1,0:T(8,128)(2,1)S(1)}, bf16[5,128,128]{2,1,0:T(8,128)(2,1)S(1)}, u32[]{:S(2)}, u32[]{:S(2)}) collective-permute-start(bf16[5,128,128]{2,1,0:T(8,128)(2,1)S(1)} %collective-permute-done.22.refs_2_), channel_id=1, source_target_pairs={{0,2},{1,7},{2,4},{3,1},{4,6},{5,3},{6,0},{7,5},{8,10},{9,15},{10,... | collective-permute-start | bytes 491528 | tf_op jit(solution)/shard_map/ppermute | solution.py:311
  53.6 7.8 %collective-permute-start.30 = (bf16[6,128,128]{2,1,0:T(8,128)(2,1)S(1)}, bf16[6,128,128]{2,1,0:T(8,128)(2,1)S(1)}, u32[]{:S(2)}, u32[]{:S(2)}) collective-permute-start(bf16[6,128,128]{2,1,0:T(8,128)(2,1)S(1)} %get-tuple-element.101.refs_0_), channel_id=1, source_target_pairs={{0,1},{1,0},{2,3},{3,2},{4,5},{5,4},{6,7},{7,6},{8,9},{9,8},{10,11... | collective-permute-start | bytes 589832 | tf_op jit(solution)/shard_map/ppermute | solution.py:296
  57.1 7.9 %collective-permute-start.28 = (bf16[5,128,128]{2,1,0:T(8,128)(2,1)S(1)}, bf16[5,128,128]{2,1,0:T(8,128)(2,1)S(1)}, u32[]{:S(2)}, u32[]{:S(2)}) collective-permute-start(bf16[5,128,128]{2,1,0:T(8,128)(2,1)S(1)} %get-tuple-element.102.refs_1_), channel_id=1, source_target_pairs={{0,1},{1,0},{2,3},{3,2},{4,5},{5,4},{6,7},{7,6},{8,9},{9,8},{10,11... | collective-permute-start | bytes 491528 | tf_op jit(solution)/shard_map/ppermute | solution.py:296
  60.4 8.4 %collective-permute-start.27 = (bf16[8,128,128]{2,1,0:T(8,128)(2,1)S(1)}, bf16[8,128,128]{2,1,0:T(8,128)(2,1)S(1)}, u32[]{:S(2)}, u32[]{:S(2)}) collective-permute-start(bf16[8,128,128]{2,1,0:T(8,128)(2,1)S(1)} %get-tuple-element.107), channel_id=1, source_target_pairs={{0,24},{8,16},{16,8},{24,0},{1,25},{9,17},{17,9},{25,1},{2,26},{10... | collective-permute-start | bytes 786440 | tf_op jit(solution)/shard_map/ppermute | solution.py:297
  60.5 8.8 %collective-permute-start.24 = (bf16[8,128,128]{2,1,0:T(8,128)(2,1)S(1)}, bf16[8,128,128]{2,1,0:T(8,128)(2,1)S(1)}, u32[]{:S(2)}, u32[]{:S(2)}) collective-permute-start(bf16[8,128,128]{2,1,0:T(8,128)(2,1)S(1)} %get-tuple-element.100), channel_id=1, source_target_pairs={{0,8},{8,0},{16,24},{24,16},{1,9},{9,1},{17,25},{25,17},{2,10},{10... | collective-permute-start | bytes 786440 | tf_op jit(solution)/shard_map/ppermute | solution.py:297
  61.5 9.6 %collective-permute-start.31 = (bf16[6,128,128]{2,1,0:T(8,128)(2,1)S(1)}, bf16[6,128,128]{2,1,0:T(8,128)(2,1)S(1)}, u32[]{:S(2)}, u32[]{:S(2)}) collective-permute-start(bf16[6,128,128]{2,1,0:T(8,128)(2,1)S(1)} %collective-permute-done.30.refs_2_), channel_id=1, source_target_pairs={{0,2},{1,7},{2,4},{3,1},{4,6},{5,3},{6,0},{7,5},{8,10},{9,15},{10,... | collective-permute-start | bytes 589832 | tf_op jit(solution)/shard_map/ppermute | solution.py:311
  65.0 9.6 %collective-permute-start.29 = (bf16[5,128,128]{2,1,0:T(8,128)(2,1)S(1)}, bf16[5,128,128]{2,1,0:T(8,128)(2,1)S(1)}, u32[]{:S(2)}, u32[]{:S(2)}) collective-permute-start(bf16[5,128,128]{2,1,0:T(8,128)(2,1)S(1)} %order.1.refs_4_), channel_id=1, source_target_pairs={{0,2},{1,7},{2,4},{3,1},{4,6},{5,3},{6,0},{7,5},{8,10},{9,15},{10,... | collective-permute-start | bytes 491528 | tf_op jit(solution)/shard_map/ppermute | solution.py:311
  67.5 9.4 %collective-permute-start.26 = (bf16[5,128,128]{2,1,0:T(8,128)(2,1)S(1)}, bf16[5,128,128]{2,1,0:T(8,128)(2,1)S(1)}, u32[]{:S(2)}, u32[]{:S(2)}) collective-permute-start(bf16[5,128,128]{2,1,0:T(8,128)(2,1)S(1)} %collective-permute-done.25.refs_2_), channel_id=1, source_target_pairs={{0,2},{1,7},{2,4},{3,1},{4,6},{5,3},{6,0},{7,5},{8,10},{9,15},{10,... | collective-permute-start | bytes 491528 | tf_op jit(solution)/shard_map/ppermute | solution.py:311
  (8 other events, 57.3 us)

commit v7 on v5

--- a/solution.py
+++ b/solution.py
@@ -150,17 +150,22 @@
         edge[pl.ds(mine[0] % PLANE, len(mine))] = sent_out[pl.ds(mine[0] - piece[0], len(mine))]
 
 
-def first_kernel(piece, residual_hbm, *refs):
-    planes = len(planes_in(piece))
-    residual, sent_out, *edges, sems = refs[-3 - planes :]
+def first_kernel(pieces, residual_hbm, *refs):
+    out, sems = refs[:-1], refs[-1]
     copies = [
-        pltpu.make_async_copy(residual_hbm.at[0, place_of(site)], residual.at[s], sems.at[s])
+        pltpu.make_async_copy(residual_hbm.at[0, place_of(site)], out[i].at[s], sems.at[site])
+        for i, piece in enumerate(pieces)
         for s, site in enumerate(piece)
     ]
     for copy in copies:
         copy.start()
-    for s, copy in enumerate(copies):
+    for copy in copies:
         copy.wait()
+
+
+def direction_kernel(piece, residual, *refs):
+    sent_out, *edges = refs[-1 - len(planes_in(piece)) :]
+    for s in range(len(piece)):
         sent_out[s] = (residual[s].astype(F32) * (half_width / center_value)).astype(BF16)
     store_edges(piece, sent_out, edges)
 
@@ -270,21 +275,26 @@
         return outs[: -len(planes)]
 
     weight_local, weight_time = prep(self_block, hop_blocks, sites)
-    start, sent, edges = [], [], {}
+    start = call(
+        functools.partial(first_kernel, pieces),
+        [vector(piece, BF16) for piece in pieces],
+        [residual_in],
+        0,
+        "residual",
+        in_specs=[IN_HBM],
+        scratch=[pltpu.SemaphoreType.DMA((sites,))],
+    )
+    sent, edges = [], {}
     for i, piece in enumerate(pieces):
         tie = [weight_local[0]] if i == 1 else []
-        outs = with_edges(
-            functools.partial(first_kernel, piece),
-            [vector(piece, BF16)] * 2,
-            [residual_in] + tie,
+        sent += with_edges(
+            functools.partial(direction_kernel, piece),
+            [vector(piece, BF16)],
+            [start[i]] + tie,
             edges,
             0,
             "first_direction",
-            in_specs=[IN_HBM] + [WHOLE] * len(tie),
-            scratch=[pltpu.SemaphoreType.DMA((len(piece),))],
-        )
-        start.append(outs[0])
-        sent.append(outs[1])
+        )
     residual, direction = start, start
     directions = []
     for number in range(STEPS):

time: 78.2 us -> 77.4 us (0.990)
  Pallas kernels: 16.2 us -> 14.8 us
  starting transfers between devices: 22.7 us -> 23.6 us
    ppermute x12, starting transfers between devices: 4.06 us -> 5.93 us  [body(): far = [lax.ppermute(v, 'site', relay) for v in near]]
    pallas_call x25 -> x26, Pallas kernels: 16.2 us -> 14.8 us  [call(): pl.pallas_call(kernel, out_shape=outs, in_specs=in_specs, out_specs=out_s...]
    ppermute x12, waiting for transfers between devices: 19.7 us -> 18.7 us  [body(): near = [lax.ppermute(v, 'site', swap) for v in sent]]
    ppermute x12, starting transfers between devices: 16.3 us -> 15.5 us  [body(): near = [lax.ppermute(v, 'site', swap) for v in sent]]
  transfers between devices with their start and end apart: 32 -> 32, of which waited for: 20 -> 20; matrix products, arithmetic and copies ran while one was open for 0% -> 0% of each run, Pallas kernels for 18% -> 16%
where the time goes in v7:
time: 77.4 us; the launch traced here: 77.2 us
  waiting for transfers between devices  38 us (49%)
  starting transfers between devices  23.6 us (30%)
  Pallas kernels  14.8 us (19%)
  between operations  0.83 us (1%)
    ppermute x12, waiting for transfers between devices, body(): near = [lax.ppermute(v, 'site', swap) for v in sent]  18.7 us
    ppermute x12, waiting for transfers between devices, body(): far = [lax.ppermute(v, 'site', relay) for v in near]  18.6 us
    ppermute x12, starting transfers between devices, body(): near = [lax.ppermute(v, 'site', swap) for v in sent]  15.5 us
    pallas_call x26, Pallas kernels, call(): pl.pallas_call(kernel, out_shape=outs, in_specs=in_specs, out_specs=out_s...  14.8 us
    ppermute x12, starting transfers between devices, body(): far = [lax.ppermute(v, 'site', relay) for v in near]  5.93 us
    ppermute x4, starting transfers between devices, body(): lax.ppermute(edges[0], 'group', chips)  1.6 us
  transfers between devices with their start and end apart: 32, of which 20 were waited for; matrix products, arithmetic and copies ran while one was open for 0% of the time, Pallas kernels for 16%

profile of v7, /device:TPU:0, one launch (start us, length us, event | category | flops | bytes accessed | tf_op | source)
XLA Modules:
  0.0 77.2 jit_solution(5811136683744726303)
XLA Ops:
  1.8 3.0 %collective-permute-start.1 = (bf16[6,128,128]{2,1,0:T(8,128)(2,1)S(1)}, bf16[6,128,128]{2,1,0:T(8,128)(2,1)S(1)}, u32[]{:S(2)}, u32[]{:S(2)}) collective-permute-start(bf16[6,128,128]{2,1,0:T(8,128)(2,1)S(1)} %get-tuple-element.61.refs_0_), channel_id=1, source_target_pairs={{0,1},{1,0},{2,3},{3,2},{4,5},{5,4},{6,7},{7,6},{8,9},{9,8},{10,11... | collective-permute-start | bytes 589832 | tf_op jit(solution)/shard_map/ppermute | solution.py:302
  4.9 2.4 %prep.1 = (bf16[8,128,768]{2,1,0:T(8,128)(2,1)S(1)}, bf16[8,128,768]{2,1,0:T(8,128)(2,1)S(1)}, bf16[8,128,256]{2,1,0:T(8,128)(2,1)S(1)}, bf16[8,128,256]{2,1,0:T(8,128)(2,1)S(1)}) custom-call(bf16[1,64,64,128]{3,2,1,0:T(8,128)(2,1)} %self_hbm.1, bf16[1,64,8,64,128]{4,3,2,1,0:T(8,128)(2,1)} %hop_hbm.1), custom_call_target="tpu_custom_call" | custom-call | bytes 9437184 | tf_op jit(solution)/shard_map/prep/pallas_call | solution.py:44
  8.5 1.2 %collective-permute-done.1.refs_2_ = bf16[6,128,128]{2,1,0:T(8,128)(2,1)S(1)} collective-permute-done((bf16[6,128,128]{2,1,0:T(8,128)(2,1)S(1)}, bf16[6,128,128]{2,1,0:T(8,128)(2,1)S(1)}, u32[]{:S(2)}, u32[]{:S(2)}) %collective-permute-start.1) | collective-permute-done | bytes 196640 | tf_op jit(solution)/shard_map/ppermute | solution.py:302
  9.8 1.8 %collective-permute-start.2 = (bf16[6,128,128]{2,1,0:T(8,128)(2,1)S(1)}, bf16[6,128,128]{2,1,0:T(8,128)(2,1)S(1)}, u32[]{:S(2)}, u32[]{:S(2)}) collective-permute-start(bf16[6,128,128]{2,1,0:T(8,128)(2,1)S(1)} %collective-permute-done.1.refs_2_), channel_id=1, source_target_pairs={{0,2},{1,7},{2,4},{3,1},{4,6},{5,3},{6,0},{7,5},{8,10},{9,15},{10,... | collective-permute-start | bytes 589832 | tf_op jit(solution)/shard_map/ppermute | solution.py:304
  11.7 3.6 %collective-permute-start.6 = (bf16[5,128,128]{2,1,0:T(8,128)(2,1)S(1)}, bf16[5,128,128]{2,1,0:T(8,128)(2,1)S(1)}, u32[]{:S(2)}, u32[]{:S(2)}) collective-permute-start(bf16[5,128,128]{2,1,0:T(8,128)(2,1)S(1)} %get-tuple-element.64.refs_2_), channel_id=1, source_target_pairs={{0,1},{1,0},{2,3},{3,2},{4,5},{5,4},{6,7},{7,6},{8,9},{9,8},{10,11... | collective-permute-start | bytes 491528 | tf_op jit(solution)/shard_map/ppermute | solution.py:302
  15.3 1.4 %collective-permute-start.5 = (bf16[5,128,128]{2,1,0:T(8,128)(2,1)S(1)}, bf16[5,128,128]{2,1,0:T(8,128)(2,1)S(1)}, u32[]{:S(2)}, u32[]{:S(2)}) collective-permute-start(bf16[5,128,128]{2,1,0:T(8,128)(2,1)S(1)} %collective-permute-done.4.refs_4_), channel_id=1, source_target_pairs={{0,2},{1,7},{2,4},{3,1},{4,6},{5,3},{6,0},{7,5},{8,10},{9,15},{10,... | collective-permute-start | bytes 491528 | tf_op jit(solution)/shard_map/ppermute | solution.py:304
  18.2 2.0 %collective-permute-start.9 = (bf16[6,128,128]{2,1,0:T(8,128)(2,1)S(1)}, bf16[6,128,128]{2,1,0:T(8,128)(2,1)S(1)}, u32[]{:S(2)}, u32[]{:S(2)}) collective-permute-start(bf16[6,128,128]{2,1,0:T(8,128)(2,1)S(1)} %get-tuple-element.75.refs_0_), channel_id=1, source_target_pairs={{0,1},{1,0},{2,3},{3,2},{4,5},{5,4},{6,7},{7,6},{8,9},{9,8},{10,11... | collective-permute-start | bytes 589832 | tf_op jit(solution)/shard_map/ppermute | solution.py:302
  20.8 2.6 %collective-permute-done.5.refs_5_ = bf16[5,128,128]{2,1,0:T(8,128)(2,1)S(1)} collective-permute-done((bf16[5,128,128]{2,1,0:T(8,128)(2,1)S(1)}, bf16[5,128,128]{2,1,0:T(8,128)(2,1)S(1)}, u32[]{:S(2)}, u32[]{:S(2)}) %collective-permute-start.5) | collective-permute-done | bytes 163872 | tf_op jit(solution)/shard_map/ppermute | solution.py:304
  25.8 2.0 %collective-permute-done.7.refs_3_ = bf16[5,128,128]{2,1,0:T(8,128)(2,1)S(1)} collective-permute-done((bf16[5,128,128]{2,1,0:T(8,128)(2,1)S(1)}, bf16[5,128,128]{2,1,0:T(8,128)(2,1)S(1)}, u32[]{:S(2)}, u32[]{:S(2)}) %collective-permute-start.7) | collective-permute-done | bytes 163872 | tf_op jit(solution)/shard_map/ppermute | solution.py:304
  28.1 1.2 %collective-permute-start.14 = (bf16[5,128,128]{2,1,0:T(8,128)(2,1)S(1)}, bf16[5,128,128]{2,1,0:T(8,128)(2,1)S(1)}, u32[]{:S(2)}, u32[]{:S(2)}) collective-permute-start(bf16[5,128,128]{2,1,0:T(8,128)(2,1)S(1)} %get-tuple-element.77.refs_2_), channel_id=1, source_target_pairs={{0,1},{1,0},{2,3},{3,2},{4,5},{5,4},{6,7},{7,6},{8,9},{9,8},{10,11... | collective-permute-start | bytes 491528 | tf_op jit(solution)/shard_map/ppermute | solution.py:302
  29.3 2.0 %collective-permute-done.12.refs_4_ = bf16[5,128,128]{2,1,0:T(8,128)(2,1)S(1)} collective-permute-done((bf16[5,128,128]{2,1,0:T(8,128)(2,1)S(1)}, bf16[5,128,128]{2,1,0:T(8,128)(2,1)S(1)}, u32[]{:S(2)}, u32[]{:S(2)}) %collective-permute-start.12) | collective-permute-done | bytes 163872 | tf_op jit(solution)/shard_map/ppermute | solution.py:302
  31.3 3.7 %collective-permute-done.14.refs_2_ = bf16[5,128,128]{2,1,0:T(8,128)(2,1)S(1)} collective-permute-done((bf16[5,128,128]{2,1,0:T(8,128)(2,1)S(1)}, bf16[5,128,128]{2,1,0:T(8,128)(2,1)S(1)}, u32[]{:S(2)}, u32[]{:S(2)}) %collective-permute-start.14) | collective-permute-done | bytes 163872 | tf_op jit(solution)/shard_map/ppermute | solution.py:302
  35.9 3.0 %collective-permute-start.17 = (bf16[6,128,128]{2,1,0:T(8,128)(2,1)S(1)}, bf16[6,128,128]{2,1,0:T(8,128)(2,1)S(1)}, u32[]{:S(2)}, u32[]{:S(2)}) collective-permute-start(bf16[6,128,128]{2,1,0:T(8,128)(2,1)S(1)} %get-tuple-element.88.refs_0_), channel_id=1, source_target_pairs={{0,1},{1,0},{2,3},{3,2},{4,5},{5,4},{6,7},{7,6},{8,9},{9,8},{10,11... | collective-permute-start | bytes 589832 | tf_op jit(solution)/shard_map/ppermute | solution.py:302
  40.2 2.8 %collective-permute-done.15.refs_3_ = bf16[5,128,128]{2,1,0:T(8,128)(2,1)S(1)} collective-permute-done((bf16[5,128,128]{2,1,0:T(8,128)(2,1)S(1)}, bf16[5,128,128]{2,1,0:T(8,128)(2,1)S(1)}, u32[]{:S(2)}, u32[]{:S(2)}) %collective-permute-start.15) | collective-permute-done | bytes 163872 | tf_op jit(solution)/shard_map/ppermute | solution.py:304
  43.9 3.1 %collective-permute-done.20.refs_4_ = bf16[5,128,128]{2,1,0:T(8,128)(2,1)S(1)} collective-permute-done((bf16[5,128,128]{2,1,0:T(8,128)(2,1)S(1)}, bf16[5,128,128]{2,1,0:T(8,128)(2,1)S(1)}, u32[]{:S(2)}, u32[]{:S(2)}) %collective-permute-start.20) | collective-permute-done | bytes 163872 | tf_op jit(solution)/shard_map/ppermute | solution.py:302
  47.4 3.1 %collective-permute-done.22.refs_2_ = bf16[5,128,128]{2,1,0:T(8,128)(2,1)S(1)} collective-permute-done((bf16[5,128,128]{2,1,0:T(8,128)(2,1)S(1)}, bf16[5,128,128]{2,1,0:T(8,128)(2,1)S(1)}, u32[]{:S(2)}, u32[]{:S(2)}) %collective-permute-start.22) | collective-permute-done | bytes 163872 | tf_op jit(solution)/shard_map/ppermute | solution.py:302
  51.1 1.9 %collective-permute-done.18.refs_3_ = bf16[6,128,128]{2,1,0:T(8,128)(2,1)S(1)} collective-permute-done((bf16[6,128,128]{2,1,0:T(8,128)(2,1)S(1)}, bf16[6,128,128]{2,1,0:T(8,128)(2,1)S(1)}, u32[]{:S(2)}, u32[]{:S(2)}) %collective-permute-start.18) | collective-permute-done | bytes 196640 | tf_op jit(solution)/shard_map/ppermute | solution.py:304
  55.0 1.6 %collective-permute-done.21.refs_5_ = bf16[5,128,128]{2,1,0:T(8,128)(2,1)S(1)} collective-permute-done((bf16[5,128,128]{2,1,0:T(8,128)(2,1)S(1)}, bf16[5,128,128]{2,1,0:T(8,128)(2,1)S(1)}, u32[]{:S(2)}, u32[]{:S(2)}) %collective-permute-start.21) | collective-permute-done | bytes 163872 | tf_op jit(solution)/shard_map/ppermute | solution.py:304
  57.7 2.0 %collective-permute-done.23.refs_3_ = bf16[5,128,128]{2,1,0:T(8,128)(2,1)S(1)} collective-permute-done((bf16[5,128,128]{2,1,0:T(8,128)(2,1)S(1)}, bf16[5,128,128]{2,1,0:T(8,128)(2,1)S(1)}, u32[]{:S(2)}, u32[]{:S(2)}) %collective-permute-start.23) | collective-permute-done | bytes 163872 | tf_op jit(solution)/shard_map/ppermute | solution.py:304
  61.1 2.8 %collective-permute-done.28.refs_4_ = bf16[5,128,128]{2,1,0:T(8,128)(2,1)S(1)} collective-permute-done((bf16[5,128,128]{2,1,0:T(8,128)(2,1)S(1)}, bf16[5,128,128]{2,1,0:T(8,128)(2,1)S(1)}, u32[]{:S(2)}, u32[]{:S(2)}) %collective-permute-start.28) | collective-permute-done | bytes 163872 | tf_op jit(solution)/shard_map/ppermute | solution.py:302
  64.6 2.0 %collective-permute-done.25.refs_2_ = bf16[5,128,128]{2,1,0:T(8,128)(2,1)S(1)} collective-permute-done((bf16[5,128,128]{2,1,0:T(8,128)(2,1)S(1)}, bf16[5,128,128]{2,1,0:T(8,128)(2,1)S(1)}, u32[]{:S(2)}, u32[]{:S(2)}) %collective-permute-start.25) | collective-permute-done | bytes 163872 | tf_op jit(solution)/shard_map/ppermute | solution.py:302
  66.6 1.2 %correction.1 = f32[1,16,128,128]{3,2,1,0:T(8,128)} custom-call(bf16[6,128,128]{2,1,0:T(8,128)(2,1)S(1)} %get-tuple-element.55.residual.refs_3_.refs_4_.refs_0_, bf16[5,128,128]{2,1,0:T(8,128)(2,1)S(1)} %get-tuple-element.56.residual.refs_4_.refs_6_.refs_1_, bf16[5,128,128]{2,1,0:T(8,128)(2,1)S(1)} %get-tuple-element.57.residual.refs_5_.refs_4_.refs_2_, ...), custom_call_target="tpu_custom_call" | custom-call | bytes 3670016 | tf_op jit(solution)/shard_map/correction/pallas_call | solution.py:44
  71.1 2.5 %collective-permute-done.29.refs_5_ = bf16[5,128,128]{2,1,0:T(8,128)(2,1)S(1)} collective-permute-done((bf16[5,128,128]{2,1,0:T(8,128)(2,1)S(1)}, bf16[5,128,128]{2,1,0:T(8,128)(2,1)S(1)}, u32[]{:S(2)}, u32[]{:S(2)}) %collective-permute-start.29) | collective-permute-done | bytes 163872 | tf_op jit(solution)/shard_map/ppermute | solution.py:304
  74.5 1.7 %collective-permute-done.26.refs_3_ = bf16[5,128,128]{2,1,0:T(8,128)(2,1)S(1)} collective-permute-done((bf16[5,128,128]{2,1,0:T(8,128)(2,1)S(1)}, bf16[5,128,128]{2,1,0:T(8,128)(2,1)S(1)}, u32[]{:S(2)}, u32[]{:S(2)}) %collective-permute-start.26) | collective-permute-done | bytes 163872 | tf_op jit(solution)/shard_map/ppermute | solution.py:304
  (66 shorter events, 21.6 us)
Async XLA Ops:
  1.8 7.9 %collective-permute-start.1 = (bf16[6,128,128]{2,1,0:T(8,128)(2,1)S(1)}, bf16[6,128,128]{2,1,0:T(8,128)(2,1)S(1)}, u32[]{:S(2)}, u32[]{:S(2)}) collective-permute-start(bf16[6,128,128]{2,1,0:T(8,128)(2,1)S(1)} %get-tuple-element.61.refs_0_), channel_id=1, source_target_pairs={{0,1},{1,0},{2,3},{3,2},{4,5},{5,4},{6,7},{7,6},{8,9},{9,8},{10,11... | collective-permute-start | bytes 589832 | tf_op jit(solution)/shard_map/ppermute | solution.py:302
  7.3 9.4 %collective-permute-start = (bf16[8,128,128]{2,1,0:T(8,128)(2,1)S(1)}, bf16[8,128,128]{2,1,0:T(8,128)(2,1)S(1)}, u32[]{:S(2)}, u32[]{:S(2)}) collective-permute-start(bf16[8,128,128]{2,1,0:T(8,128)(2,1)S(1)} %get-tuple-element.60), channel_id=1, source_target_pairs={{0,24},{8,16},{16,8},{24,0},{1,25},{9,17},{17,9},{25,1},{2,26},{10... | collective-permute-start | bytes 786440 | tf_op jit(solution)/shard_map/ppermute | solution.py:303
  8.0 7.3 %collective-permute-start.4 = (bf16[5,128,128]{2,1,0:T(8,128)(2,1)S(1)}, bf16[5,128,128]{2,1,0:T(8,128)(2,1)S(1)}, u32[]{:S(2)}, u32[]{:S(2)}) collective-permute-start(bf16[5,128,128]{2,1,0:T(8,128)(2,1)S(1)} %get-tuple-element.62.refs_1_), channel_id=1, source_target_pairs={{0,1},{1,0},{2,3},{3,2},{4,5},{5,4},{6,7},{7,6},{8,9},{9,8},{10,11... | collective-permute-start | bytes 491528 | tf_op jit(solution)/shard_map/ppermute | solution.py:302
  9.8 8.1 %collective-permute-start.2 = (bf16[6,128,128]{2,1,0:T(8,128)(2,1)S(1)}, bf16[6,128,128]{2,1,0:T(8,128)(2,1)S(1)}, u32[]{:S(2)}, u32[]{:S(2)}) collective-permute-start(bf16[6,128,128]{2,1,0:T(8,128)(2,1)S(1)} %collective-permute-done.1.refs_2_), channel_id=1, source_target_pairs={{0,2},{1,7},{2,4},{3,1},{4,6},{5,3},{6,0},{7,5},{8,10},{9,15},{10,... | collective-permute-start | bytes 589832 | tf_op jit(solution)/shard_map/ppermute | solution.py:304
  11.6 8.6 %collective-permute-start.3 = (bf16[8,128,128]{2,1,0:T(8,128)(2,1)S(1)}, bf16[8,128,128]{2,1,0:T(8,128)(2,1)S(1)}, u32[]{:S(2)}, u32[]{:S(2)}) collective-permute-start(bf16[8,128,128]{2,1,0:T(8,128)(2,1)S(1)} %get-tuple-element.67), channel_id=1, source_target_pairs={{0,8},{8,0},{16,24},{24,16},{1,9},{9,1},{17,25},{25,17},{2,10},{10... | collective-permute-start | bytes 786440 | tf_op jit(solution)/shard_map/ppermute | solution.py:303
  11.7 8.5 %collective-permute-start.6 = (bf16[5,128,128]{2,1,0:T(8,128)(2,1)S(1)}, bf16[5,128,128]{2,1,0:T(8,128)(2,1)S(1)}, u32[]{:S(2)}, u32[]{:S(2)}) collective-permute-start(bf16[5,128,128]{2,1,0:T(8,128)(2,1)S(1)} %get-tuple-element.64.refs_2_), channel_id=1, source_target_pairs={{0,1},{1,0},{2,3},{3,2},{4,5},{5,4},{6,7},{7,6},{8,9},{9,8},{10,11... | collective-permute-start | bytes 491528 | tf_op jit(solution)/shard_map/ppermute | solution.py:302
  15.3 8.1 %collective-permute-start.5 = (bf16[5,128,128]{2,1,0:T(8,128)(2,1)S(1)}, bf16[5,128,128]{2,1,0:T(8,128)(2,1)S(1)}, u32[]{:S(2)}, u32[]{:S(2)}) collective-permute-start(bf16[5,128,128]{2,1,0:T(8,128)(2,1)S(1)} %collective-permute-done.4.refs_4_), channel_id=1, source_target_pairs={{0,2},{1,7},{2,4},{3,1},{4,6},{5,3},{6,0},{7,5},{8,10},{9,15},{10,... | collective-permute-start | bytes 491528 | tf_op jit(solution)/shard_map/ppermute | solution.py:304
  20.2 7.7 %collective-permute-start.7 = (bf16[5,128,128]{2,1,0:T(8,128)(2,1)S(1)}, bf16[5,128,128]{2,1,0:T(8,128)(2,1)S(1)}, u32[]{:S(2)}, u32[]{:S(2)}) collective-permute-start(bf16[5,128,128]{2,1,0:T(8,128)(2,1)S(1)} %collective-permute-done.6.refs_2_), channel_id=1, source_target_pairs={{0,2},{1,7},{2,4},{3,1},{4,6},{5,3},{6,0},{7,5},{8,10},{9,15},{10,... | collective-permute-start | bytes 491528 | tf_op jit(solution)/shard_map/ppermute | solution.py:304
  23.7 11.4 %collective-permute-start.8 = (bf16[8,128,128]{2,1,0:T(8,128)(2,1)S(1)}, bf16[8,128,128]{2,1,0:T(8,128)(2,1)S(1)}, u32[]{:S(2)}, u32[]{:S(2)}) collective-permute-start(bf16[8,128,128]{2,1,0:T(8,128)(2,1)S(1)} %get-tuple-element.74), channel_id=1, source_target_pairs={{0,24},{8,16},{16,8},{24,0},{1,25},{9,17},{17,9},{25,1},{2,26},{10... | collective-permute-start | bytes 786440 | tf_op jit(solution)/shard_map/ppermute | solution.py:303
  25.1 10.6 %collective-permute-start.10 = (bf16[6,128,128]{2,1,0:T(8,128)(2,1)S(1)}, bf16[6,128,128]{2,1,0:T(8,128)(2,1)S(1)}, u32[]{:S(2)}, u32[]{:S(2)}) collective-permute-start(bf16[6,128,128]{2,1,0:T(8,128)(2,1)S(1)} %collective-permute-done.9.refs_2_), channel_id=1, source_target_pairs={{0,2},{1,7},{2,4},{3,1},{4,6},{5,3},{6,0},{7,5},{8,10},{9,15},{10,... | collective-permute-start | bytes 589832 | tf_op jit(solution)/shard_map/ppermute | solution.py:304
  29.3 9.6 %collective-permute-start.11 = (bf16[8,128,128]{2,1,0:T(8,128)(2,1)S(1)}, bf16[8,128,128]{2,1,0:T(8,128)(2,1)S(1)}, u32[]{:S(2)}, u32[]{:S(2)}) collective-permute-start(bf16[8,128,128]{2,1,0:T(8,128)(2,1)S(1)} %get-tuple-element.82), channel_id=1, source_target_pairs={{0,8},{8,0},{16,24},{24,16},{1,9},{9,1},{17,25},{25,17},{2,10},{10... | collective-permute-start | bytes 786440 | tf_op jit(solution)/shard_map/ppermute | solution.py:303
  31.3 8.5 %collective-permute-start.13 = (bf16[5,128,128]{2,1,0:T(8,128)(2,1)S(1)}, bf16[5,128,128]{2,1,0:T(8,128)(2,1)S(1)}, u32[]{:S(2)}, u32[]{:S(2)}) collective-permute-start(bf16[5,128,128]{2,1,0:T(8,128)(2,1)S(1)} %collective-permute-done.12.refs_4_), channel_id=1, source_target_pairs={{0,2},{1,7},{2,4},{3,1},{4,6},{5,3},{6,0},{7,5},{8,10},{9,15},{10,... | collective-permute-start | bytes 491528 | tf_op jit(solution)/shard_map/ppermute | solution.py:304
  35.0 8.0 %collective-permute-start.15 = (bf16[5,128,128]{2,1,0:T(8,128)(2,1)S(1)}, bf16[5,128,128]{2,1,0:T(8,128)(2,1)S(1)}, u32[]{:S(2)}, u32[]{:S(2)}) collective-permute-start(bf16[5,128,128]{2,1,0:T(8,128)(2,1)S(1)} %collective-permute-done.14.refs_2_), channel_id=1, source_target_pairs={{0,2},{1,7},{2,4},{3,1},{4,6},{5,3},{6,0},{7,5},{8,10},{9,15},{10,... | collective-permute-start | bytes 491528 | tf_op jit(solution)/shard_map/ppermute | solution.py:304
  35.9 7.6 %collective-permute-start.17 = (bf16[6,128,128]{2,1,0:T(8,128)(2,1)S(1)}, bf16[6,128,128]{2,1,0:T(8,128)(2,1)S(1)}, u32[]{:S(2)}, u32[]{:S(2)}) collective-permute-start(bf16[6,128,128]{2,1,0:T(8,128)(2,1)S(1)} %get-tuple-element.88.refs_0_), channel_id=1, source_target_pairs={{0,1},{1,0},{2,3},{3,2},{4,5},{5,4},{6,7},{7,6},{8,9},{9,8},{10,11... | collective-permute-start | bytes 589832 | tf_op jit(solution)/shard_map/ppermute | solution.py:302
  40.1 10.5 %collective-permute-start.16 = (bf16[8,128,128]{2,1,0:T(8,128)(2,1)S(1)}, bf16[8,128,128]{2,1,0:T(8,128)(2,1)S(1)}, u32[]{:S(2)}, u32[]{:S(2)}) collective-permute-start(bf16[8,128,128]{2,1,0:T(8,128)(2,1)S(1)} %get-tuple-element.87), channel_id=1, source_target_pairs={{0,24},{8,16},{16,8},{24,0},{1,25},{9,17},{17,9},{25,1},{2,26},{10... | collective-permute-start | bytes 786440 | tf_op jit(solution)/shard_map/ppermute | solution.py:303
  43.4 11.0 %collective-permute-start.19 = (bf16[8,128,128]{2,1,0:T(8,128)(2,1)S(1)}, bf16[8,128,128]{2,1,0:T(8,128)(2,1)S(1)}, u32[]{:S(2)}, u32[]{:S(2)}) collective-permute-start(bf16[8,128,128]{2,1,0:T(8,128)(2,1)S(1)} %get-tuple-element.95), channel_id=1, source_target_pairs={{0,8},{8,0},{16,24},{24,16},{1,9},{9,1},{17,25},{25,17},{2,10},{10... | collective-permute-start | bytes 786440 | tf_op jit(solution)/shard_map/ppermute | solution.py:303
  43.5 9.5 %collective-permute-start.18 = (bf16[6,128,128]{2,1,0:T(8,128)(2,1)S(1)}, bf16[6,128,128]{2,1,0:T(8,128)(2,1)S(1)}, u32[]{:S(2)}, u32[]{:S(2)}) collective-permute-start(bf16[6,128,128]{2,1,0:T(8,128)(2,1)S(1)} %collective-permute-done.17.refs_2_), channel_id=1, source_target_pairs={{0,2},{1,7},{2,4},{3,1},{4,6},{5,3},{6,0},{7,5},{8,10},{9,15},{10,... | collective-permute-start | bytes 589832 | tf_op jit(solution)/shard_map/ppermute | solution.py:304
  47.1 9.5 %collective-permute-start.21 = (bf16[5,128,128]{2,1,0:T(8,128)(2,1)S(1)}, bf16[5,128,128]{2,1,0:T(8,128)(2,1)S(1)}, u32[]{:S(2)}, u32[]{:S(2)}) collective-permute-start(bf16[5,128,128]{2,1,0:T(8,128)(2,1)S(1)} %collective-permute-done.20.refs_4_), channel_id=1, source_target_pairs={{0,2},{1,7},{2,4},{3,1},{4,6},{5,3},{6,0},{7,5},{8,10},{9,15},{10,... | collective-permute-start | bytes 491528 | tf_op jit(solution)/shard_map/ppermute | solution.py:304
  50.5 9.1 %collective-permute-start.23 = (bf16[5,128,128]{2,1,0:T(8,128)(2,1)S(1)}, bf16[5,128,128]{2,1,0:T(8,128)(2,1)S(1)}, u32[]{:S(2)}, u32[]{:S(2)}) collective-permute-start(bf16[5,128,128]{2,1,0:T(8,128)(2,1)S(1)} %collective-permute-done.22.refs_2_), channel_id=1, source_target_pairs={{0,2},{1,7},{2,4},{3,1},{4,6},{5,3},{6,0},{7,5},{8,10},{9,15},{10,... | collective-permute-start | bytes 491528 | tf_op jit(solution)/shard_map/ppermute | solution.py:304
  60.1 8.4 %collective-permute-start.27 = (bf16[8,128,128]{2,1,0:T(8,128)(2,1)S(1)}, bf16[8,128,128]{2,1,0:T(8,128)(2,1)S(1)}, u32[]{:S(2)}, u32[]{:S(2)}) collective-permute-start(bf16[8,128,128]{2,1,0:T(8,128)(2,1)S(1)} %get-tuple-element.107), channel_id=1, source_target_pairs={{0,24},{8,16},{16,8},{24,0},{1,25},{9,17},{17,9},{25,1},{2,26},{10... | collective-permute-start | bytes 786440 | tf_op jit(solution)/shard_map/ppermute | solution.py:303
  60.1 8.9 %collective-permute-start.24 = (bf16[8,128,128]{2,1,0:T(8,128)(2,1)S(1)}, bf16[8,128,128]{2,1,0:T(8,128)(2,1)S(1)}, u32[]{:S(2)}, u32[]{:S(2)}) collective-permute-start(bf16[8,128,128]{2,1,0:T(8,128)(2,1)S(1)} %get-tuple-element.100), channel_id=1, source_target_pairs={{0,8},{8,0},{16,24},{24,16},{1,9},{9,1},{17,25},{25,17},{2,10},{10... | collective-permute-start | bytes 786440 | tf_op jit(solution)/shard_map/ppermute | solution.py:303
  60.5 9.6 %collective-permute-start.31 = (bf16[6,128,128]{2,1,0:T(8,128)(2,1)S(1)}, bf16[6,128,128]{2,1,0:T(8,128)(2,1)S(1)}, u32[]{:S(2)}, u32[]{:S(2)}) collective-permute-start(bf16[6,128,128]{2,1,0:T(8,128)(2,1)S(1)} %collective-permute-done.30.refs_2_), channel_id=1, source_target_pairs={{0,2},{1,7},{2,4},{3,1},{4,6},{5,3},{6,0},{7,5},{8,10},{9,15},{10,... | collective-permute-start | bytes 589832 | tf_op jit(solution)/shard_map/ppermute | solution.py:304
  63.9 9.7 %collective-permute-start.29 = (bf16[5,128,128]{2,1,0:T(8,128)(2,1)S(1)}, bf16[5,128,128]{2,1,0:T(8,128)(2,1)S(1)}, u32[]{:S(2)}, u32[]{:S(2)}) collective-permute-start(bf16[5,128,128]{2,1,0:T(8,128)(2,1)S(1)} %collective-permute-done.28.refs_4_), channel_id=1, source_target_pairs={{0,2},{1,7},{2,4},{3,1},{4,6},{5,3},{6,0},{7,5},{8,10},{9,15},{10,... | collective-permute-start | bytes 491528 | tf_op jit(solution)/shard_map/ppermute | solution.py:304
  66.6 9.7 %collective-permute-start.26 = (bf16[5,128,128]{2,1,0:T(8,128)(2,1)S(1)}, bf16[5,128,128]{2,1,0:T(8,128)(2,1)S(1)}, u32[]{:S(2)}, u32[]{:S(2)}) collective-permute-start(bf16[5,128,128]{2,1,0:T(8,128)(2,1)S(1)} %collective-permute-done.25.refs_2_), channel_id=1, source_target_pairs={{0,2},{1,7},{2,4},{3,1},{4,6},{5,3},{6,0},{7,5},{8,10},{9,15},{10,... | collective-permute-start | bytes 491528 | tf_op jit(solution)/shard_map/ppermute | solution.py:304
  (8 other events, 55.6 us)
